TPU v7x, 256 devices: a whole 4x4x8 slice. The times are simulated.
256 devices in a mesh: dom: 32 (over z, y), rep: 8 (over x, core).
Axes of the slice: x: 4, y: 4, z: 8, core: 2. Of those that a mesh axis runs over, the one named last changes fastest.
Arguments:
- features: bfloat16 [131072, 256], P(('dom', 'rep')), may hold values from -6 to 6
- cotangent: bfloat16 [131072, 256], P(('dom', 'rep')), may hold values from -6 to 6
- w_self: bfloat16 [256, 256], replicated, may hold values from -0.375 to 0.375
- w_neigh: bfloat16 [256, 256], replicated, may hold values from -0.375 to 0.375
- tile_values: bfloat16 [32, 8, 256, 128, 128], P('dom', 'rep'), may hold values from -0.109375 to 0.109375
- tile_rows: int32 [32, 8, 256], P('dom', 'rep'), may hold values from 0 to 31
- tile_sources: int32 [32, 8, 256], P('dom', 'rep'), may hold values from 0 to 31
- tile_counts: int32 [32, 8], P('dom', 'rep'), may hold values from 32 to 256, as said below
- needed: int32 [32, 8, 32], replicated, may hold values from 0 to 3
Outputs:
- output: bfloat16 [131072, 256], P(('dom', 'rep'))
- grad_features: bfloat16 [131072, 256], P(('dom', 'rep'))
- grad_w_self: float32 [256, 256], replicated
- grad_w_neigh: float32 [256, 256], replicated
Inputs may be any that keep to these rules, and one draw needn't show every extreme that they name: Slots from tile_counts on are not part of the adjacency. In every draw some devices use all 256 slots.
All inputs are finite; a program needn't handle non-finite values.
Results may differ from a plain program's by a relative error of at most 0.022.
Values may be sent and summed in bfloat16 or wider, within the bound.
No kernel may reach another device: no remote copies, remote signals or barrier semaphores. Data moves between devices by JAX's collectives and lax.ppermute only.
A program may use at most 128 MiB of HBM per device.

v0:
```python
import math

import jax
import jax.numpy as jnp
from jax import lax
from jax.sharding import PartitionSpec as P

BLOCK = 32


def tile_forward(tile_block, row_ids, source_ids, used_count, columns, row_tiles):
    tile_size = tile_block.shape[-1]
    feat_dim = columns.shape[-1]
    running = jnp.zeros((row_tiles, tile_size, feat_dim), jnp.float32)
    block_count = (used_count + BLOCK - 1) // BLOCK

    def block_step(b, running):
        offset = b * BLOCK
        block_vals = lax.dynamic_slice_in_dim(tile_block, offset, BLOCK, 0)
        block_rows = lax.dynamic_slice_in_dim(row_ids, offset, BLOCK, 0)
        block_srcs = lax.dynamic_slice_in_dim(source_ids, offset, BLOCK, 0)
        inside = offset + jnp.arange(BLOCK) < used_count
        picked = columns[block_srcs]
        product = jnp.einsum("kij,kjf->kif", block_vals, picked, preferred_element_type=jnp.float32)
        product = jnp.where(inside[:, None, None], product, 0.0)
        return running.at[block_rows].add(product)

    return lax.fori_loop(0, block_count, block_step, running)


def tile_backward(tile_block, row_ids, source_ids, used_count, grad_rows, partitions):
    tile_size = tile_block.shape[-1]
    feat_dim = grad_rows.shape[-1]
    running = jnp.zeros((partitions, tile_size, feat_dim), jnp.float32)
    block_count = (used_count + BLOCK - 1) // BLOCK

    def block_step(b, running):
        offset = b * BLOCK
        block_vals = lax.dynamic_slice_in_dim(tile_block, offset, BLOCK, 0)
        block_rows = lax.dynamic_slice_in_dim(row_ids, offset, BLOCK, 0)
        block_srcs = lax.dynamic_slice_in_dim(source_ids, offset, BLOCK, 0)
        inside = offset + jnp.arange(BLOCK) < used_count
        picked = grad_rows[block_rows]
        contrib = jnp.einsum("kji,kjf->kif", block_vals, picked, preferred_element_type=jnp.float32)
        contrib = jnp.where(inside[:, None, None], contrib, 0.0)
        return running.at[block_srcs].add(contrib)

    return lax.fori_loop(0, block_count, block_step, running)


def body(
    features, cotangent, w_self, w_neigh, tile_values, tile_rows, tile_sources, tile_counts, needed
):
    domain = lax.axis_index("dom")
    replica = lax.axis_index("rep")
    partitions = lax.axis_size("dom")
    replicas = lax.axis_size("rep")
    shard_rows, feat_dim = features.shape
    tile_size = tile_values.shape[-1]
    col_tiles = shard_rows // tile_size
    row_tiles = replicas * col_tiles
    tile_block = tile_values[0, 0]
    row_ids = tile_rows[0, 0]
    source_ids = tile_sources[0, 0]
    used_count = tile_counts[0, 0]
    wanted = needed[domain, replica]
    gathered = lax.all_gather(features, "dom", axis=0, tiled=True)
    columns = gathered.reshape(partitions, col_tiles, tile_size, feat_dim)[
        jnp.arange(partitions), wanted
    ]
    partial_value = tile_forward(tile_block, row_ids, source_ids, used_count, columns, row_tiles)
    partial_value = partial_value.reshape(row_tiles * tile_size, feat_dim)
    aggregate = lax.psum_scatter(
        partial_value.astype(jnp.bfloat16), "rep", scatter_dimension=0, tiled=True
    )
    pre_act = jnp.dot(features, w_self, preferred_element_type=jnp.float32) + jnp.dot(
        aggregate, w_neigh, preferred_element_type=jnp.float32
    )
    logistic = jax.nn.sigmoid(pre_act)
    output = (pre_act * logistic).astype(jnp.bfloat16)
    derivative = logistic * (1.0 + pre_act * (1.0 - logistic))
    grad_pre = (cotangent.astype(jnp.float32) * derivative).astype(jnp.bfloat16)
    grad_agg = jnp.einsum(
        "ng,fg->nf", grad_pre, w_neigh, preferred_element_type=jnp.float32
    ).astype(jnp.bfloat16)
    local_self = jnp.einsum("nf,ng->fg", features, grad_pre, preferred_element_type=jnp.float32)
    local_neigh = jnp.einsum("nf,ng->fg", aggregate, grad_pre, preferred_element_type=jnp.float32)
    summed_self, summed_neigh = lax.psum((local_self, local_neigh), ("dom", "rep"))
    grad_scale = 1.0 / math.sqrt(shard_rows * partitions * replicas)
    grad_rows = lax.all_gather(grad_agg, "rep", axis=0, tiled=True).reshape(
        row_tiles, tile_size, feat_dim
    )
    returns_local = tile_backward(
        tile_block, row_ids, source_ids, used_count, grad_rows, partitions
    )
    placed = jnp.zeros((partitions, col_tiles, tile_size, feat_dim), jnp.float32)
    placed = placed.at[jnp.arange(partitions), wanted].set(returns_local)
    returned = lax.psum_scatter(
        placed.reshape(partitions * shard_rows, feat_dim).astype(jnp.bfloat16),
        "dom",
        scatter_dimension=0,
        tiled=True,
    ).astype(jnp.float32)
    self_grad = jnp.einsum("ng,fg->nf", grad_pre, w_self, preferred_element_type=jnp.float32)
    grad_features = (self_grad + returned).astype(jnp.bfloat16)
    return (output, grad_features, summed_self * grad_scale, summed_neigh * grad_scale)


def solution(mesh):
    in_specs = (
        P(("dom", "rep"), None),
        P(("dom", "rep"), None),
        P(),
        P(),
        P("dom", "rep", None, None, None),
        P("dom", "rep", None),
        P("dom", "rep", None),
        P("dom", "rep"),
        P(),
    )
    out_specs = (P(("dom", "rep"), None), P(("dom", "rep"), None), P(), P())
    return jax.shard_map(body, mesh=mesh, in_specs=in_specs, out_specs=out_specs, check_vma=False)
```

profile of v0, /device:TPU:1, one launch (start us, length us, event | category | flops | bytes accessed | tf_op | source)
XLA Modules:
  0.0 816.3 jit_solution(17678514797949250232)
XLA Ops:
  9.4 103.2 %all-gather.3.cloned.1.call-done = bf16[16384,256]{1,0:T(8,128)(2,1)} async-done(((bf16[512,256]{1,0:T(8,128)(2,1)}), bf16[16384,256]{1,0:T(8,128)(2,1)}) %all-gather.3.cloned.1.call-update) | async-done | bytes 8388624 | tf_op jit(solution)/shard_map/all_gather | solution.py:67
  112.6 5.5 gather_fusion.2
  118.0 2.5 broadcast.60.clone
  120.5 33.7 %while.20 = (s32[]{:T(128)}, f32[32,128,256]{2,1,0:T(8,128)}, s32[]{:T(128)}, s32[256]{0:T(256)S(1)}, s32[]{:T(128)}, /*index=5*/bf16[256,128,128]{2,1,0:T(8,128...) while((s32[]{:T(128)}, f32[32,128,256]{2,1,0:T(8,128)}, ...), condition=%wide.region_2.3_spmd, body=%wide.region_0.2_spmd.sunk | while | flops 270533888 | bytes 24122484 | solution.py:28
  121.2 2.3 gather_fusion
  123.5 3.9 convolution_select_fusion.4
  127.4 9.9 %scatter_fusion = f32[32,128,256]{2,1,0:T(8,128)} fusion(f32[32,128,256]{2,1,0:T(8,128)} %get-tuple-element.269, s32[32]{0:T(128)S(1)} %get-tuple-element.244, f32[32,128,256]{2,1,0:T(8,128)} %convolution_select_fusion.4), kind=kCustom, calls=%fused_computation.3.clone.1 | custom fusion | flops 1048576 | bytes 12583040 | tf_op jit(solution)/shard_map/while/body/scatter-add | solution.py:26
  138.0 2.3 gather_fusion
  140.3 3.9 convolution_select_fusion.4
  144.2 10.0 %scatter_fusion = f32[32,128,256]{2,1,0:T(8,128)} fusion(f32[32,128,256]{2,1,0:T(8,128)} %get-tuple-element.269, s32[32]{0:T(128)S(1)} %get-tuple-element.244, f32[32,128,256]{2,1,0:T(8,128)} %convolution_select_fusion.4), kind=kCustom, calls=%fused_computation.3.clone.1 | custom fusion | flops 1048576 | bytes 12583040 | tf_op jit(solution)/shard_map/while/body/scatter-add | solution.py:26
  154.2 3.9 convert_element_type.30
  158.4 130.3 %reduce-scatter.3.cloned.1.call-done = bf16[512,256]{1,0:T(8,128)(2,1)} async-done(((bf16[4096,256]{1,0:T(8,128)(2,1)}), bf16[512,256]{1,0:T(8,128)(2,1)}) %reduce-scatter.3.cloned.1.call-update) | async-done | bytes 262160 | tf_op jit(solution)/shard_map/reduce_scatter | solution.py:73
  288.8 2.1 multiply_convert_fusion
  291.9 12.0 %copy.13 = bf16[1,1,256,128,128]{3,4,2,1,0:T(8,128)(2,1)} copy(bf16[1,1,256,128,128]{4,3,2,1,0:T(8,128)(2,1)} %bitcast.41) | data formatting | bytes 16777216 | tf_op args[4]
  303.9 1.0 convolution_bitcast_fusion
  304.9 1.0 fusion.10
  305.9 15.6 %all-gather.5.cloned.1.call-done = bf16[4096,256]{1,0:T(8,128)(2,1)} async-done(((bf16[512,256]{1,0:T(8,128)(2,1)}), bf16[4096,256]{1,0:T(8,128)(2,1)}) %all-gather.5.cloned.1.call-update) | async-done | bytes 2097168 | tf_op jit(solution)/shard_map/all_gather | solution.py:90
  321.6 2.4 broadcast.60
  324.0 33.6 %while.21 = (s32[]{:T(128)}, f32[32,128,256]{2,1,0:T(8,128)}, s32[]{:T(128)}, s32[256]{0:T(256)S(1)}, s32[]{:T(128)}, /*index=5*/bf16[256,128,128]{1,2,0:T(8,128...) while((s32[]{:T(128)}, f32[32,128,256]{2,1,0:T(8,128)}, ...), condition=%wide.region_6.7_spmd, body=%wide.region_4.6_spmd.sunk | while | flops 270533888 | bytes 24122484 | solution.py:48
  324.7 2.3 gather_fusion.1
  327.0 3.9 convolution_select_fusion.5
  330.9 9.8 %scatter_fusion.1 = f32[32,128,256]{2,1,0:T(8,128)} fusion(f32[32,128,256]{2,1,0:T(8,128)} %get-tuple-element.305, s32[32]{0:T(128)S(1)} %get-tuple-element.254, f32[32,128,256]{2,1,0:T(8,128)} %convolution_select_fusion.5), kind=kCustom, calls=%fused_computation.4.clone.1 | custom fusion | flops 1048576 | bytes 12583040 | tf_op jit(solution)/shard_map/while/body/scatter-add | solution.py:46
  341.5 2.3 gather_fusion.1
  343.7 3.9 convolution_select_fusion.5
  347.6 9.9 %scatter_fusion.1 = f32[32,128,256]{2,1,0:T(8,128)} fusion(f32[32,128,256]{2,1,0:T(8,128)} %get-tuple-element.305, s32[32]{0:T(128)S(1)} %get-tuple-element.254, f32[32,128,256]{2,1,0:T(8,128)} %convolution_select_fusion.5), kind=kCustom, calls=%fused_computation.4.clone.1 | custom fusion | flops 1048576 | bytes 12583040 | tf_op jit(solution)/shard_map/while/body/scatter-add | solution.py:46
  357.6 7.8 broadcast_in_dim.41
  365.4 8.8 %scatter_fusion.2 = f32[32,4,128,256]{3,2,1,0:T(8,128)} fusion(f32[32,4,128,256]{3,2,1,0:T(8,128)} %broadcast_in_dim.41, s32[32]{0:T(128)S(1)} %get-tuple-element.138, f32[32,128,256]{2,1,0:T(8,128)} %get-tuple-element.91), kind=kCustom, calls=%fused_computation.5 | custom fusion | bytes 12583168 | tf_op jit(solution)/shard_map/scatter | solution.py:97
  374.2 9.1 %convert_element_type.36 = bf16[32,4,128,256]{3,2,1,0:T(8,128)(2,1)} convert(f32[32,4,128,256]{3,2,1,0:T(8,128)} %scatter_fusion.2) | non-fusion elementwise | flops 4194304 | bytes 25165824 | tf_op jit(solution)/shard_map/convert_element_type | solution.py:99
  383.3 195.3 %all-reduce.3.cloned.1.call-done = (f32[256,256]{0,1:T(8,128)}, f32[256,256]{0,1:T(8,128)}) async-done(((f32[256,256]{0,1:T(8,128)}, f32[256,256]{0,1:T(8,128)}), (f32[256,256]{0,1:T(8,128)}, f32[256,256]{0,1:T(8,128)})) %all-reduce.3.cloned.1.call-update) | async-done | bytes 524304 | tf_op jit(solution)/shard_map/psum | solution.py:88
  578.5 1.1 broadcast_multiply_fusion
  581.3 226.5 %reduce-scatter.5.cloned.1.call-done = bf16[512,256]{1,0:T(8,128)(2,1)} async-done(((bf16[16384,256]{1,0:T(8,128)(2,1)}), bf16[512,256]{1,0:T(8,128)(2,1)}) %reduce-scatter.5.cloned.1.call-update) | async-done | bytes 262160 | tf_op jit(solution)/shard_map/reduce_scatter | solution.py:98
  807.8 1.9 fusion.4
  (44 shorter events, 7.5 us)
Async XLA Ops:
  7.2 281.6 %copy-start = (bf16[256,256]{1,0:T(8,128)(2,1)S(1)}, bf16[256,256]{1,0:T(8,128)(2,1)}, u32[]{:S(2)}) copy-start(bf16[256,256]{1,0:T(8,128)(2,1)} %param.16) | copy-start | bytes 393220
  7.2 105.4 %all-gather.3.cloned.1.call-start = ((), (), s32[]{:S(2)}) async-start(), calls=%async_computation.2 | async-start | bytes 8650752 | tf_op jit(solution)/shard_map/all_gather | solution.py:67
  7.9 280.8 %reduce-scatter.3.cloned.1.call-start = ((), (), s32[]{:S(2)}) async-start(), calls=%async_computation.3 | async-start | bytes 2359296 | tf_op jit(solution)/shard_map/reduce_scatter | solution.py:73
  112.6 7.9 copy-start.5
  112.6 7.9 copy-start.6
  154.2 4.0 copy-start.2
  154.2 4.0 copy-start.3
  154.2 134.5 %copy-start.7 = (bf16[512,256]{1,0:T(8,128)(2,1)S(1)}, bf16[512,256]{1,0:T(8,128)(2,1)}, u32[]{:S(2)}) copy-start(bf16[512,256]{1,0:T(8,128)(2,1)} %param.14) | copy-start | bytes 786436
  158.1 163.4 %all-gather.5.cloned.1.call-start = ((), (), s32[]{:S(2)}) async-start(), calls=%async_computation.4 | async-start | bytes 2359296 | tf_op jit(solution)/shard_map/all_gather | solution.py:90
  291.8 286.7 %all-reduce.3.cloned.1.call-start = ((), (), s32[]{:S(2)}) async-start(), calls=%async_computation.6 | async-start | bytes 1048576 | tf_op jit(solution)/shard_map/psum | solution.py:88
  291.9 13.0 %copy-start.4 = (bf16[512,256]{1,0:T(8,128)(2,1)S(1)}, bf16[512,256]{1,0:T(8,128)(2,1)}, u32[]{:S(2)}) copy-start(bf16[512,256]{1,0:T(8,128)(2,1)} %reduce-scatter.3.cloned.1.call-done) | copy-start | bytes 786436
  305.9 502.0 %reduce-scatter.5.cloned.1.call-start = ((), (), s32[]{:S(2)}) async-start(), calls=%async_computation.5 | async-start | bytes 8650752 | tf_op jit(solution)/shard_map/reduce_scatter | solution.py:98
  383.2 426.5 %copy-start.1 = (bf16[256,256]{1,0:T(8,128)(2,1)S(1)}, bf16[256,256]{1,0:T(8,128)(2,1)}, u32[]{:S(2)}) copy-start(bf16[256,256]{1,0:T(8,128)(2,1)} %param.16) | copy-start | bytes 393220
Sparse Core Ops, SparseCore 0:
  10.6 101.9 all-gather.2
  158.3 130.4 reduce-scatter.2
  291.9 29.5 all-gather.4
  327.6 250.8 all-reduce.2
  582.4 225.3 reduce-scatter.4
where the time goes:
time: 822 us; the launch traced here: 816 us
  waiting for transfers between devices  672 us (82%)
  other arithmetic  57.3 us (7%)
  local copies, waits for them, and re-layouts  49.8 us (6%)
  matrix products  22.6 us (3%)
  between operations  14.5 us (2%)
    reduce_scatter x1, waiting for transfers between devices, body(): lax.psum_scatter(placed.reshape(partitions * shard_rows, feat_dim).astype...  227 us
    psum x1, waiting for transfers between devices, body(): lax.psum((local_self, local_neigh), ('dom', 'rep'))  195 us
    reduce_scatter x1, waiting for transfers between devices, body(): lax.psum_scatter(partial_value.astype(jnp.bfloat16), 'rep', scatter_dimen...  130 us
    all_gather x1, waiting for transfers between devices, body(): gathered = lax.all_gather(features, 'dom', axis=0, tiled=True)  103 us
    scatter-add x2, other arithmetic, block_step(): return running.at[block_rows].add(product)  19.9 us
    scatter-add x2, other arithmetic, block_step(): return running.at[block_srcs].add(contrib)  19.7 us
  transfers between devices with their start and end apart: 5, of which 5 were waited for; matrix products, arithmetic and copies ran while one was open for 10% of the time, Pallas kernels for 0%

commit v1 on v0

v1 whole, which is shorter than its diff:
```python
import functools
import math

import jax
import jax.numpy as jnp
from jax import lax
from jax.experimental import pallas as pl
from jax.experimental.pallas import tpu as pltpu
from jax.sharding import Mesh
from jax.sharding import PartitionSpec as P

F32 = jnp.float32
BF16 = jnp.bfloat16
BLOCK = 32
UNROLL = 16
VMEM_LIMIT = 40 * 2**20
AXES = ("z", "y", "x", "c")
SIZES = (8, 4, 4, 2)
DOM = ("z", "y")
REP = ("x", "c")


def select_kernel(index, blocks, out, sems):
    copies = [
        pltpu.make_async_copy(blocks.at[index[i]], out.at[i], sems.at[i])
        for i in range(out.shape[0])
    ]
    for copy in copies:
        copy.start()
    for copy in copies:
        copy.wait()


def select(index, blocks):
    count = index.shape[0]
    return pl.pallas_call(
        select_kernel,
        out_shape=jax.ShapeDtypeStruct((count,) + blocks.shape[1:], blocks.dtype),
        grid_spec=pltpu.PrefetchScalarGridSpec(
            num_scalar_prefetch=1,
            grid=(),
            in_specs=[pl.BlockSpec(memory_space=pl.ANY)],
            out_specs=pl.BlockSpec(memory_space=pl.ANY),
            scratch_shapes=[pltpu.SemaphoreType.DMA((count,))],
        ),
        name="select",
    )(index, blocks)


def accumulate_slots(step, used, add_slot):
    def group(g, carry):
        for u in range(UNROLL):
            k = g * UNROLL + u
            add_slot(k, step * BLOCK + k, step * BLOCK + k < used)
        return carry

    left = jnp.clip(used - step * BLOCK, 0, BLOCK)
    lax.fori_loop(0, (left + UNROLL - 1) // UNROLL, group, 0)


def forward_kernel(rows, sources, info, values, columns, keep, send, total):
    step = pl.program_id(0)
    used = info[0]
    core = info[1]

    @pl.when(step == 0)
    def _():
        total[...] = jnp.zeros_like(total)

    def add_slot(k, slot, inside):
        row = jnp.where(inside, rows[slot], 32)
        source = sources[slot]
        place = (source % 4) * 8 + source // 4
        total[row] += jnp.dot(values[k], columns[place], preferred_element_type=F32)

    accumulate_slots(step, used, add_slot)

    @pl.when(step == pl.num_programs(0) - 1)
    def _():
        for x in range(4):
            keep[x] = total[pl.ds(x * 8 + core * 4, 4)].astype(BF16)
            send[x] = total[pl.ds(x * 8 + (1 - core) * 4, 4)].astype(BF16)


def backward_kernel(rows, sources, info, values, grads, out, total):
    step = pl.program_id(0)
    used = info[0]

    @pl.when(step == 0)
    def _():
        total[...] = jnp.zeros_like(total)

    def add_slot(k, slot, inside):
        source = jnp.where(inside, sources[slot], 32)
        total[source] += lax.dot_general(
            values[k], grads[rows[slot]], (((0,), (0,)), ((), ())), preferred_element_type=F32
        )

    accumulate_slots(step, used, add_slot)

    @pl.when(step == pl.num_programs(0) - 1)
    def _():
        out[...] = total[:32].astype(BF16)


def over_slots(kernel, name, out_shapes, rows, sources, info, values, operand):
    slots = values.shape[0]

    def values_at(step, rows, sources, info):
        return (jnp.minimum(step, (info[0] - 1) // BLOCK), 0, 0)

    def whole(shape):
        return pl.BlockSpec(shape, lambda *_: (0,) * len(shape))

    return pl.pallas_call(
        kernel,
        out_shape=[jax.ShapeDtypeStruct(shape, BF16) for shape in out_shapes],
        grid_spec=pltpu.PrefetchScalarGridSpec(
            num_scalar_prefetch=3,
            grid=(slots // BLOCK,),
            in_specs=[pl.BlockSpec((BLOCK, 128, 128), values_at), whole(operand.shape)],
            out_specs=[whole(shape) for shape in out_shapes],
            scratch_shapes=[pltpu.VMEM((33, 128, 256), F32)],
        ),
        compiler_params=pltpu.CompilerParams(vmem_limit_bytes=VMEM_LIMIT),
        cost_estimate=pl.CostEstimate(
            flops=2 * slots * 128 * 128 * 256, bytes_accessed=slots * 32768 + 2**22, transcendentals=0
        ),
        name=name,
    )(rows, sources, info, values, operand)


def dense_kernel(features, cotangent, w_self, w_neigh, parts, output, grad_pre, grad_agg, aggregate):
    summed = parts[0].astype(F32)
    for x in range(1, 4):
        summed += parts[x].astype(F32)
    agg = summed.astype(BF16)
    aggregate[...] = agg
    pre = jnp.dot(features[...], w_self[...], preferred_element_type=F32)
    pre += jnp.dot(agg, w_neigh[...], preferred_element_type=F32)
    logistic = jax.nn.sigmoid(pre)
    output[...] = (pre * logistic).astype(BF16)
    derivative = logistic * (1.0 + pre * (1.0 - logistic))
    grad = (cotangent[...].astype(F32) * derivative).astype(BF16)
    grad_pre[...] = grad
    grad_agg[...] = lax.dot_general(
        grad, w_neigh[...], (((1,), (1,)), ((), ())), preferred_element_type=F32
    ).astype(BF16)


def dense(features, cotangent, w_self, w_neigh, parts):
    shape = jax.ShapeDtypeStruct(features.shape, BF16)
    return pl.pallas_call(
        dense_kernel,
        out_shape=[shape] * 4,
        compiler_params=pltpu.CompilerParams(vmem_limit_bytes=VMEM_LIMIT),
        name="dense",
    )(features, cotangent, w_self, w_neigh, parts)


def final_kernel(index, self_grad, returned, out, total):
    step = pl.program_id(0)
    count = returned.shape[0]

    @pl.when(step == 0)
    def _():
        total[...] = self_grad[...]

    for i in range(count):
        total[index[step * count + i]] += returned[i].astype(F32)

    @pl.when(step == pl.num_programs(0) - 1)
    def _():
        out[...] = total[...].astype(BF16)


def final(index, self_grad, returned):
    shape = self_grad.shape
    return pl.pallas_call(
        final_kernel,
        out_shape=jax.ShapeDtypeStruct(shape, BF16),
        grid_spec=pltpu.PrefetchScalarGridSpec(
            num_scalar_prefetch=1,
            grid=(4,),
            in_specs=[
                pl.BlockSpec(shape, lambda *_: (0, 0, 0)),
                pl.BlockSpec((8, 128, 256), lambda i, _: (i, 0, 0)),
            ],
            out_specs=pl.BlockSpec(shape, lambda *_: (0, 0, 0)),
            scratch_shapes=[pltpu.VMEM(shape, F32)],
        ),
        name="final",
    )(index, self_grad, returned)


def body(
    features, cotangent, w_self, w_neigh, tile_values, tile_rows, tile_sources, tile_counts, needed
):
    z, y, x, c = (lax.axis_index(a) for a in AXES)
    rank = x * 2 + c
    values = tile_values[0, 0]
    rows = tile_rows[0, 0]
    sources = tile_sources[0, 0]
    info = jnp.stack([tile_counts[0, 0], c.astype(jnp.int32)])
    shape = (4, 128, 256)

    with jax.named_scope("gather_columns"):
        wanted = needed.reshape(8, 4, 8, 8, 4)
        asked = lax.dynamic_slice(wanted, (z, 0, rank, 0, y), (1, 4, 1, 8, 1)).reshape(4, 8)
        asked = (asked + 4 * jnp.arange(8)[None, :]).reshape(32)
        column_blocks = lax.all_gather(features.reshape(shape), "z", axis=0, tiled=True)
        columns = lax.all_to_all(select(asked, column_blocks), "y", 0, 0, tiled=True)

    with jax.named_scope("aggregate"):
        kept, sent = over_slots(
            forward_kernel, "forward", [(4,) + shape] * 2, rows, sources, info, values, columns
        )
        other = lax.ppermute(sent, "c", [(0, 1), (1, 0)])
        pair = (kept.astype(F32) + other.astype(F32)).astype(BF16)
        parts = lax.all_to_all(pair, "x", 0, 0, tiled=True)

    with jax.named_scope("dense"):
        output, grad_pre, grad_agg, aggregate = dense(
            features, cotangent, w_self, w_neigh, parts.reshape(4, 512, 256)
        )

    with jax.named_scope("backward"):
        grads = lax.all_gather(grad_agg.reshape(shape), REP, axis=0, tiled=True)
        (neighbour,) = over_slots(
            backward_kernel, "backward", [(32, 128, 256)], rows, sources, info, values, grads
        )
        returned = lax.all_to_all(neighbour, DOM, 0, 0, tiled=True)

    with jax.named_scope("weights"):
        local = jnp.concatenate(
            [
                lax.dot_general(a, grad_pre, (((0,), (0,)), ((), ())), preferred_element_type=F32)
                for a in (features, aggregate)
            ]
        )
        share = lax.all_to_all(local.reshape(8, 64, 256), REP, 0, 0, tiled=True).sum(0)
        share = lax.all_gather(share, "y", axis=0, tiled=False).sum(0)
        share = lax.all_gather(share, "z", axis=0, tiled=False).sum(0)
        share = share * (1.0 / math.sqrt(512 * 256))
        grad_w = lax.all_gather(share, REP, axis=0, tiled=True)

    with jax.named_scope("final"):
        self_grad = lax.dot_general(
            grad_pre, w_self, (((1,), (1,)), ((), ())), preferred_element_type=F32
        )
        mine = lax.dynamic_slice(needed, (0, rank, z * 4 + y), (32, 1, 1)).reshape(32)
        grad_features = final(mine, self_grad.reshape(shape), returned)

    return (output, grad_features.reshape(512, 256), grad_w[:256], grad_w[256:])


def solution(mesh):
    chips = Mesh(mesh.devices.reshape(SIZES), AXES)
    nodes = P(AXES, None)
    in_specs = (
        nodes,
        nodes,
        P(),
        P(),
        P(DOM, REP, None, None, None),
        P(DOM, REP, None),
        P(DOM, REP, None),
        P(DOM, REP),
        P(),
    )
    out_specs = (nodes, nodes, P(), P())
    return jax.shard_map(body, mesh=chips, in_specs=in_specs, out_specs=out_specs, check_vma=False)
```

time: 822 us -> 323 us (0.39)
  waiting for transfers between devices: 672 us -> 86.3 us
  blocking collectives: 0 us -> 94.5 us
  Pallas kernels: 0 us -> 81.7 us
  other arithmetic: 57.3 us -> 1.85 us
  local copies, waits for them, and re-layouts: 49.8 us -> 14.8 us
  starting transfers between devices: 0.2 us -> 27.2 us
  matrix products: 22.6 us -> 1.59 us
    reduce_scatter x2 -> x0, waiting for transfers between devices: 357 us -> none  [the longest x1 227 us: body(): lax.psum_scatter(placed.reshape(partitions * shard_rows, feat_dim).astype...]
    psum x1 -> x0, waiting for transfers between devices: 195 us -> none  [body(): lax.psum((local_self, local_neigh), ('dom', 'rep'))]
    pallas_call x0 -> x5, Pallas kernels: none -> 81.7 us  [the longest x1 65.6 us: select(): pl.pallas_call(select_kernel, out_shape=jax.ShapeDtypeStruct((count,) + b...]
    all_gather x0 -> x3, blocking collectives: none -> 76.7 us  [the longest x1 44 us: body(): share = lax.all_gather(share, 'z', axis=0, tiled=False).sum(0)]
    all_gather x2, waiting for transfers between devices: 119 us -> 62.4 us  [the longest x1 40.5 us: body(): lax.all_gather(features.reshape(shape), 'z', axis=0, tiled=True)]
    scatter-add x4 -> x0, other arithmetic: 39.6 us -> none  [the longest x2 19.9 us: block_step(): return running.at[block_rows].add(product)]
    all_to_all x0 -> x3, starting transfers between devices: none -> 22.4 us  [the longest x1 13.2 us: body(): returned = lax.all_to_all(neighbour, DOM, 0, 0, tiled=True)]
    dot_general x10 -> x3, matrix products: 22.6 us -> 1.59 us  [the longest x1 1.05 us: body(): lax.dot_general(grad_pre, w_self, (((1,), (1,)), ((), ())), preferred_ele...]
  transfers between devices with their start and end apart: 5 -> 6, of which waited for: 5 -> 4; matrix products, arithmetic and copies ran while one was open for 10% -> 3% of each run, Pallas kernels for 0% -> 2%
where the time goes in v1:
time: 323 us
  blocking collectives  94.5 us (29%)
  waiting for transfers between devices  86.3 us (27%)
  Pallas kernels  81.7 us (25%)
  starting transfers between devices  27.2 us (8%)
  local copies, waits for them, and re-layouts  14.8 us (5%)
  between operations  14.8 us (5%)
    pallas_call x1, Pallas kernels, select(): pl.pallas_call(select_kernel, out_shape=jax.ShapeDtypeStruct((count,) + b...  65.6 us
    all_gather x1, blocking collectives, body(): share = lax.all_gather(share, 'z', axis=0, tiled=False).sum(0)  44 us
    all_gather x1, waiting for transfers between devices, body(): lax.all_gather(features.reshape(shape), 'z', axis=0, tiled=True)  40.5 us
    all_gather x1, waiting for transfers between devices, body(): grads = lax.all_gather(grad_agg.reshape(shape), REP, axis=0, tiled=True)  21.9 us
    all_to_all x1, waiting for transfers between devices, body(): lax.all_to_all(select(asked, column_blocks), 'y', 0, 0, tiled=True)  21 us
    all_to_all x1, blocking collectives, body(): parts = lax.all_to_all(pair, 'x', 0, 0, tiled=True)  17.8 us
    all_gather x1, blocking collectives, body(): grad_w = lax.all_gather(share, REP, axis=0, tiled=True)  16.7 us
    all_gather x1, blocking collectives, body(): share = lax.all_gather(share, 'y', axis=0, tiled=False).sum(0)  15.9 us
  transfers between devices with their start and end apart: 6, of which 4 were waited for; matrix products, arithmetic and copies ran while one was open for 3% of the time, Pallas kernels for 2%

profile of v1, /device:TPU:1, one launch (start us, length us, event | category | flops | bytes accessed | tf_op | source)
XLA Modules:
  0.0 322.8 jit_solution(14070474154034006021)
XLA Ops:
  7.2 0.7 all-gather.5.cloned.1.call-update
  8.0 1.1 copy.17
  9.1 0.7 dynamic-slice_reduce_fusion.1
  10.0 0.5 add.39.index
  10.5 40.5 %all-gather.5.cloned.1.call-done.blocks = bf16[32,128,256]{2,1,0:T(8,128)(2,1)} async-done(((bf16[4,128,256]{2,1,0:T(8,128)(2,1)}), bf16[32,128,256]{2,1,0:T(8,128)(2,1)}) %all-gather.5.cloned.1.call-update) | async-done | bytes 2097168 | tf_op jit(solution)/shard_map/gather_columns/all_gather | solution.py:211
  51.0 65.6 %select.1 = bf16[32,128,256]{2,1,0:T(8,128)(2,1)} custom-call(s32[32]{0:T(128)} %add.39.index, bf16[32,128,256]{2,1,0:T(8,128)(2,1)} %all-gather.5.cloned.1.call-done.blocks), custom_call_target="tpu_custom_call" | custom-call | tf_op jit(solution)/shard_map/gather_columns/select/pallas_call | solution.py:36
  116.7 4.0 %all-to-all-start = ((bf16[32,128,256]{2,1,0:T(8,128)(2,1)}), bf16[32,128,256]{2,1,0:T(8,128)(2,1)S(1)}, u32[]{:S(2)}, u32[]{:S(2)}) async-start(bf16[32,128,256]{2,1,0:T(8,128)(2,1)} %select.1), calls=%async_computation | async-start | bytes 4194304 | tf_op jit(solution)/shard_map/gather_columns/all_to_all | solution.py:212
  121.4 21.0 %all-to-all-done.columns = bf16[32,128,256]{2,1,0:T(8,128)(2,1)S(1)} async-done(((bf16[32,128,256]{2,1,0:T(8,128)(2,1)}), bf16[32,128,256]{2,1,0:T(8,128)(2,1)S(1)}, u32[]{:S(2)}, u32[]{:S(2)}) %all-to-all-start) | async-done | bytes 2097184 | tf_op jit(solution)/shard_map/gather_columns/all_to_all | solution.py:212
  142.4 3.4 %copy-done = bf16[1,1,256,128,128]{4,3,2,1,0:T(8,128)(2,1)S(1)} copy-done((bf16[1,1,256,128,128]{4,3,2,1,0:T(8,128)(2,1)S(1)}, bf16[1,1,256,128,128]{4,3,2,1,0:T(8,128)(2,1)}, u32[]{:S(2)}) %copy-start) | copy-done | bytes 8388632
  145.7 4.7 %forward.1 = (bf16[4,4,128,256]{3,2,1,0:T(8,128)(2,1)S(1)}, bf16[4,4,128,256]{3,2,1,0:T(8,128)(2,1)S(1)}) custom-call(s32[256]{0:T(256)S(1)} %bitcast.27, s32[256]{0:T(256)S(1)} %bitcast.29, s32[2]{0:T(128)S(1)} %pad_add_fusion.info, bf16[256,128,128]{2,1,0:T(8,128)(2,1)S(1)} %bitcast.23, bf16[32,128,256]{2,1,0:T(8,128)(2,1)S(1)} %all-to-all-done.columns), custom_call_target="tpu_custom_call" | custom-call | flops 2147483648 | bytes 12582912 | tf_op jit(solution)/shard_map/aggregate/forward/pallas_call | solution.py:115
  150.4 4.8 %collective-permute-start = (bf16[4,4,128,256]{3,2,1,0:T(8,128)(2,1)S(1)}, bf16[4,4,128,256]{3,2,1,0:T(8,128)(2,1)S(1)}, u32[]{:S(2)}, u32[]{:S(2)}) collective-permute-start(bf16[4,4,128,256]{3,2,1,0:T(8,128)(2,1)S(1)} %get-tuple-element.11), channel_id=1, source_target_pairs={{0,1},{1,0},{2,3},{3,2},{4,5},{5,4},{6,7},{7,6},{8,9},{9,8},{10,11... | collective-permute-start | bytes 3145736 | tf_op jit(solution)/shard_map/aggregate/ppermute | solution.py:218
  155.2 2.3 collective-permute-done
  157.5 0.3 add_convert_fusion
  157.8 17.8 %all_to_all.20 = bf16[4,4,128,256]{3,2,1,0:T(8,128)(2,1)S(1)} all-to-all(bf16[4,4,128,256]{3,2,1,0:T(8,128)(2,1)S(1)} %add_convert_fusion), channel_id=1, replica_groups=mesh['z'=8,'y'=4,'x'=4,'c'=2] {'x'}, dimensions={0} | all-to-all | bytes 2097152 | tf_op jit(solution)/shard_map/aggregate/all_to_all | solution.py:220
  175.7 1.3 dense.1
  176.9 0.3 convolution_bitcast_fusion
  177.2 0.3 fusion.2
  177.5 0.8 pad_maximum_fusion
  178.3 5.2 %all-to-all-start.3 = ((f32[8,64,256]{2,1,0:T(8,128)}), f32[8,64,256]{2,1,0:T(8,128)S(1)}, u32[]{:S(2)}, u32[]{:S(2)}) async-start(f32[8,64,256]{2,1,0:T(8,128)} %bitcast.12), calls=%async_computation.3 | async-start | bytes 1048576 | tf_op jit(solution)/shard_map/weights/all_to_all | solution.py:241
  183.5 21.9 %all-gather.7.cloned.1.call-done.grads = bf16[32,128,256]{2,1,0:T(8,128)(2,1)} async-done(((bf16[4,128,256]{2,1,0:T(8,128)(2,1)}), bf16[32,128,256]{2,1,0:T(8,128)(2,1)}) %all-gather.7.cloned.1.call-update) | async-done | bytes 2097168 | tf_op jit(solution)/shard_map/backward/all_gather | solution.py:228
  205.4 3.4 %copy-done.1 = bf16[1,1,256,128,128]{4,3,2,1,0:T(8,128)(2,1)S(1)} copy-done((bf16[1,1,256,128,128]{4,3,2,1,0:T(8,128)(2,1)S(1)}, bf16[1,1,256,128,128]{4,3,2,1,0:T(8,128)(2,1)}, u32[]{:S(2)}) %copy-start.1) | copy-done | bytes 8388632
  208.8 1.6 copy-done.3
  210.4 6.1 %backward.1 = bf16[32,128,256]{2,1,0:T(8,128)(2,1)} custom-call(s32[256]{0:T(256)S(1)} %bitcast.28, s32[256]{0:T(256)S(1)} %bitcast.30, s32[2]{0:T(128)S(1)} %pad_add_fusion.info, bf16[256,128,128]{2,1,0:T(8,128)(2,1)S(1)} %bitcast.24, bf16[32,128,256]{2,1,0:T(8,128)(2,1)S(1)} %copy-done.3), custom_call_target="tpu_custom_call" | custom-call | flops 2147483648 | bytes 12582912 | tf_op jit(solution)/shard_map/backward/backward/pallas_call | solution.py:115
  216.5 13.2 %all-to-all-start.2 = ((bf16[32,128,256]{2,1,0:T(8,128)(2,1)}), bf16[32,128,256]{2,1,0:T(8,128)(2,1)S(1)}, u32[]{:S(2)}, u32[]{:S(2)}) async-start(bf16[32,128,256]{2,1,0:T(8,128)(2,1)} %backward.1), calls=%async_computation.2 | async-start | bytes 4194304 | tf_op jit(solution)/shard_map/backward/all_to_all | solution.py:232
  229.7 2.2 dynamic-slice_reduce_fusion.index
  231.9 1.0 fusion.1
  233.0 15.9 %all-gather = f32[256,256]{1,0:T(8,128)S(1)} all-gather(f32[64,256]{1,0:T(8,128)S(1)} %reduce_sum.27), channel_id=2, replica_groups=mesh['z'=8,'y'=4,'x'=4,'c'=2] {'y'}, dimensions={0}, use_global_device_ids=true | all-gather | bytes 327680 | tf_op jit(solution)/shard_map/weights/all_gather | solution.py:242
  248.9 44.0 %all-gather.1 = f32[512,256]{1,0:T(8,128)S(1)} all-gather(f32[64,256]{1,0:T(8,128)S(1)} %reduce_sum.28), channel_id=3, replica_groups=mesh['z'=8,'y'=4,'x'=4,'c'=2] {'z'}, dimensions={0}, use_global_device_ids=true | all-gather | bytes 589824 | tf_op jit(solution)/shard_map/weights/all_gather | solution.py:243
  293.0 16.7 %all_gather.27 = f32[512,256]{1,0:T(8,128)S(1)} all-gather(f32[64,256]{1,0:T(8,128)S(1)} %broadcast_multiply_fusion), channel_id=1, replica_groups=mesh['z'=8,'y'=4,'x'=4,'c'=2] {'x','c'}, dimensions={0}, use_global_device_ids=true | all-gather | bytes 589824 | tf_op jit(solution)/shard_map/weights/all_gather | solution.py:245
  309.7 0.8 fusion
  310.6 1.3 copy-done.9
  311.9 4.1 %final.1 = bf16[4,128,256]{2,1,0:T(8,128)(2,1)} custom-call(s32[32]{0:T(128)} %dynamic-slice_reduce_fusion.index, f32[4,128,256]{2,1,0:T(8,128)} %bitcast.31, bf16[32,128,256]{2,1,0:T(8,128)(2,1)} %copy-done.9), custom_call_target="tpu_custom_call" | custom-call | tf_op jit(solution)/shard_map/final/final/pallas_call | solution.py:179
  (30 shorter events, 0.4 us)
Async XLA Ops:
  7.2 43.9 %all-gather.5.cloned.1.call-start = ((), (), s32[]{:S(2)}) async-start(), calls=%async_computation.4 | async-start | bytes 2359296 | tf_op jit(solution)/shard_map/gather_columns/all_gather | solution.py:211
  116.6 25.7 %copy-start.7 = (s32[1,1,256]{2,1,0:T(1,128)S(1)}, s32[1,1,256]{2,1,0:T(1,128)}, u32[]{:S(2)}) copy-start(s32[1,1,256]{2,1,0:T(1,128)} %param.14) | copy-start | bytes 3076
  116.6 25.7 %copy-start.8 = (s32[1,1,256]{2,1,0:T(1,128)S(1)}, s32[1,1,256]{2,1,0:T(1,128)}, u32[]{:S(2)}) copy-start(s32[1,1,256]{2,1,0:T(1,128)} %param.15) | copy-start | bytes 3076
  116.7 25.7 %all-to-all-start = ((bf16[32,128,256]{2,1,0:T(8,128)(2,1)}), bf16[32,128,256]{2,1,0:T(8,128)(2,1)S(1)}, u32[]{:S(2)}, u32[]{:S(2)}) async-start(bf16[32,128,256]{2,1,0:T(8,128)(2,1)} %select.1), calls=%async_computation | async-start | bytes 4194304 | tf_op jit(solution)/shard_map/gather_columns/all_to_all | solution.py:212
  120.7 84.7 %all-gather.7.cloned.1.call-start = ((), (), s32[]{:S(2)}) async-start(), calls=%async_computation.5 | async-start | bytes 2359296 | tf_op jit(solution)/shard_map/backward/all_gather | solution.py:228
  142.4 3.4 %copy-start = (bf16[1,1,256,128,128]{4,3,2,1,0:T(8,128)(2,1)S(1)}, bf16[1,1,256,128,128]{4,3,2,1,0:T(8,128)(2,1)}, u32[]{:S(2)}) copy-start(bf16[1,1,256,128,128]{4,3,2,1,0:T(8,128)(2,1)} %param.13) | copy-start | bytes 25165828
  150.4 7.1 %collective-permute-start = (bf16[4,4,128,256]{3,2,1,0:T(8,128)(2,1)S(1)}, bf16[4,4,128,256]{3,2,1,0:T(8,128)(2,1)S(1)}, u32[]{:S(2)}, u32[]{:S(2)}) collective-permute-start(bf16[4,4,128,256]{3,2,1,0:T(8,128)(2,1)S(1)} %get-tuple-element.11), channel_id=1, source_target_pairs={{0,1},{1,0},{2,3},{3,2},{4,5},{5,4},{6,7},{7,6},{8,9},{9,8},{10,11... | collective-permute-start | bytes 3145736 | tf_op jit(solution)/shard_map/aggregate/ppermute | solution.py:218
  157.5 18.2 %copy-start.2 = (bf16[512,256]{1,0:T(8,128)(2,1)S(1)}, bf16[512,256]{1,0:T(8,128)(2,1)}, u32[]{:S(2)}) copy-start(bf16[512,256]{1,0:T(8,128)(2,1)} %features.1) | copy-start | bytes 786436
  157.5 18.2 %copy-start.4 = (bf16[256,256]{1,0:T(8,128)(2,1)S(1)}, bf16[256,256]{1,0:T(8,128)(2,1)}, u32[]{:S(2)}) copy-start(bf16[256,256]{1,0:T(8,128)(2,1)} %w_self.1) | copy-start | bytes 393220
  157.5 18.2 %copy-start.5 = (bf16[512,256]{1,0:T(8,128)(2,1)S(1)}, bf16[512,256]{1,0:T(8,128)(2,1)}, u32[]{:S(2)}) copy-start(bf16[512,256]{1,0:T(8,128)(2,1)} %cotangent.1) | copy-start | bytes 786436
  157.5 18.2 %copy-start.6 = (bf16[256,256]{1,0:T(8,128)(2,1)S(1)}, bf16[256,256]{1,0:T(8,128)(2,1)}, u32[]{:S(2)}) copy-start(bf16[256,256]{1,0:T(8,128)(2,1)} %w_neigh.1) | copy-start | bytes 393220
  178.3 38.2 %all-to-all-start.3 = ((f32[8,64,256]{2,1,0:T(8,128)}), f32[8,64,256]{2,1,0:T(8,128)S(1)}, u32[]{:S(2)}, u32[]{:S(2)}) async-start(f32[8,64,256]{2,1,0:T(8,128)} %bitcast.12), calls=%async_computation.3 | async-start | bytes 1048576 | tf_op jit(solution)/shard_map/weights/all_to_all | solution.py:241
  205.4 3.4 %copy-start.1 = (bf16[1,1,256,128,128]{4,3,2,1,0:T(8,128)(2,1)S(1)}, bf16[1,1,256,128,128]{4,3,2,1,0:T(8,128)(2,1)}, u32[]{:S(2)}) copy-start(bf16[1,1,256,128,128]{4,3,2,1,0:T(8,128)(2,1)} %param.13) | copy-start | bytes 25165828
  208.8 1.6 copy-start.3
  216.5 94.1 %all-to-all-start.2 = ((bf16[32,128,256]{2,1,0:T(8,128)(2,1)}), bf16[32,128,256]{2,1,0:T(8,128)(2,1)S(1)}, u32[]{:S(2)}, u32[]{:S(2)}) async-start(bf16[32,128,256]{2,1,0:T(8,128)(2,1)} %backward.1), calls=%async_computation.2 | async-start | bytes 4194304 | tf_op jit(solution)/shard_map/backward/all_to_all | solution.py:232
  310.6 1.3 copy-start.9
Sparse Core Ops, SparseCore 0:
  9.8 41.1 all-gather.4
  177.1 28.2 all-gather.6

commit v2 on v1

v2 whole, which is shorter than its diff:
```python
import functools
import math

import jax
import jax.numpy as jnp
from jax import lax
from jax.experimental import pallas as pl
from jax.experimental.pallas import tpu as pltpu
from jax.sharding import Mesh
from jax.sharding import PartitionSpec as P

F32 = jnp.float32
BF16 = jnp.bfloat16
PARTS = 2
WIDTH = 256 // PARTS
BLOCK = 16
VMEM_LIMIT = 54 * 2**20
AXES = ("z", "y", "x", "c")
SIZES = (8, 4, 4, 2)
DOM = ("z", "y")
REP = ("x", "c")


def select_kernel(index, blocks, out):
    for i in range(out.shape[0]):
        out[i] = blocks[index[i]]


def select(index, blocks):
    return pl.pallas_call(
        select_kernel,
        out_shape=jax.ShapeDtypeStruct((index.shape[0],) + blocks.shape[1:], blocks.dtype),
        grid_spec=pltpu.PrefetchScalarGridSpec(
            num_scalar_prefetch=1,
            grid=(),
            in_specs=[pl.BlockSpec(memory_space=pltpu.VMEM)],
            out_specs=pl.BlockSpec(memory_space=pltpu.VMEM),
        ),
        compiler_params=pltpu.CompilerParams(vmem_limit_bytes=8 * 2**20),
        name="select",
    )(index, blocks)


def copies_of(source, target, size, sems):
    rows = pl.ds(0, target.shape[1])
    return [
        pltpu.make_async_copy(
            source.at[pl.ds(i * size, size), rows], target.at[pl.ds(i * size, size)], sems.at[i]
        )
        for i in range(source.shape[0] // size)
    ]


def accumulate_slots(used, values, tiles, total, sems, piece_copies, add_slot):
    for copy in piece_copies:
        copy.start()
    for copy in copies_of(values, tiles, BLOCK, sems):
        copy.start()
    total[...] = jnp.zeros_like(total)
    for copy in piece_copies:
        copy.wait()

    def block(b, carry):
        first = b * BLOCK
        pltpu.make_async_copy(
            values.at[pl.ds(first, BLOCK)], tiles.at[pl.ds(first, BLOCK)], sems.at[b]
        ).wait()

        @pl.when(first < used)
        def _():
            for u in range(BLOCK):
                add_slot(first + u)

        return carry

    lax.fori_loop(0, values.shape[0] // BLOCK, block, 0)


def forward_kernel(targets, places, info, values, columns, keep, send, tiles, total, sems):
    used, x, core = info[0], info[1], info[2]

    def add_slot(k):
        total[targets[k]] += jnp.dot(tiles[k], columns[places[k]], preferred_element_type=F32)

    accumulate_slots(used, values, tiles, total, sems, [], add_slot)
    for k in range(4):
        chip = lax.rem(x + k, 4) * 8
        keep[k] = total[pl.ds(chip + core * 4, 4)].astype(BF16)
        send[k] = total[pl.ds(chip + (1 - core) * 4, 4)].astype(BF16)


def backward_kernel(targets, places, info, values, *refs):
    pieces, (out, tiles, total, sems, held, piece_sems) = refs[:8], refs[-6:]

    def add_slot(k):
        total[targets[k]] += jnp.dot(held[places[k]], tiles[k], preferred_element_type=F32)

    piece_copies = [
        pltpu.make_async_copy(piece, held.at[pl.ds(i * 4, 4)], piece_sems.at[i])
        for i, piece in enumerate(pieces)
    ]
    accumulate_slots(info[0], values, tiles, total, sems, piece_copies, add_slot)
    out[:, :WIDTH, :] = total[:32].astype(BF16)
    for share in refs[8:-6]:
        for i in range(32):
            out[i, WIDTH:, :] = share[...]


def over_slots(kernel, name, out_shapes, targets, places, info, values, pieces, extra=()):
    slots = values.shape[0]
    tile = pieces[0].shape[1:]
    scratch = [
        pltpu.VMEM(values.shape, BF16),
        pltpu.VMEM((33,) + tile, F32),
        pltpu.SemaphoreType.DMA((slots // BLOCK,)),
    ]
    if len(pieces) > 1:
        scratch += [
            pltpu.VMEM((32,) + tile, BF16),
            pltpu.SemaphoreType.DMA((len(pieces),)),
        ]
    piece_space = pl.ANY if len(pieces) > 1 else pltpu.VMEM
    return pl.pallas_call(
        kernel,
        out_shape=[jax.ShapeDtypeStruct(shape, BF16) for shape in out_shapes],
        grid_spec=pltpu.PrefetchScalarGridSpec(
            num_scalar_prefetch=3,
            grid=(),
            in_specs=[pl.BlockSpec(memory_space=pltpu.HBM)]
            + [pl.BlockSpec(memory_space=piece_space)] * len(pieces)
            + [pl.BlockSpec(memory_space=pltpu.VMEM)] * len(extra),
            out_specs=[pl.BlockSpec(memory_space=pltpu.VMEM)] * len(out_shapes),
            scratch_shapes=scratch,
        ),
        compiler_params=pltpu.CompilerParams(vmem_limit_bytes=VMEM_LIMIT),
        cost_estimate=pl.CostEstimate(
            flops=2 * slots * 128 * 128 * 256, bytes_accessed=slots * 32768 + 2**22, transcendentals=0
        ),
        name=name,
    )(targets, places, info, values, *pieces, *extra)


def dense_kernel(features, cotangent, w_self, w_neigh, *refs):
    sums, refs = refs[:4], refs[4:]
    output, grad_pre, grad_aggs, local_weights = refs[0], refs[1], refs[2 : 2 + PARTS], refs[2 + PARTS]
    summed = sums[0][...].astype(F32)
    for part in sums[1:]:
        summed += part[...].astype(F32)
    agg = summed.astype(BF16)
    pre = jnp.dot(features[...], w_self[...], preferred_element_type=F32)
    pre += jnp.dot(agg, w_neigh[...], preferred_element_type=F32)
    logistic = jax.nn.sigmoid(pre)
    output[...] = (pre * logistic).astype(BF16)
    derivative = logistic * (1.0 + pre * (1.0 - logistic))
    grad = (cotangent[...].astype(F32) * derivative).astype(BF16)
    grad_pre[...] = grad
    for h in range(PARTS):
        turned = lax.dot_general(
            w_neigh[h * WIDTH : (h + 1) * WIDTH, :],
            grad,
            (((1,), (1,)), ((), ())),
            preferred_element_type=F32,
        ).astype(BF16)
        for t in range(4):
            grad_aggs[h][t] = turned[:, t * 128 : (t + 1) * 128]
    for i, left in enumerate((features[...], agg)):
        product = lax.dot_general(left, grad, (((0,), (0,)), ((), ())), preferred_element_type=F32)
        local_weights[i * 256 : (i + 1) * 256, :] = product.astype(BF16)


def dense(features, cotangent, w_self, w_neigh, sums):
    whole = jax.ShapeDtypeStruct(features.shape, BF16)
    part = jax.ShapeDtypeStruct((4, WIDTH, 128), BF16)
    return pl.pallas_call(
        dense_kernel,
        out_shape=[whole, whole] + [part] * PARTS + [whole],
        compiler_params=pltpu.CompilerParams(vmem_limit_bytes=16 * 2**20),
        name="dense",
    )(features, cotangent, w_self, w_neigh, *sums)


def place_kernel(part, index, grad_pre, w_self, returned, *refs):
    out, held, total, sems = refs[-4:]
    size = held.shape[0] // sems.shape[0]
    copies = copies_of(returned, held, size, sems)
    for copy in copies:
        copy.start()
    turned = lax.dot_general(
        w_self[part * WIDTH : (part + 1) * WIDTH, :],
        grad_pre[...],
        (((1,), (1,)), ((), ())),
        preferred_element_type=F32,
    )
    for t in range(4):
        total[t] = turned[:, t * 128 : (t + 1) * 128]
    for i, copy in enumerate(copies):
        copy.wait()
        for j in range(i * size, (i + 1) * size):
            total[index[j]] += held[j].astype(F32)
    for t in range(4):
        out[t] = total[t].T.astype(BF16)


def place(part, index, grad_pre, w_self, returned, earlier=None):
    def whole(shape):
        return pl.BlockSpec(shape, lambda *_: (0,) * len(shape))

    return pl.pallas_call(
        functools.partial(place_kernel, part),
        out_shape=jax.ShapeDtypeStruct((4, 128, 256), BF16),
        grid_spec=pltpu.PrefetchScalarGridSpec(
            num_scalar_prefetch=1,
            grid=(1,),
            in_specs=[whole(grad_pre.shape), whole(w_self.shape), pl.BlockSpec(memory_space=pl.ANY)]
            + ([] if earlier is None else [pl.BlockSpec(memory_space=pl.ANY)]),
            out_specs=pl.BlockSpec((4, 128, WIDTH), lambda *_: (0, 0, part)),
            scratch_shapes=[
                pltpu.VMEM((32, WIDTH, 128), BF16),
                pltpu.VMEM((4, WIDTH, 128), F32),
                pltpu.SemaphoreType.DMA((8,)),
            ],
        ),
        input_output_aliases={} if earlier is None else {4: 0},
        compiler_params=pltpu.CompilerParams(vmem_limit_bytes=8 * 2**20),
        name="place",
    )(index, grad_pre, w_self, returned, *([] if earlier is None else [earlier]))


def assemble_kernel(returned, w_self, w_neigh, held, sem):
    rows = returned.shape[1] - WIDTH
    copy = pltpu.make_async_copy(returned.at[:, pl.ds(WIDTH, rows)], held, sem)
    copy.start()
    copy.wait()
    scale = 1.0 / math.sqrt(512 * 256)
    for i in range(16):
        for out, block in ((w_self, held[i]), (w_neigh, held[16 + i])):
            block = block.astype(F32) * scale
            out[i, :, :128] = block[:16]
            out[i, :, 128:] = block[16:]


def assemble(returned):
    half = jax.ShapeDtypeStruct((16, 16, 256), F32)
    w_self, w_neigh = pl.pallas_call(
        assemble_kernel,
        out_shape=[half, half],
        in_specs=[pl.BlockSpec(memory_space=pl.ANY)],
        scratch_shapes=[pltpu.VMEM((32, 32, 128), BF16), pltpu.SemaphoreType.DMA],
        compiler_params=pltpu.CompilerParams(vmem_limit_bytes=8 * 2**20),
        name="assemble",
    )(returned)
    return w_self.reshape(256, 256), w_neigh.reshape(256, 256)


def sum_over_rep(share):
    share = share + flip(share, "c", 1)
    share = share + flip(share, "x", 1)
    return share + flip(share, "x", 2)


def shift(a, axis, by):
    size = lax.axis_size(axis)
    return lax.ppermute(a, axis, [(i, (i + by) % size) for i in range(size)])


def flip(a, axis, bit):
    return lax.ppermute(a, axis, [(i, i ^ bit) for i in range(lax.axis_size(axis))])


def body(
    features, cotangent, w_self, w_neigh, tile_values, tile_rows, tile_sources, tile_counts, needed
):
    z, y, x, c = (lax.axis_index(a) for a in AXES)
    rank = x * 2 + c
    values = tile_values[0, 0]
    rows = tile_rows[0, 0]
    sources = tile_sources[0, 0]
    info = jnp.stack([tile_counts[0, 0], x.astype(jnp.int32), c.astype(jnp.int32)])
    inside = jnp.arange(rows.shape[0]) < tile_counts[0, 0]
    forward_targets = jnp.where(inside, rows, 32)
    backward_targets = jnp.where(inside, sources, 32)
    backward_places = jnp.where((rows // 4) % 2 == c, 0, 16) + ((x - rows // 8) & 3) * 4 + rows % 4

    with jax.named_scope("gather_columns"):
        asked = lax.dynamic_slice(needed, (0, rank, z * 4 + y), (32, 1, 1)).reshape(32)
        outgoing = select(asked, features.reshape(4, 128, 256))
        columns = lax.all_to_all(outgoing, DOM, 0, 0, tiled=True)

    with jax.named_scope("aggregate"):
        shapes = [(4, 4, 128, 256)] * 2
        kept, sent = over_slots(
            forward_kernel, "forward", shapes, forward_targets, sources, info, values, [columns]
        )
        other = shift(sent, "c", 1)
        sums = []
        for k in range(4):
            pair = (kept[k].astype(F32) + other[k].astype(F32)).astype(BF16)
            sums.append((shift(pair, "x", k) if k else pair).reshape(512, 256))

    with jax.named_scope("dense"):
        output, grad_pre, *grad_aggs, local_weights = dense(features, cotangent, w_self, w_neigh, sums)

    with jax.named_scope("backward"):
        returned = []
        for h, part in enumerate(grad_aggs):
            behind = [part] + [shift(part, "x", k) for k in (1, 2, 3)]
            pieces, extra = list(behind), []
            if h == 0:
                local_weights, *pieces[:4] = lax.optimization_barrier((local_weights, *pieces[:4]))
                local_weights = lax.all_to_all(
                    local_weights.reshape(32, 16, 256), DOM, 0, 0, tiled=True
                )
            pieces += [shift(piece, "c", 1) for piece in pieces]
            if h == 1:
                share = sum_over_rep(local_weights.astype(F32).sum(0)).astype(BF16)
                extra = [jnp.concatenate([share[:, :128], share[:, 128:]])]
            (neighbour,) = over_slots(
                backward_kernel,
                "backward",
                [(32, WIDTH + 32 * len(extra), 128)],
                backward_targets,
                backward_places,
                info,
                values,
                pieces,
                extra,
            )
            returned.append(lax.all_to_all(neighbour, DOM, 0, 0, tiled=True))

    with jax.named_scope("weights"):
        grad_w_self, grad_w_neigh = assemble(returned[1])

    with jax.named_scope("final"):
        grad_features = None
        for h in range(PARTS):
            grad_features = place(h, asked, grad_pre, w_self, returned[h], grad_features)

    return (output, grad_features.reshape(512, 256), grad_w_self, grad_w_neigh)


def solution(mesh):
    chips = Mesh(mesh.devices.reshape(SIZES), AXES)
    nodes = P(AXES, None)
    in_specs = (
        nodes,
        nodes,
        P(),
        P(),
        P(DOM, REP, None, None, None),
        P(DOM, REP, None),
        P(DOM, REP, None),
        P(DOM, REP),
        P(),
    )
    out_specs = (nodes, nodes, P(), P())
    return jax.shard_map(body, mesh=chips, in_specs=in_specs, out_specs=out_specs, check_vma=False)
```

time: 323 us -> 211 us (0.65); the launches traced: 323 us -> 206 us
  blocking collectives: 94.5 us -> 0 us
  Pallas kernels: 81.7 us -> 31.9 us
  starting transfers between devices: 27.2 us -> 66 us
  between operations: 14.8 us -> 1.73 us
  waiting for transfers between devices: 86.3 us -> 96.9 us
  local copies, waits for them, and re-layouts: 14.8 us -> 5.94 us
    all_gather x3 -> x0, blocking collectives: 76.7 us -> none  [the longest x1 44 us: body(): share = lax.all_gather(share, 'z', axis=0, tiled=False).sum(0)]
    all_gather x2 -> x0, waiting for transfers between devices: 62.4 us -> none  [the longest x1 40.5 us: body(): lax.all_gather(features.reshape(shape), 'z', axis=0, tiled=True)]
    pallas_call x3 -> x5, Pallas kernels: 70.9 us -> 9.94 us  [the longest x2 5.39 us: place(): pl.pallas_call(functools.partial(place_kernel, part), out_shape=jax.Shape...]
    all_to_all x3 -> x4, waiting for transfers between devices: 21 us -> 73.7 us  [the longest x1 46.7 us: body(): columns = lax.all_to_all(outgoing, DOM, 0, 0, tiled=True)]
    ppermute x1 -> x21, starting transfers between devices: 4.77 us -> 28.4 us  [the longest x18 25.1 us: shift(): return lax.ppermute(a, axis, [(i, (i + by) % size) for i in range(size)])]
    ppermute x1 -> x21, waiting for transfers between devices: 2.29 us -> 23.3 us  [the longest x18 19.3 us: shift(): return lax.ppermute(a, axis, [(i, (i + by) % size) for i in range(size)])]
    all_to_all x1 -> x0, blocking collectives: 17.8 us -> none  [body(): parts = lax.all_to_all(pair, 'x', 0, 0, tiled=True)]
    all_to_all x3 -> x4, starting transfers between devices: 22.4 us -> 37.6 us  [the longest x2 19.5 us: body(): returned.append(lax.all_to_all(neighbour, DOM, 0, 0, tiled=True))]
  transfers between devices with their start and end apart: 6 -> 25, of which waited for: 4 -> 14; matrix products, arithmetic and copies ran while one was open for 3% -> 1% of each run, Pallas kernels for 2% -> 9%
where the time goes in v2:
time: 211 us; the launch traced here: 206 us
  waiting for transfers between devices  96.9 us (46%)
  starting transfers between devices  66 us (31%)
  Pallas kernels  31.9 us (15%)
  local copies, waits for them, and re-layouts  5.94 us (3%)
  other arithmetic  3.91 us (2%)
    all_to_all x1, waiting for transfers between devices, body(): columns = lax.all_to_all(outgoing, DOM, 0, 0, tiled=True)  46.7 us
    all_to_all x2, waiting for transfers between devices, body(): returned.append(lax.all_to_all(neighbour, DOM, 0, 0, tiled=True))  27 us
    ppermute x18, starting transfers between devices, shift(): return lax.ppermute(a, axis, [(i, (i + by) % size) for i in range(size)])  25.1 us
    pallas_call x3, Pallas kernels, over_slots(): pl.pallas_call(kernel, out_shape=[jax.ShapeDtypeStruct(shape, BF16) for s...  22 us
    all_to_all x2, starting transfers between devices, body(): returned.append(lax.all_to_all(neighbour, DOM, 0, 0, tiled=True))  19.5 us
    ppermute x18, waiting for transfers between devices, shift(): return lax.ppermute(a, axis, [(i, (i + by) % size) for i in range(size)])  19.3 us
    all_to_all x1, starting transfers between devices, body(): columns = lax.all_to_all(outgoing, DOM, 0, 0, tiled=True)  12.2 us
    all_to_all x1, starting transfers between devices, body(): lax.all_to_all(local_weights.reshape(32, 16, 256), DOM, 0, 0, tiled=True)  5.89 us
  transfers between devices with their start and end apart: 25, of which 14 were waited for; matrix products, arithmetic and copies ran while one was open for 1% of the time, Pallas kernels for 9%

profile of v2, /device:TPU:1, one launch (start us, length us, event | category | flops | bytes accessed | tf_op | source)
XLA Modules:
  0.0 206.5 jit_solution(12822710823996308697)
XLA Ops:
  3.2 2.0 select.13
  5.3 12.2 %all-to-all-start = ((bf16[32,128,256]{2,1,0:T(8,128)(2,1)}), bf16[32,128,256]{2,1,0:T(8,128)(2,1)S(1)}, u32[]{:S(2)}, u32[]{:S(2)}) async-start(bf16[32,128,256]{2,1,0:T(8,128)(2,1)} %select.13), calls=%async_computation | async-start | bytes 4194304 | tf_op jit(solution)/shard_map/gather_columns/all_to_all | solution.py:287
  19.3 46.7 %all-to-all-done.columns = bf16[32,128,256]{2,1,0:T(8,128)(2,1)S(1)} async-done(((bf16[32,128,256]{2,1,0:T(8,128)(2,1)}), bf16[32,128,256]{2,1,0:T(8,128)(2,1)S(1)}, u32[]{:S(2)}, u32[]{:S(2)}) %all-to-all-start) | async-done | bytes 2097184 | tf_op jit(solution)/shard_map/gather_columns/all_to_all | solution.py:287
  65.9 1.3 copy-done.8
  67.3 7.4 %forward.1 = (bf16[4,4,128,256]{3,2,1,0:T(8,128)(2,1)}, bf16[4,4,128,256]{3,2,1,0:T(8,128)(2,1)}) custom-call(s32[256]{0:T(256)} %get-tuple-element.39.targets, s32[256]{0:T(256)} %bitcast.34, s32[3]{0:T(128)} %pad_add_fusion.info, bf16[256,128,128]{2,1,0:T(8,128)(2,1)} %bitcast.30, bf16[32,128,256]{2,1,0:T(8,128)(2,1)} %copy-done.8), custom_call_target="tpu_custom_call" | custom-call | flops 2147483648 | bytes 12582912 | tf_op jit(solution)/shard_map/aggregate/forward/pallas_call | solution.py:123
  74.7 4.0 %collective-permute-start = (bf16[4,4,128,256]{3,2,1,0:T(8,128)(2,1)}, bf16[4,4,128,256]{3,2,1,0:T(8,128)(2,1)S(1)}, u32[]{:S(2)}, u32[]{:S(2)}) collective-permute-start(bf16[4,4,128,256]{3,2,1,0:T(8,128)(2,1)} %get-tuple-element.19), channel_id=1, source_target_pairs={{0,1},{1,0},{2,3},{3,2},{4,5},{5,4},{6,7},{7,6},{8,9},{9,8},{10,11... | collective-permute-start | bytes 3145736 | tf_op jit(solution)/shard_map/aggregate/ppermute | solution.py:263
  78.7 2.5 %collective-permute-done = bf16[4,4,128,256]{3,2,1,0:T(8,128)(2,1)S(1)} collective-permute-done((bf16[4,4,128,256]{3,2,1,0:T(8,128)(2,1)}, bf16[4,4,128,256]{3,2,1,0:T(8,128)(2,1)S(1)}, u32[]{:S(2)}, u32[]{:S(2)}) %collective-permute-start) | collective-permute-done | bytes 1048608 | tf_op jit(solution)/shard_map/aggregate/ppermute | solution.py:263
  81.2 1.5 fusion.2
  82.7 2.5 %collective-permute-start.1 = (bf16[4,128,256]{2,1,0:T(8,128)(2,1)S(1)}, bf16[4,128,256]{2,1,0:T(8,128)(2,1)S(1)}, u32[]{:S(2)}, u32[]{:S(2)}) collective-permute-start(bf16[4,128,256]{2,1,0:T(8,128)(2,1)S(1)} %get-tuple-element.34), channel_id=1, source_target_pairs={{0,2},{2,4},{4,6},{6,0},{1,3},{3,5},{5,7},{7,1},{8,10},{10,12},{12... | collective-permute-start | bytes 786440 | tf_op jit(solution)/shard_map/aggregate/ppermute | solution.py:263
  85.2 2.5 %collective-permute-start.2 = (bf16[4,128,256]{2,1,0:T(8,128)(2,1)S(1)}, bf16[4,128,256]{2,1,0:T(8,128)(2,1)S(1)}, u32[]{:S(2)}, u32[]{:S(2)}) collective-permute-start(bf16[4,128,256]{2,1,0:T(8,128)(2,1)S(1)} %get-tuple-element.33), channel_id=1, source_target_pairs={{0,4},{2,6},{4,0},{6,2},{1,5},{3,7},{5,1},{7,3},{8,12},{10,14},{12... | collective-permute-start | bytes 786440 | tf_op jit(solution)/shard_map/aggregate/ppermute | solution.py:263
  87.6 1.2 collective-permute-start.3
  88.8 4.2 %collective-permute-done.1 = bf16[4,128,256]{2,1,0:T(8,128)(2,1)S(1)} collective-permute-done((bf16[4,128,256]{2,1,0:T(8,128)(2,1)S(1)}, bf16[4,128,256]{2,1,0:T(8,128)(2,1)S(1)}, u32[]{:S(2)}, u32[]{:S(2)}) %collective-permute-start.1) | collective-permute-done | bytes 262176 | tf_op jit(solution)/shard_map/aggregate/ppermute | solution.py:263
  93.0 6.6 %collective-permute-done.2 = bf16[4,128,256]{2,1,0:T(8,128)(2,1)S(1)} collective-permute-done((bf16[4,128,256]{2,1,0:T(8,128)(2,1)S(1)}, bf16[4,128,256]{2,1,0:T(8,128)(2,1)S(1)}, u32[]{:S(2)}, u32[]{:S(2)}) %collective-permute-start.2) | collective-permute-done | bytes 262176 | tf_op jit(solution)/shard_map/aggregate/ppermute | solution.py:263
  99.6 1.7 dense.1
  101.9 2.9 %collective-permute-start.12 = (bf16[4,128,128]{2,1,0:T(8,128)(2,1)S(1)}, bf16[4,128,128]{2,1,0:T(8,128)(2,1)S(1)}, u32[]{:S(2)}, u32[]{:S(2)}) collective-permute-start(bf16[4,128,128]{2,1,0:T(8,128)(2,1)S(1)} %get-tuple-element.26.refs_0_), channel_id=1, source_target_pairs={{0,4},{2,6},{4,0},{6,2},{1,5},{3,7},{5,1},{7,3},{8,12},{10,14},{12... | collective-permute-start | bytes 393224 | tf_op jit(solution)/shard_map/backward/ppermute | solution.py:263
  106.3 4.4 %collective-permute-done.12.refs_2_ = bf16[4,128,128]{2,1,0:T(8,128)(2,1)S(1)} collective-permute-done((bf16[4,128,128]{2,1,0:T(8,128)(2,1)S(1)}, bf16[4,128,128]{2,1,0:T(8,128)(2,1)S(1)}, u32[]{:S(2)}, u32[]{:S(2)}) %collective-permute-start.12) | collective-permute-done | bytes 131104 | tf_op jit(solution)/shard_map/backward/ppermute | solution.py:263
  110.7 5.9 %all-to-all-start.1 = ((bf16[32,16,256]{2,1,0:T(8,128)(2,1)}), bf16[32,16,256]{2,1,0:T(8,128)(2,1)S(1)}, u32[]{:S(2)}, u32[]{:S(2)}) async-start(bf16[32,16,256]{2,1,0:T(8,128)(2,1)} %bitcast.15), calls=%async_computation.1 | async-start | bytes 524288 | tf_op jit(solution)/shard_map/backward/all_to_all | solution.py:310
  116.6 1.7 collective-permute-start.17
  120.8 6.9 %backward.3 = bf16[32,128,128]{2,1,0:T(8,128)(2,1)} custom-call(s32[256]{0:T(256)} %fusion.6.targets, s32[256]{0:T(256)} %get-tuple-element.38.places, s32[3]{0:T(128)} %pad_add_fusion.info, bf16[256,128,128]{2,1,0:T(8,128)(2,1)} %bitcast.31, bf16[4,128,128]{2,1,0:T(8,128)(2,1)} %copy-done.5, bf16[4,128,128]{2,1,0:T(8,128)(2,1)} %copy-done.9, ...), custom_call_target="tpu_custom_call" | custom-call | flops 2147483648 | bytes 12582912 | tf_op jit(solution)/shard_map/backward/backward/pallas_call | solution.py:123
  127.7 9.8 %all-to-all-start.3 = ((bf16[32,128,128]{2,1,0:T(8,128)(2,1)}), bf16[32,128,128]{2,1,0:T(8,128)(2,1)S(1)}, u32[]{:S(2)}, u32[]{:S(2)}) async-start(bf16[32,128,128]{2,1,0:T(8,128)(2,1)} %backward.3), calls=%async_computation.3 | async-start | bytes 2097152 | tf_op jit(solution)/shard_map/backward/all_to_all | solution.py:328
  137.6 5.5 %collective-permute-start.6 = (bf16[4,128,128]{2,1,0:T(8,128)(2,1)S(1)}, bf16[4,128,128]{2,1,0:T(8,128)(2,1)S(1)}, u32[]{:S(2)}, u32[]{:S(2)}) collective-permute-start(bf16[4,128,128]{2,1,0:T(8,128)(2,1)S(1)} %get-tuple-element.22.refs_0_), channel_id=1, source_target_pairs={{0,6},{2,0},{4,2},{6,4},{1,7},{3,1},{5,3},{7,5},{8,14},{10,8},{12,... | collective-permute-start | bytes 393224 | tf_op jit(solution)/shard_map/backward/ppermute | solution.py:263
  143.1 1.3 collective-permute-start.5
  144.5 1.2 collective-permute-done.14
  145.7 2.0 collective-permute-start.15
  147.7 1.5 collective-permute-done.15
  149.2 1.3 collective-permute-start.16
  152.2 1.3 collective-permute-done.16
  155.6 7.7 %backward.2 = bf16[32,160,128]{2,1,0:T(8,128)(2,1)} custom-call(s32[256]{0:T(256)} %fusion.6.targets, s32[256]{0:T(256)} %get-tuple-element.38.places, s32[3]{0:T(128)} %pad_add_fusion.info, bf16[256,128,128]{2,1,0:T(8,128)(2,1)} %bitcast.32, bf16[4,128,128]{2,1,0:T(8,128)(2,1)} %copy-done.7, bf16[4,128,128]{2,1,0:T(8,128)(2,1)} %copy-done.17, ...), custom_call_target="tpu_custom_call" | custom-call | flops 2147483648 | bytes 12582912 | tf_op jit(solution)/shard_map/backward/backward/pallas_call | solution.py:123
  163.4 9.7 %all-to-all-start.2 = ((bf16[32,160,128]{2,1,0:T(8,128)(2,1)}), bf16[32,160,128]{2,1,0:T(8,128)(2,1)S(1)}, u32[]{:S(2)}, u32[]{:S(2)}) async-start(bf16[32,160,128]{2,1,0:T(8,128)(2,1)} %backward.2), calls=%async_computation.2 | async-start | bytes 2621440 | tf_op jit(solution)/shard_map/backward/all_to_all | solution.py:328
  173.1 3.2 %place.2.refs_0_ = bf16[4,128,256]{2,1,0:T(8,128)(2,1)} custom-call(s32[32]{0:T(128)S(1)} %dynamic-slice_reduce_fusion.index, bf16[512,256]{1,0:T(8,128)(2,1)S(1)} %get-tuple-element.21.grad_pre, bf16[256,256]{1,0:T(8,128)(2,1)S(1)} %copy-done.1, bf16[32,128,128]{2,1,0:T(8,128)(2,1)S(1)} %all-to-all-done.3.returned), custom_call_target="tpu_custom_call" | custom-call | tf_op jit(solution)/shard_map/final/place/pallas_call | solution.py:208
  176.3 26.9 %all-to-all-done.2.returned = bf16[32,160,128]{2,1,0:T(8,128)(2,1)S(1)} async-done(((bf16[32,160,128]{2,1,0:T(8,128)(2,1)}), bf16[32,160,128]{2,1,0:T(8,128)(2,1)S(1)}, u32[]{:S(2)}, u32[]{:S(2)}) %all-to-all-start.2) | async-done | bytes 1310752 | tf_op jit(solution)/shard_map/backward/all_to_all | solution.py:328
  204.1 2.2 %place.3 = bf16[4,128,256]{2,1,0:T(8,128)(2,1)} custom-call(s32[32]{0:T(128)S(1)} %dynamic-slice_reduce_fusion.index, bf16[512,256]{1,0:T(8,128)(2,1)S(1)} %get-tuple-element.21.grad_pre, bf16[256,256]{1,0:T(8,128)(2,1)S(1)} %copy-done.1, bf16[32,160,128]{2,1,0:T(8,128)(2,1)S(1)} %all-to-all-done.2.returned, ...), custom_call_target="tpu_custom_call", output_to_operand_aliasing={{}: (4, {})} | custom-call | tf_op jit(solution)/shard_map/final/place/pallas_call | solution.py:208
  (87 shorter events, 13.3 us)
Async XLA Ops:
  5.3 60.7 %all-to-all-start = ((bf16[32,128,256]{2,1,0:T(8,128)(2,1)}), bf16[32,128,256]{2,1,0:T(8,128)(2,1)S(1)}, u32[]{:S(2)}, u32[]{:S(2)}) async-start(bf16[32,128,256]{2,1,0:T(8,128)(2,1)} %select.13), calls=%async_computation | async-start | bytes 4194304 | tf_op jit(solution)/shard_map/gather_columns/all_to_all | solution.py:287
  74.6 24.9 %copy-start.1 = (bf16[256,256]{1,0:T(8,128)(2,1)S(1)}, bf16[256,256]{1,0:T(8,128)(2,1)}, u32[]{:S(2)}) copy-start(bf16[256,256]{1,0:T(8,128)(2,1)} %w_self.5) | copy-start | bytes 393220
  74.6 24.9 %copy-start.3 = (bf16[512,256]{1,0:T(8,128)(2,1)S(1)}, bf16[512,256]{1,0:T(8,128)(2,1)}, u32[]{:S(2)}) copy-start(bf16[512,256]{1,0:T(8,128)(2,1)} %features.1) | copy-start | bytes 786436
  74.7 24.9 %copy-start.4 = (bf16[512,256]{1,0:T(8,128)(2,1)S(1)}, bf16[512,256]{1,0:T(8,128)(2,1)}, u32[]{:S(2)}) copy-start(bf16[512,256]{1,0:T(8,128)(2,1)} %cotangent.1) | copy-start | bytes 786436
  74.7 24.9 %copy-start.6 = (bf16[256,256]{1,0:T(8,128)(2,1)S(1)}, bf16[256,256]{1,0:T(8,128)(2,1)}, u32[]{:S(2)}) copy-start(bf16[256,256]{1,0:T(8,128)(2,1)} %w_neigh.1) | copy-start | bytes 393220
  74.7 6.5 %collective-permute-start = (bf16[4,4,128,256]{3,2,1,0:T(8,128)(2,1)}, bf16[4,4,128,256]{3,2,1,0:T(8,128)(2,1)S(1)}, u32[]{:S(2)}, u32[]{:S(2)}) collective-permute-start(bf16[4,4,128,256]{3,2,1,0:T(8,128)(2,1)} %get-tuple-element.19), channel_id=1, source_target_pairs={{0,1},{1,0},{2,3},{3,2},{4,5},{5,4},{6,7},{7,6},{8,9},{9,8},{10,11... | collective-permute-start | bytes 3145736 | tf_op jit(solution)/shard_map/aggregate/ppermute | solution.py:263
  81.2 37.7 %copy-start.23 = (s32[1,1,256]{2,1,0:T(1,128)S(1)}, s32[1,1,256]{2,1,0:T(1,128)}, u32[]{:S(2)}) copy-start(s32[1,1,256]{2,1,0:T(1,128)} %param.15) | copy-start | bytes 3076
  82.7 10.3 %collective-permute-start.1 = (bf16[4,128,256]{2,1,0:T(8,128)(2,1)S(1)}, bf16[4,128,256]{2,1,0:T(8,128)(2,1)S(1)}, u32[]{:S(2)}, u32[]{:S(2)}) collective-permute-start(bf16[4,128,256]{2,1,0:T(8,128)(2,1)S(1)} %get-tuple-element.34), channel_id=1, source_target_pairs={{0,2},{2,4},{4,6},{6,0},{1,3},{3,5},{5,7},{7,1},{8,10},{10,12},{12... | collective-permute-start | bytes 786440 | tf_op jit(solution)/shard_map/aggregate/ppermute | solution.py:263
  85.2 14.4 %collective-permute-start.2 = (bf16[4,128,256]{2,1,0:T(8,128)(2,1)S(1)}, bf16[4,128,256]{2,1,0:T(8,128)(2,1)S(1)}, u32[]{:S(2)}, u32[]{:S(2)}) collective-permute-start(bf16[4,128,256]{2,1,0:T(8,128)(2,1)S(1)} %get-tuple-element.33), channel_id=1, source_target_pairs={{0,4},{2,6},{4,0},{6,2},{1,5},{3,7},{5,1},{7,3},{8,12},{10,14},{12... | collective-permute-start | bytes 786440 | tf_op jit(solution)/shard_map/aggregate/ppermute | solution.py:263
  87.6 11.9 %collective-permute-start.3 = (bf16[4,128,256]{2,1,0:T(8,128)(2,1)S(1)}, bf16[4,128,256]{2,1,0:T(8,128)(2,1)S(1)}, u32[]{:S(2)}, u32[]{:S(2)}) collective-permute-start(bf16[4,128,256]{2,1,0:T(8,128)(2,1)S(1)} %get-tuple-element.32), channel_id=1, source_target_pairs={{0,6},{2,0},{4,2},{6,4},{1,7},{3,1},{5,3},{7,5},{8,14},{10,8},{12,... | collective-permute-start | bytes 786440 | tf_op jit(solution)/shard_map/aggregate/ppermute | solution.py:263
  101.3 18.9 %copy-start.5 = (bf16[4,128,128]{2,1,0:T(8,128)(2,1)}, bf16[4,128,128]{2,1,0:T(8,128)(2,1)S(1)}, u32[]{:S(2)}) copy-start(bf16[4,128,128]{2,1,0:T(8,128)(2,1)S(1)} %get-tuple-element.26.refs_0_) | copy-start | bytes 393220
  101.3 49.2 %copy-start.7 = (bf16[4,128,128]{2,1,0:T(8,128)(2,1)}, bf16[4,128,128]{2,1,0:T(8,128)(2,1)S(1)}, u32[]{:S(2)}) copy-start(bf16[4,128,128]{2,1,0:T(8,128)(2,1)S(1)} %get-tuple-element.22.refs_0_) | copy-start | bytes 393220
  101.3 5.0 %collective-permute-start.11 = (bf16[4,128,128]{2,1,0:T(8,128)(2,1)S(1)}, bf16[4,128,128]{2,1,0:T(8,128)(2,1)S(1)}, u32[]{:S(2)}, u32[]{:S(2)}) collective-permute-start(bf16[4,128,128]{2,1,0:T(8,128)(2,1)S(1)} %get-tuple-element.26.refs_0_), channel_id=1, source_target_pairs={{0,2},{2,4},{4,6},{6,0},{1,3},{3,5},{5,7},{7,1},{8,10},{10,12},{12... | collective-permute-start | bytes 393224 | tf_op jit(solution)/shard_map/backward/ppermute | solution.py:263
  101.9 8.8 %collective-permute-start.12 = (bf16[4,128,128]{2,1,0:T(8,128)(2,1)S(1)}, bf16[4,128,128]{2,1,0:T(8,128)(2,1)S(1)}, u32[]{:S(2)}, u32[]{:S(2)}) collective-permute-start(bf16[4,128,128]{2,1,0:T(8,128)(2,1)S(1)} %get-tuple-element.26.refs_0_), channel_id=1, source_target_pairs={{0,4},{2,6},{4,0},{6,2},{1,5},{3,7},{5,1},{7,3},{8,12},{10,14},{12... | collective-permute-start | bytes 393224 | tf_op jit(solution)/shard_map/backward/ppermute | solution.py:263
  104.8 5.9 %collective-permute-start.13 = (bf16[4,128,128]{2,1,0:T(8,128)(2,1)S(1)}, bf16[4,128,128]{2,1,0:T(8,128)(2,1)S(1)}, u32[]{:S(2)}, u32[]{:S(2)}) collective-permute-start(bf16[4,128,128]{2,1,0:T(8,128)(2,1)S(1)} %get-tuple-element.26.refs_0_), channel_id=1, source_target_pairs={{0,6},{2,0},{4,2},{6,4},{1,7},{3,1},{5,3},{7,5},{8,14},{10,8},{12,... | collective-permute-start | bytes 393224 | tf_op jit(solution)/shard_map/backward/ppermute | solution.py:263
  110.7 17.0 %all-to-all-start.1 = ((bf16[32,16,256]{2,1,0:T(8,128)(2,1)}), bf16[32,16,256]{2,1,0:T(8,128)(2,1)S(1)}, u32[]{:S(2)}, u32[]{:S(2)}) async-start(bf16[32,16,256]{2,1,0:T(8,128)(2,1)} %bitcast.15), calls=%async_computation.1 | async-start | bytes 524288 | tf_op jit(solution)/shard_map/backward/all_to_all | solution.py:310
  116.6 2.9 %collective-permute-start.17 = (bf16[4,128,128]{2,1,0:T(8,128)(2,1)S(1)}, bf16[4,128,128]{2,1,0:T(8,128)(2,1)S(1)}, u32[]{:S(2)}, u32[]{:S(2)}) collective-permute-start(bf16[4,128,128]{2,1,0:T(8,128)(2,1)S(1)} %get-tuple-element.26.refs_0_), channel_id=1, source_target_pairs={{0,1},{1,0},{2,3},{3,2},{4,5},{5,4},{6,7},{7,6},{8,9},{9,8},{10,11... | collective-permute-start | bytes 393224 | tf_op jit(solution)/shard_map/backward/ppermute | solution.py:263
  118.3 1.3 collective-permute-start.18
  118.4 1.4 collective-permute-start.19
  118.8 1.3 collective-permute-start.20
  127.7 35.6 %all-to-all-start.3 = ((bf16[32,128,128]{2,1,0:T(8,128)(2,1)}), bf16[32,128,128]{2,1,0:T(8,128)(2,1)S(1)}, u32[]{:S(2)}, u32[]{:S(2)}) async-start(bf16[32,128,128]{2,1,0:T(8,128)(2,1)} %backward.3), calls=%async_computation.3 | async-start | bytes 2097152 | tf_op jit(solution)/shard_map/backward/all_to_all | solution.py:328
  137.6 14.0 %collective-permute-start.6 = (bf16[4,128,128]{2,1,0:T(8,128)(2,1)S(1)}, bf16[4,128,128]{2,1,0:T(8,128)(2,1)S(1)}, u32[]{:S(2)}, u32[]{:S(2)}) collective-permute-start(bf16[4,128,128]{2,1,0:T(8,128)(2,1)S(1)} %get-tuple-element.22.refs_0_), channel_id=1, source_target_pairs={{0,6},{2,0},{4,2},{6,4},{1,7},{3,1},{5,3},{7,5},{8,14},{10,8},{12,... | collective-permute-start | bytes 393224 | tf_op jit(solution)/shard_map/backward/ppermute | solution.py:263
  143.1 8.6 %collective-permute-start.4 = (bf16[4,128,128]{2,1,0:T(8,128)(2,1)S(1)}, bf16[4,128,128]{2,1,0:T(8,128)(2,1)S(1)}, u32[]{:S(2)}, u32[]{:S(2)}) collective-permute-start(bf16[4,128,128]{2,1,0:T(8,128)(2,1)S(1)} %get-tuple-element.22.refs_0_), channel_id=1, source_target_pairs={{0,2},{2,4},{4,6},{6,0},{1,3},{3,5},{5,7},{7,1},{8,10},{10,12},{12... | collective-permute-start | bytes 393224 | tf_op jit(solution)/shard_map/backward/ppermute | solution.py:263
  143.1 9.0 %collective-permute-start.5 = (bf16[4,128,128]{2,1,0:T(8,128)(2,1)S(1)}, bf16[4,128,128]{2,1,0:T(8,128)(2,1)S(1)}, u32[]{:S(2)}, u32[]{:S(2)}) collective-permute-start(bf16[4,128,128]{2,1,0:T(8,128)(2,1)S(1)} %get-tuple-element.22.refs_0_), channel_id=1, source_target_pairs={{0,4},{2,6},{4,0},{6,2},{1,5},{3,7},{5,1},{7,3},{8,12},{10,14},{12... | collective-permute-start | bytes 393224 | tf_op jit(solution)/shard_map/backward/ppermute | solution.py:263
  144.4 1.3 collective-permute-start.14
  145.7 3.5 %collective-permute-start.15 = (f32[16,256]{1,0:T(8,128)S(1)}, f32[16,256]{1,0:T(8,128)S(1)}, u32[]{:S(2)}, u32[]{:S(2)}) collective-permute-start(f32[16,256]{1,0:T(8,128)S(1)} %add.68), channel_id=1, source_target_pairs={{0,2},{2,0},{4,6},{6,4},{1,3},{3,1},{5,7},{7,5},{8,10},{10,8},{12,... | collective-permute-start | bytes 49160 | tf_op jit(solution)/shard_map/backward/ppermute | solution.py:267
  149.2 4.4 %collective-permute-start.16 = (f32[16,256]{1,0:T(8,128)S(1)}, f32[16,256]{1,0:T(8,128)S(1)}, u32[]{:S(2)}, u32[]{:S(2)}) collective-permute-start(f32[16,256]{1,0:T(8,128)S(1)} %add.69), channel_id=1, source_target_pairs={{0,4},{2,6},{4,0},{6,2},{1,5},{3,7},{5,1},{7,3},{8,12},{10,14},{12... | collective-permute-start | bytes 49160 | tf_op jit(solution)/shard_map/backward/ppermute | solution.py:267
  150.4 3.7 %collective-permute-start.7 = (bf16[4,128,128]{2,1,0:T(8,128)(2,1)S(1)}, bf16[4,128,128]{2,1,0:T(8,128)(2,1)S(1)}, u32[]{:S(2)}, u32[]{:S(2)}) collective-permute-start(bf16[4,128,128]{2,1,0:T(8,128)(2,1)S(1)} %get-tuple-element.22.refs_0_), channel_id=1, source_target_pairs={{0,1},{1,0},{2,3},{3,2},{4,5},{5,4},{6,7},{7,6},{8,9},{9,8},{10,11... | collective-permute-start | bytes 393224 | tf_op jit(solution)/shard_map/backward/ppermute | solution.py:263
  151.6 2.6 %collective-permute-start.10 = (bf16[4,128,128]{2,1,0:T(8,128)(2,1)S(1)}, bf16[4,128,128]{2,1,0:T(8,128)(2,1)S(1)}, u32[]{:S(2)}, u32[]{:S(2)}) collective-permute-start(bf16[4,128,128]{2,1,0:T(8,128)(2,1)S(1)} %collective-permute-done.6.refs_3_), channel_id=1, source_target_pairs={{0,1},{1,0},{2,3},{3,2},{4,5},{5,4},{6,7},{7,6},{8,9},{9,8},{10,11... | collective-permute-start | bytes 393224 | tf_op jit(solution)/shard_map/backward/ppermute | solution.py:263
  151.7 2.5 %collective-permute-start.8 = (bf16[4,128,128]{2,1,0:T(8,128)(2,1)S(1)}, bf16[4,128,128]{2,1,0:T(8,128)(2,1)S(1)}, u32[]{:S(2)}, u32[]{:S(2)}) collective-permute-start(bf16[4,128,128]{2,1,0:T(8,128)(2,1)S(1)} %collective-permute-done.4.refs_1_), channel_id=1, source_target_pairs={{0,1},{1,0},{2,3},{3,2},{4,5},{5,4},{6,7},{7,6},{8,9},{9,8},{10,11... | collective-permute-start | bytes 393224 | tf_op jit(solution)/shard_map/backward/ppermute | solution.py:263
  152.1 2.1 %collective-permute-start.9 = (bf16[4,128,128]{2,1,0:T(8,128)(2,1)S(1)}, bf16[4,128,128]{2,1,0:T(8,128)(2,1)S(1)}, u32[]{:S(2)}, u32[]{:S(2)}) collective-permute-start(bf16[4,128,128]{2,1,0:T(8,128)(2,1)S(1)} %collective-permute-done.5.refs_2_), channel_id=1, source_target_pairs={{0,1},{1,0},{2,3},{3,2},{4,5},{5,4},{6,7},{7,6},{8,9},{9,8},{10,11... | collective-permute-start | bytes 393224 | tf_op jit(solution)/shard_map/backward/ppermute | solution.py:263
  163.4 39.9 %all-to-all-start.2 = ((bf16[32,160,128]{2,1,0:T(8,128)(2,1)}), bf16[32,160,128]{2,1,0:T(8,128)(2,1)S(1)}, u32[]{:S(2)}, u32[]{:S(2)}) async-start(bf16[32,160,128]{2,1,0:T(8,128)(2,1)} %backward.2), calls=%async_computation.2 | async-start | bytes 2621440 | tf_op jit(solution)/shard_map/backward/all_to_all | solution.py:328
  (18 other events, 62.2 us)

commit v3 on v2

--- a/solution.py
+++ b/solution.py
@@ -14,7 +14,9 @@
 PARTS = 2
 WIDTH = 256 // PARTS
 BLOCK = 16
-VMEM_LIMIT = 54 * 2**20
+GROUP = 32
+AHEAD = 8
+VMEM_LIMIT = 48 * 2**20
 AXES = ("z", "y", "x", "c")
 SIZES = (8, 4, 4, 2)
 DOM = ("z", "y")
@@ -52,28 +54,37 @@
 
 
 def accumulate_slots(used, values, tiles, total, sems, piece_copies, add_slot):
+    blocks = values.shape[0] // BLOCK
+
+    def copy_of(b):
+        span = pl.ds(b * BLOCK, BLOCK)
+        return pltpu.make_async_copy(values.at[span], tiles.at[span], sems.at[b])
+
     for copy in piece_copies:
         copy.start()
-    for copy in copies_of(values, tiles, BLOCK, sems):
-        copy.start()
+    for b in range(AHEAD):
+        copy_of(b).start()
     total[...] = jnp.zeros_like(total)
     for copy in piece_copies:
         copy.wait()
 
-    def block(b, carry):
-        first = b * BLOCK
-        pltpu.make_async_copy(
-            values.at[pl.ds(first, BLOCK)], tiles.at[pl.ds(first, BLOCK)], sems.at[b]
-        ).wait()
-
-        @pl.when(first < used)
+    def group(g, carry):
+        for i in range(GROUP // BLOCK):
+            b = g * (GROUP // BLOCK) + i
+            copy_of(b).wait()
+
+            @pl.when(b + AHEAD < blocks)
+            def _():
+                copy_of(b + AHEAD).start()
+
+        @pl.when(g * GROUP < used)
         def _():
-            for u in range(BLOCK):
-                add_slot(first + u)
+            for u in range(GROUP):
+                add_slot(g * GROUP + u)
 
         return carry
 
-    lax.fori_loop(0, values.shape[0] // BLOCK, block, 0)
+    lax.fori_loop(0, values.shape[0] // GROUP, group, 0)
 
 
 def forward_kernel(targets, places, info, values, columns, keep, send, tiles, total, sems):
@@ -90,7 +101,7 @@
 
 
 def backward_kernel(targets, places, info, values, *refs):
-    pieces, (out, tiles, total, sems, held, piece_sems) = refs[:8], refs[-6:]
+    pieces, (out, tiles, total, sems, held, piece_sems, rounded) = refs[:8], refs[-7:]
 
     def add_slot(k):
         total[targets[k]] += jnp.dot(held[places[k]], tiles[k], preferred_element_type=F32)
@@ -100,10 +111,16 @@
         for i, piece in enumerate(pieces)
     ]
     accumulate_slots(info[0], values, tiles, total, sems, piece_copies, add_slot)
-    out[:, :WIDTH, :] = total[:32].astype(BF16)
-    for share in refs[8:-6]:
-        for i in range(32):
-            out[i, WIDTH:, :] = share[...]
+    copies = copies_of(rounded, out, 4, piece_sems)
+    for i, copy in enumerate(copies):
+        span = slice(4 * i, 4 * i + 4)
+        rounded[span, :WIDTH, :] = total[span].astype(BF16)
+        for share in refs[8:-7]:
+            for j in range(4 * i, 4 * i + 4):
+                rounded[j, WIDTH:, :] = share[...]
+        copy.start()
+    for copy in copies:
+        copy.wait()
 
 
 def over_slots(kernel, name, out_shapes, targets, places, info, values, pieces, extra=()):
@@ -118,6 +135,7 @@
         scratch += [
             pltpu.VMEM((32,) + tile, BF16),
             pltpu.SemaphoreType.DMA((len(pieces),)),
+            pltpu.VMEM(out_shapes[0], BF16),
         ]
     piece_space = pl.ANY if len(pieces) > 1 else pltpu.VMEM
     return pl.pallas_call(
@@ -129,7 +147,7 @@
             in_specs=[pl.BlockSpec(memory_space=pltpu.HBM)]
             + [pl.BlockSpec(memory_space=piece_space)] * len(pieces)
             + [pl.BlockSpec(memory_space=pltpu.VMEM)] * len(extra),
-            out_specs=[pl.BlockSpec(memory_space=pltpu.VMEM)] * len(out_shapes),
+            out_specs=[pl.BlockSpec(memory_space=piece_space)] * len(out_shapes),
             scratch_shapes=scratch,
         ),
         compiler_params=pltpu.CompilerParams(vmem_limit_bytes=VMEM_LIMIT),
@@ -303,10 +321,13 @@
     with jax.named_scope("backward"):
         returned = []
         for h, part in enumerate(grad_aggs):
-            behind = [part] + [shift(part, "x", k) for k in (1, 2, 3)]
+            behind = [part, shift(part, "x", 1), None, shift(part, "x", 3)]
+            behind[2] = shift(behind[1], "x", 1)
             pieces, extra = list(behind), []
             if h == 0:
-                local_weights, *pieces[:4] = lax.optimization_barrier((local_weights, *pieces[:4]))
+                local_weights, pieces[1], pieces[3] = lax.optimization_barrier(
+                    (local_weights, pieces[1], pieces[3])
+                )
                 local_weights = lax.all_to_all(
                     local_weights.reshape(32, 16, 256), DOM, 0, 0, tiled=True
                 )

time: 211 us -> 198 us (0.938); the launches traced: 206 us -> 196 us
  starting transfers between devices: 66 us -> 58.3 us
  waiting for transfers between devices: 96.9 us -> 103 us
  other arithmetic: 3.91 us -> 0.48 us
  local copies, waits for them, and re-layouts: 5.94 us -> 2.61 us
    ppermute x18, starting transfers between devices: 25.1 us -> 18.7 us  [shift(): return lax.ppermute(a, axis, [(i, (i + by) % size) for i in range(size)])]
    all_to_all x2, waiting for transfers between devices: 27 us -> 32.4 us  [body(): returned.append(lax.all_to_all(neighbour, DOM, 0, 0, tiled=True))]
    all_to_all x2, starting transfers between devices: 19.5 us -> 15.6 us  [body(): returned.append(lax.all_to_all(neighbour, DOM, 0, 0, tiled=True))]
    unnamed x50 -> x16, local copies, waits for them, and re-layouts: 5.2 us -> 1.88 us
  transfers between devices with their start and end apart: 25 -> 25, of which waited for: 14 -> 17; matrix products, arithmetic and copies ran while one was open for 1% -> 0% of each run, Pallas kernels for 9% -> 9%
where the time goes in v3:
time: 198 us; the launch traced here: 196 us
  waiting for transfers between devices  103 us (52%)
  starting transfers between devices  58.3 us (29%)
  Pallas kernels  29.8 us (15%)
  local copies, waits for them, and re-layouts  2.61 us (1%)
    all_to_all x1, waiting for transfers between devices, body(): columns = lax.all_to_all(outgoing, DOM, 0, 0, tiled=True)  47.7 us
    all_to_all x2, waiting for transfers between devices, body(): returned.append(lax.all_to_all(neighbour, DOM, 0, 0, tiled=True))  32.4 us
    ppermute x18, waiting for transfers between devices, shift(): return lax.ppermute(a, axis, [(i, (i + by) % size) for i in range(size)])  20.8 us
    pallas_call x3, Pallas kernels, over_slots(): pl.pallas_call(kernel, out_shape=[jax.ShapeDtypeStruct(shape, BF16) for s...  19.9 us
    ppermute x18, starting transfers between devices, shift(): return lax.ppermute(a, axis, [(i, (i + by) % size) for i in range(size)])  18.7 us
    all_to_all x2, starting transfers between devices, body(): returned.append(lax.all_to_all(neighbour, DOM, 0, 0, tiled=True))  15.6 us
    all_to_all x1, starting transfers between devices, body(): columns = lax.all_to_all(outgoing, DOM, 0, 0, tiled=True)  12.2 us
    all_to_all x1, starting transfers between devices, body(): lax.all_to_all(local_weights.reshape(32, 16, 256), DOM, 0, 0, tiled=True)  6.36 us
  transfers between devices with their start and end apart: 25, of which 17 were waited for; matrix products, arithmetic and copies ran while one was open for 0% of the time, Pallas kernels for 9%

profile of v3, /device:TPU:1, one launch (start us, length us, event | category | flops | bytes accessed | tf_op | source)
XLA Modules:
  0.0 196.3 jit_solution(14147767604318987192)
XLA Ops:
  3.2 2.0 %select.13 = bf16[32,128,256]{2,1,0:T(8,128)(2,1)} custom-call(s32[32]{0:T(128)S(1)} %dynamic-slice_reduce_fusion.index, bf16[4,128,256]{2,1,0:T(8,128)(2,1)S(1)} %bitcast.25), custom_call_target="tpu_custom_call" | custom-call | tf_op jit(solution)/shard_map/gather_columns/select/pallas_call | solution.py:32
  5.3 12.2 %all-to-all-start = ((bf16[32,128,256]{2,1,0:T(8,128)(2,1)}), bf16[32,128,256]{2,1,0:T(8,128)(2,1)S(1)}, u32[]{:S(2)}, u32[]{:S(2)}) async-start(bf16[32,128,256]{2,1,0:T(8,128)(2,1)} %select.13), calls=%async_computation | async-start | bytes 4194304 | tf_op jit(solution)/shard_map/gather_columns/all_to_all | solution.py:305
  18.2 47.7 %all-to-all-done.columns = bf16[32,128,256]{2,1,0:T(8,128)(2,1)S(1)} async-done(((bf16[32,128,256]{2,1,0:T(8,128)(2,1)}), bf16[32,128,256]{2,1,0:T(8,128)(2,1)S(1)}, u32[]{:S(2)}, u32[]{:S(2)}) %all-to-all-start) | async-done | bytes 2097184 | tf_op jit(solution)/shard_map/gather_columns/all_to_all | solution.py:305
  65.9 5.5 %forward.1 = (bf16[4,4,128,256]{3,2,1,0:T(8,128)(2,1)S(1)}, bf16[4,4,128,256]{3,2,1,0:T(8,128)(2,1)S(1)}) custom-call(s32[256]{0:T(256)S(1)} %get-tuple-element.35.targets, s32[256]{0:T(256)S(1)} %bitcast.30, s32[3]{0:T(128)S(1)} %pad_add_fusion.info, bf16[256,128,128]{2,1,0:T(8,128)(2,1)} %bitcast.32, bf16[32,128,256]{2,1,0:T(8,128)(2,1)S(1)} %all-to-all-done.columns), custom_call_target="tpu_custom_call" | custom-call | flops 2147483648 | bytes 12582912 | tf_op jit(solution)/shard_map/aggregate/forward/pallas_call | solution.py:141
  71.5 2.7 %collective-permute-start = (bf16[4,4,128,256]{3,2,1,0:T(8,128)(2,1)S(1)}, bf16[4,4,128,256]{3,2,1,0:T(8,128)(2,1)S(1)}, u32[]{:S(2)}, u32[]{:S(2)}) collective-permute-start(bf16[4,4,128,256]{3,2,1,0:T(8,128)(2,1)S(1)} %get-tuple-element.17), channel_id=1, source_target_pairs={{0,1},{1,0},{2,3},{3,2},{4,5},{5,4},{6,7},{7,6},{8,9},{9,8},{10,11... | collective-permute-start | bytes 3145736 | tf_op jit(solution)/shard_map/aggregate/ppermute | solution.py:281
  74.3 2.3 %collective-permute-done = bf16[4,4,128,256]{3,2,1,0:T(8,128)(2,1)S(1)} collective-permute-done((bf16[4,4,128,256]{3,2,1,0:T(8,128)(2,1)S(1)}, bf16[4,4,128,256]{3,2,1,0:T(8,128)(2,1)S(1)}, u32[]{:S(2)}, u32[]{:S(2)}) %collective-permute-start) | collective-permute-done | bytes 1048608 | tf_op jit(solution)/shard_map/aggregate/ppermute | solution.py:281
  76.9 1.3 collective-permute-start.1
  78.2 2.0 %collective-permute-start.2 = (bf16[4,128,256]{2,1,0:T(8,128)(2,1)S(1)}, bf16[4,128,256]{2,1,0:T(8,128)(2,1)S(1)}, u32[]{:S(2)}, u32[]{:S(2)}) collective-permute-start(bf16[4,128,256]{2,1,0:T(8,128)(2,1)S(1)} %get-tuple-element.29), channel_id=1, source_target_pairs={{0,4},{2,6},{4,0},{6,2},{1,5},{3,7},{5,1},{7,3},{8,12},{10,14},{12... | collective-permute-start | bytes 786440 | tf_op jit(solution)/shard_map/aggregate/ppermute | solution.py:281
  80.2 1.6 collective-permute-start.3
  81.8 3.9 %collective-permute-done.1 = bf16[4,128,256]{2,1,0:T(8,128)(2,1)S(1)} collective-permute-done((bf16[4,128,256]{2,1,0:T(8,128)(2,1)S(1)}, bf16[4,128,256]{2,1,0:T(8,128)(2,1)S(1)}, u32[]{:S(2)}, u32[]{:S(2)}) %collective-permute-start.1) | collective-permute-done | bytes 262176 | tf_op jit(solution)/shard_map/aggregate/ppermute | solution.py:281
  85.7 6.2 %collective-permute-done.2 = bf16[4,128,256]{2,1,0:T(8,128)(2,1)S(1)} collective-permute-done((bf16[4,128,256]{2,1,0:T(8,128)(2,1)S(1)}, bf16[4,128,256]{2,1,0:T(8,128)(2,1)S(1)}, u32[]{:S(2)}, u32[]{:S(2)}) %collective-permute-start.2) | collective-permute-done | bytes 262176 | tf_op jit(solution)/shard_map/aggregate/ppermute | solution.py:281
  91.9 1.6 dense.1
  93.5 1.4 collective-permute-start.11
  95.0 1.7 collective-permute-start.12
  96.6 2.7 %collective-permute-done.11.refs_1_ = bf16[4,128,128]{2,1,0:T(8,128)(2,1)S(1)} collective-permute-done((bf16[4,128,128]{2,1,0:T(8,128)(2,1)S(1)}, bf16[4,128,128]{2,1,0:T(8,128)(2,1)S(1)}, u32[]{:S(2)}, u32[]{:S(2)}) %collective-permute-start.11) | collective-permute-done | bytes 131104 | tf_op jit(solution)/shard_map/backward/ppermute | solution.py:281
  99.4 6.4 %all-to-all-start.1 = ((bf16[32,16,256]{2,1,0:T(8,128)(2,1)}), bf16[32,16,256]{2,1,0:T(8,128)(2,1)S(1)}, u32[]{:S(2)}, u32[]{:S(2)}) async-start(bf16[32,16,256]{2,1,0:T(8,128)(2,1)} %bitcast.15), calls=%async_computation.1 | async-start | bytes 524288 | tf_op jit(solution)/shard_map/backward/all_to_all | solution.py:331
  105.7 2.4 %collective-permute-start.17 = (bf16[4,128,128]{2,1,0:T(8,128)(2,1)S(1)}, bf16[4,128,128]{2,1,0:T(8,128)(2,1)S(1)}, u32[]{:S(2)}, u32[]{:S(2)}) collective-permute-start(bf16[4,128,128]{2,1,0:T(8,128)(2,1)S(1)} %get-tuple-element.22.refs_0_), channel_id=1, source_target_pairs={{0,1},{1,0},{2,3},{3,2},{4,5},{5,4},{6,7},{7,6},{8,9},{9,8},{10,11... | collective-permute-start | bytes 393224 | tf_op jit(solution)/shard_map/backward/ppermute | solution.py:281
  110.0 7.1 %backward.3 = bf16[32,128,128]{2,1,0:T(8,128)(2,1)} custom-call(s32[256]{0:T(256)S(1)} %fusion.6.targets, s32[256]{0:T(256)S(1)} %get-tuple-element.34.places, s32[3]{0:T(128)S(1)} %pad_add_fusion.info, bf16[256,128,128]{2,1,0:T(8,128)(2,1)} %bitcast.33, bf16[4,128,128]{2,1,0:T(8,128)(2,1)S(1)} %get-tuple-element.22.refs_0_, ...), custom_call_target="tpu_custom_call" | custom-call | flops 2147483648 | bytes 12582912 | tf_op jit(solution)/shard_map/backward/backward/pallas_call | solution.py:141
  117.1 9.7 %all-to-all-start.3 = ((bf16[32,128,128]{2,1,0:T(8,128)(2,1)}), bf16[32,128,128]{2,1,0:T(8,128)(2,1)S(1)}, u32[]{:S(2)}, u32[]{:S(2)}) async-start(bf16[32,128,128]{2,1,0:T(8,128)(2,1)} %backward.3), calls=%async_computation.3 | async-start | bytes 2097152 | tf_op jit(solution)/shard_map/backward/all_to_all | solution.py:349
  127.4 2.4 %collective-permute-start.6 = (bf16[4,128,128]{2,1,0:T(8,128)(2,1)S(1)}, bf16[4,128,128]{2,1,0:T(8,128)(2,1)S(1)}, u32[]{:S(2)}, u32[]{:S(2)}) collective-permute-start(bf16[4,128,128]{2,1,0:T(8,128)(2,1)S(1)} %get-tuple-element.20.refs_0_), channel_id=1, source_target_pairs={{0,6},{2,0},{4,2},{6,4},{1,7},{3,1},{5,3},{7,5},{8,14},{10,8},{12,... | collective-permute-start | bytes 393224 | tf_op jit(solution)/shard_map/backward/ppermute | solution.py:281
  129.8 3.2 %collective-permute-done.4.refs_1_ = bf16[4,128,128]{2,1,0:T(8,128)(2,1)S(1)} collective-permute-done((bf16[4,128,128]{2,1,0:T(8,128)(2,1)S(1)}, bf16[4,128,128]{2,1,0:T(8,128)(2,1)S(1)}, u32[]{:S(2)}, u32[]{:S(2)}) %collective-permute-start.4) | collective-permute-done | bytes 131104 | tf_op jit(solution)/shard_map/backward/ppermute | solution.py:281
  133.0 1.3 collective-permute-start.13
  135.1 1.2 collective-permute-start.14
  136.3 1.7 collective-permute-done.14
  138.0 2.9 %collective-permute-start.15 = (f32[16,256]{1,0:T(8,128)S(1)}, f32[16,256]{1,0:T(8,128)S(1)}, u32[]{:S(2)}, u32[]{:S(2)}) collective-permute-start(f32[16,256]{1,0:T(8,128)S(1)} %add.69), channel_id=1, source_target_pairs={{0,4},{2,6},{4,0},{6,2},{1,5},{3,7},{5,1},{7,3},{8,12},{10,14},{12... | collective-permute-start | bytes 49160 | tf_op jit(solution)/shard_map/backward/ppermute | solution.py:285
  140.9 1.5 collective-permute-start.7
  144.3 7.2 %backward.2 = bf16[32,160,128]{2,1,0:T(8,128)(2,1)} custom-call(s32[256]{0:T(256)S(1)} %fusion.6.targets, s32[256]{0:T(256)S(1)} %get-tuple-element.34.places, s32[3]{0:T(128)S(1)} %pad_add_fusion.info, bf16[256,128,128]{2,1,0:T(8,128)(2,1)} %bitcast.34, bf16[4,128,128]{2,1,0:T(8,128)(2,1)S(1)} %get-tuple-element.20.refs_0_, ...), custom_call_target="tpu_custom_call" | custom-call | flops 2147483648 | bytes 12582912 | tf_op jit(solution)/shard_map/backward/backward/pallas_call | solution.py:141
  151.5 3.3 %all-to-all-done.3.returned = bf16[32,128,128]{2,1,0:T(8,128)(2,1)S(1)} async-done(((bf16[32,128,128]{2,1,0:T(8,128)(2,1)}), bf16[32,128,128]{2,1,0:T(8,128)(2,1)S(1)}, u32[]{:S(2)}, u32[]{:S(2)}) %all-to-all-start.3) | async-done | bytes 1048608 | tf_op jit(solution)/shard_map/backward/all_to_all | solution.py:349
  154.8 5.9 %all-to-all-start.2 = ((bf16[32,160,128]{2,1,0:T(8,128)(2,1)}), bf16[32,160,128]{2,1,0:T(8,128)(2,1)S(1)}, u32[]{:S(2)}, u32[]{:S(2)}) async-start(bf16[32,160,128]{2,1,0:T(8,128)(2,1)} %backward.2), calls=%async_computation.2 | async-start | bytes 2621440 | tf_op jit(solution)/shard_map/backward/all_to_all | solution.py:349
  160.8 3.2 %place.2.refs_0_ = bf16[4,128,256]{2,1,0:T(8,128)(2,1)} custom-call(s32[32]{0:T(128)S(1)} %dynamic-slice_reduce_fusion.index, bf16[512,256]{1,0:T(8,128)(2,1)S(1)} %get-tuple-element.19.grad_pre, bf16[256,256]{1,0:T(8,128)(2,1)S(1)} %copy-done.1, bf16[32,128,128]{2,1,0:T(8,128)(2,1)S(1)} %all-to-all-done.3.returned), custom_call_target="tpu_custom_call" | custom-call | tf_op jit(solution)/shard_map/final/place/pallas_call | solution.py:226
  164.0 29.1 %all-to-all-done.2.returned = bf16[32,160,128]{2,1,0:T(8,128)(2,1)S(1)} async-done(((bf16[32,160,128]{2,1,0:T(8,128)(2,1)}), bf16[32,160,128]{2,1,0:T(8,128)(2,1)S(1)}, u32[]{:S(2)}, u32[]{:S(2)}) %all-to-all-start.2) | async-done | bytes 1310752 | tf_op jit(solution)/shard_map/backward/all_to_all | solution.py:349
  193.9 2.2 %place.3 = bf16[4,128,256]{2,1,0:T(8,128)(2,1)} custom-call(s32[32]{0:T(128)S(1)} %dynamic-slice_reduce_fusion.index, bf16[512,256]{1,0:T(8,128)(2,1)S(1)} %get-tuple-element.19.grad_pre, bf16[256,256]{1,0:T(8,128)(2,1)S(1)} %copy-done.1, bf16[32,160,128]{2,1,0:T(8,128)(2,1)S(1)} %all-to-all-done.2.returned, ...), custom_call_target="tpu_custom_call", output_to_operand_aliasing={{}: (4, {})} | custom-call | tf_op jit(solution)/shard_map/final/place/pallas_call | solution.py:226
  (53 shorter events, 9.1 us)
Async XLA Ops:
  2.3 1.0 copy-start.2
  5.3 12.9 %copy-start.7 = (s32[1,1,256]{2,1,0:T(1,128)S(1)}, s32[1,1,256]{2,1,0:T(1,128)}, u32[]{:S(2)}) copy-start(s32[1,1,256]{2,1,0:T(1,128)} %param.14) | copy-start | bytes 3076
  5.3 60.7 %copy-start.6 = (s32[1,1,256]{2,1,0:T(1,128)S(1)}, s32[1,1,256]{2,1,0:T(1,128)}, u32[]{:S(2)}) copy-start(s32[1,1,256]{2,1,0:T(1,128)} %param.15) | copy-start | bytes 3076
  5.3 60.7 %all-to-all-start = ((bf16[32,128,256]{2,1,0:T(8,128)(2,1)}), bf16[32,128,256]{2,1,0:T(8,128)(2,1)S(1)}, u32[]{:S(2)}, u32[]{:S(2)}) async-start(bf16[32,128,256]{2,1,0:T(8,128)(2,1)} %select.13), calls=%async_computation | async-start | bytes 4194304 | tf_op jit(solution)/shard_map/gather_columns/all_to_all | solution.py:305
  71.5 20.4 %copy-start.1 = (bf16[256,256]{1,0:T(8,128)(2,1)S(1)}, bf16[256,256]{1,0:T(8,128)(2,1)}, u32[]{:S(2)}) copy-start(bf16[256,256]{1,0:T(8,128)(2,1)} %w_self.5) | copy-start | bytes 393220
  71.5 20.4 %copy-start.3 = (bf16[512,256]{1,0:T(8,128)(2,1)S(1)}, bf16[512,256]{1,0:T(8,128)(2,1)}, u32[]{:S(2)}) copy-start(bf16[512,256]{1,0:T(8,128)(2,1)} %features.1) | copy-start | bytes 786436
  71.5 20.4 %copy-start.4 = (bf16[512,256]{1,0:T(8,128)(2,1)S(1)}, bf16[512,256]{1,0:T(8,128)(2,1)}, u32[]{:S(2)}) copy-start(bf16[512,256]{1,0:T(8,128)(2,1)} %cotangent.1) | copy-start | bytes 786436
  71.5 20.4 %copy-start.5 = (bf16[256,256]{1,0:T(8,128)(2,1)S(1)}, bf16[256,256]{1,0:T(8,128)(2,1)}, u32[]{:S(2)}) copy-start(bf16[256,256]{1,0:T(8,128)(2,1)} %w_neigh.1) | copy-start | bytes 393220
  71.5 5.0 %collective-permute-start = (bf16[4,4,128,256]{3,2,1,0:T(8,128)(2,1)S(1)}, bf16[4,4,128,256]{3,2,1,0:T(8,128)(2,1)S(1)}, u32[]{:S(2)}, u32[]{:S(2)}) collective-permute-start(bf16[4,4,128,256]{3,2,1,0:T(8,128)(2,1)S(1)} %get-tuple-element.17), channel_id=1, source_target_pairs={{0,1},{1,0},{2,3},{3,2},{4,5},{5,4},{6,7},{7,6},{8,9},{9,8},{10,11... | collective-permute-start | bytes 3145736 | tf_op jit(solution)/shard_map/aggregate/ppermute | solution.py:281
  76.9 8.8 %collective-permute-start.1 = (bf16[4,128,256]{2,1,0:T(8,128)(2,1)S(1)}, bf16[4,128,256]{2,1,0:T(8,128)(2,1)S(1)}, u32[]{:S(2)}, u32[]{:S(2)}) collective-permute-start(bf16[4,128,256]{2,1,0:T(8,128)(2,1)S(1)} %get-tuple-element.30), channel_id=1, source_target_pairs={{0,2},{2,4},{4,6},{6,0},{1,3},{3,5},{5,7},{7,1},{8,10},{10,12},{12... | collective-permute-start | bytes 786440 | tf_op jit(solution)/shard_map/aggregate/ppermute | solution.py:281
  78.2 13.7 %collective-permute-start.2 = (bf16[4,128,256]{2,1,0:T(8,128)(2,1)S(1)}, bf16[4,128,256]{2,1,0:T(8,128)(2,1)S(1)}, u32[]{:S(2)}, u32[]{:S(2)}) collective-permute-start(bf16[4,128,256]{2,1,0:T(8,128)(2,1)S(1)} %get-tuple-element.29), channel_id=1, source_target_pairs={{0,4},{2,6},{4,0},{6,2},{1,5},{3,7},{5,1},{7,3},{8,12},{10,14},{12... | collective-permute-start | bytes 786440 | tf_op jit(solution)/shard_map/aggregate/ppermute | solution.py:281
  80.2 11.7 %collective-permute-start.3 = (bf16[4,128,256]{2,1,0:T(8,128)(2,1)S(1)}, bf16[4,128,256]{2,1,0:T(8,128)(2,1)S(1)}, u32[]{:S(2)}, u32[]{:S(2)}) collective-permute-start(bf16[4,128,256]{2,1,0:T(8,128)(2,1)S(1)} %get-tuple-element.28), channel_id=1, source_target_pairs={{0,6},{2,0},{4,2},{6,4},{1,7},{3,1},{5,3},{7,5},{8,14},{10,8},{12,... | collective-permute-start | bytes 786440 | tf_op jit(solution)/shard_map/aggregate/ppermute | solution.py:281
  93.5 5.8 %collective-permute-start.11 = (bf16[4,128,128]{2,1,0:T(8,128)(2,1)S(1)}, bf16[4,128,128]{2,1,0:T(8,128)(2,1)S(1)}, u32[]{:S(2)}, u32[]{:S(2)}) collective-permute-start(bf16[4,128,128]{2,1,0:T(8,128)(2,1)S(1)} %get-tuple-element.22.refs_0_), channel_id=1, source_target_pairs={{0,2},{2,4},{4,6},{6,0},{1,3},{3,5},{5,7},{7,1},{8,10},{10,12},{12... | collective-permute-start | bytes 393224 | tf_op jit(solution)/shard_map/backward/ppermute | solution.py:281
  95.0 4.4 %collective-permute-start.12 = (bf16[4,128,128]{2,1,0:T(8,128)(2,1)S(1)}, bf16[4,128,128]{2,1,0:T(8,128)(2,1)S(1)}, u32[]{:S(2)}, u32[]{:S(2)}) collective-permute-start(bf16[4,128,128]{2,1,0:T(8,128)(2,1)S(1)} %get-tuple-element.22.refs_0_), channel_id=1, source_target_pairs={{0,6},{2,0},{4,2},{6,4},{1,7},{3,1},{5,3},{7,5},{8,14},{10,8},{12,... | collective-permute-start | bytes 393224 | tf_op jit(solution)/shard_map/backward/ppermute | solution.py:281
  99.4 9.2 %collective-permute-start.16 = (bf16[4,128,128]{2,1,0:T(8,128)(2,1)S(1)}, bf16[4,128,128]{2,1,0:T(8,128)(2,1)S(1)}, u32[]{:S(2)}, u32[]{:S(2)}) collective-permute-start(bf16[4,128,128]{2,1,0:T(8,128)(2,1)S(1)} %collective-permute-done.11.refs_1_), channel_id=1, source_target_pairs={{0,2},{2,4},{4,6},{6,0},{1,3},{3,5},{5,7},{7,1},{8,10},{10,12},{12... | collective-permute-start | bytes 393224 | tf_op jit(solution)/shard_map/backward/ppermute | solution.py:281
  99.4 17.7 %all-to-all-start.1 = ((bf16[32,16,256]{2,1,0:T(8,128)(2,1)}), bf16[32,16,256]{2,1,0:T(8,128)(2,1)S(1)}, u32[]{:S(2)}, u32[]{:S(2)}) async-start(bf16[32,16,256]{2,1,0:T(8,128)(2,1)} %bitcast.15), calls=%async_computation.1 | async-start | bytes 524288 | tf_op jit(solution)/shard_map/backward/all_to_all | solution.py:331
  105.7 3.3 %collective-permute-start.17 = (bf16[4,128,128]{2,1,0:T(8,128)(2,1)S(1)}, bf16[4,128,128]{2,1,0:T(8,128)(2,1)S(1)}, u32[]{:S(2)}, u32[]{:S(2)}) collective-permute-start(bf16[4,128,128]{2,1,0:T(8,128)(2,1)S(1)} %get-tuple-element.22.refs_0_), channel_id=1, source_target_pairs={{0,1},{1,0},{2,3},{3,2},{4,5},{5,4},{6,7},{7,6},{8,9},{9,8},{10,11... | collective-permute-start | bytes 393224 | tf_op jit(solution)/shard_map/backward/ppermute | solution.py:281
  108.1 1.3 collective-permute-start.18
  108.2 1.4 collective-permute-start.20
  108.6 1.3 collective-permute-start.19
  117.1 37.7 %all-to-all-start.3 = ((bf16[32,128,128]{2,1,0:T(8,128)(2,1)}), bf16[32,128,128]{2,1,0:T(8,128)(2,1)S(1)}, u32[]{:S(2)}, u32[]{:S(2)}) async-start(bf16[32,128,128]{2,1,0:T(8,128)(2,1)} %backward.3), calls=%async_computation.3 | async-start | bytes 2097152 | tf_op jit(solution)/shard_map/backward/all_to_all | solution.py:349
  126.8 6.1 %collective-permute-start.4 = (bf16[4,128,128]{2,1,0:T(8,128)(2,1)S(1)}, bf16[4,128,128]{2,1,0:T(8,128)(2,1)S(1)}, u32[]{:S(2)}, u32[]{:S(2)}) collective-permute-start(bf16[4,128,128]{2,1,0:T(8,128)(2,1)S(1)} %get-tuple-element.20.refs_0_), channel_id=1, source_target_pairs={{0,2},{2,4},{4,6},{6,0},{1,3},{3,5},{5,7},{7,1},{8,10},{10,12},{12... | collective-permute-start | bytes 393224 | tf_op jit(solution)/shard_map/backward/ppermute | solution.py:281
  127.4 15.0 %collective-permute-start.6 = (bf16[4,128,128]{2,1,0:T(8,128)(2,1)S(1)}, bf16[4,128,128]{2,1,0:T(8,128)(2,1)S(1)}, u32[]{:S(2)}, u32[]{:S(2)}) collective-permute-start(bf16[4,128,128]{2,1,0:T(8,128)(2,1)S(1)} %get-tuple-element.20.refs_0_), channel_id=1, source_target_pairs={{0,6},{2,0},{4,2},{6,4},{1,7},{3,1},{5,3},{7,5},{8,14},{10,8},{12,... | collective-permute-start | bytes 393224 | tf_op jit(solution)/shard_map/backward/ppermute | solution.py:281
  132.9 10.0 %collective-permute-start.5 = (bf16[4,128,128]{2,1,0:T(8,128)(2,1)S(1)}, bf16[4,128,128]{2,1,0:T(8,128)(2,1)S(1)}, u32[]{:S(2)}, u32[]{:S(2)}) collective-permute-start(bf16[4,128,128]{2,1,0:T(8,128)(2,1)S(1)} %collective-permute-done.4.refs_1_), channel_id=1, source_target_pairs={{0,2},{2,4},{4,6},{6,0},{1,3},{3,5},{5,7},{7,1},{8,10},{10,12},{12... | collective-permute-start | bytes 393224 | tf_op jit(solution)/shard_map/backward/ppermute | solution.py:281
  133.0 2.1 %collective-permute-start.13 = (f32[16,256]{1,0:T(8,128)S(1)}, f32[16,256]{1,0:T(8,128)S(1)}, u32[]{:S(2)}, u32[]{:S(2)}) collective-permute-start(f32[16,256]{1,0:T(8,128)S(1)} %convert_reduce_fusion), channel_id=1, source_target_pairs={{0,1},{1,0},{2,3},{3,2},{4,5},{5,4},{6,7},{7,6},{8,9},{9,8},{10,11... | collective-permute-start | bytes 49160 | tf_op jit(solution)/shard_map/backward/ppermute | solution.py:285
  135.1 2.9 %collective-permute-start.14 = (f32[16,256]{1,0:T(8,128)S(1)}, f32[16,256]{1,0:T(8,128)S(1)}, u32[]{:S(2)}, u32[]{:S(2)}) collective-permute-start(f32[16,256]{1,0:T(8,128)S(1)} %add.68), channel_id=1, source_target_pairs={{0,2},{2,0},{4,6},{6,4},{1,3},{3,1},{5,7},{7,5},{8,10},{10,8},{12,... | collective-permute-start | bytes 49160 | tf_op jit(solution)/shard_map/backward/ppermute | solution.py:285
  138.0 5.0 %collective-permute-start.15 = (f32[16,256]{1,0:T(8,128)S(1)}, f32[16,256]{1,0:T(8,128)S(1)}, u32[]{:S(2)}, u32[]{:S(2)}) collective-permute-start(f32[16,256]{1,0:T(8,128)S(1)} %add.69), channel_id=1, source_target_pairs={{0,4},{2,6},{4,0},{6,2},{1,5},{3,7},{5,1},{7,3},{8,12},{10,14},{12... | collective-permute-start | bytes 49160 | tf_op jit(solution)/shard_map/backward/ppermute | solution.py:285
  140.9 2.5 %collective-permute-start.7 = (bf16[4,128,128]{2,1,0:T(8,128)(2,1)S(1)}, bf16[4,128,128]{2,1,0:T(8,128)(2,1)S(1)}, u32[]{:S(2)}, u32[]{:S(2)}) collective-permute-start(bf16[4,128,128]{2,1,0:T(8,128)(2,1)S(1)} %get-tuple-element.20.refs_0_), channel_id=1, source_target_pairs={{0,1},{1,0},{2,3},{3,2},{4,5},{5,4},{6,7},{7,6},{8,9},{9,8},{10,11... | collective-permute-start | bytes 393224 | tf_op jit(solution)/shard_map/backward/ppermute | solution.py:281
  142.4 1.5 collective-permute-start.8
  142.4 1.5 collective-permute-start.10
  142.9 1.3 collective-permute-start.9
  154.8 38.3 %all-to-all-start.2 = ((bf16[32,160,128]{2,1,0:T(8,128)(2,1)}), bf16[32,160,128]{2,1,0:T(8,128)(2,1)S(1)}, u32[]{:S(2)}, u32[]{:S(2)}) async-start(bf16[32,160,128]{2,1,0:T(8,128)(2,1)} %backward.2), calls=%async_computation.2 | async-start | bytes 2621440 | tf_op jit(solution)/shard_map/backward/all_to_all | solution.py:349
  (1 other events, 0.9 us)

commit v4 on v3

--- a/solution.py
+++ b/solution.py
@@ -244,34 +244,39 @@
     )(index, grad_pre, w_self, returned, *([] if earlier is None else [earlier]))
 
 
-def assemble_kernel(returned, w_self, w_neigh, held, sem):
-    rows = returned.shape[1] - WIDTH
-    copy = pltpu.make_async_copy(returned.at[:, pl.ds(WIDTH, rows)], held, sem)
-    copy.start()
-    copy.wait()
+def assemble_kernel(info, own, other, w_self, w_neigh):
+    core = info[0]
     scale = 1.0 / math.sqrt(512 * 256)
-    for i in range(16):
-        for out, block in ((w_self, held[i]), (w_neigh, held[16 + i])):
-            block = block.astype(F32) * scale
-            out[i, :, :128] = block[:16]
-            out[i, :, 128:] = block[16:]
-
-
-def assemble(returned):
+    for i in range(32):
+        out = (w_self, w_neigh)[i // 16]
+        for piece, at in ((own, core), (other, 1 - core)):
+            block = piece[i].astype(F32) * scale
+            rows = pl.ds(at * 8, 8)
+            out[i % 16, rows, :128] = block[:8]
+            out[i % 16, rows, 128:] = block[8:]
+
+
+def assemble(rows):
     half = jax.ShapeDtypeStruct((16, 16, 256), F32)
     w_self, w_neigh = pl.pallas_call(
         assemble_kernel,
         out_shape=[half, half],
-        in_specs=[pl.BlockSpec(memory_space=pl.ANY)],
-        scratch_shapes=[pltpu.VMEM((32, 32, 128), BF16), pltpu.SemaphoreType.DMA],
+        grid_spec=pltpu.PrefetchScalarGridSpec(
+            num_scalar_prefetch=1,
+            grid=(),
+            in_specs=[pl.BlockSpec(memory_space=pltpu.VMEM)] * 2,
+            out_specs=[pl.BlockSpec(memory_space=pltpu.VMEM)] * 2,
+        ),
         compiler_params=pltpu.CompilerParams(vmem_limit_bytes=8 * 2**20),
         name="assemble",
-    )(returned)
+    )(lax.axis_index("c").astype(jnp.int32)[None], rows, shift(rows, "c", 1))
     return w_self.reshape(256, 256), w_neigh.reshape(256, 256)
 
 
 def sum_over_rep(share):
-    share = share + flip(share, "c", 1)
+    c = lax.axis_index("c")
+    own, other = (lax.dynamic_slice(share, (i * 8, 0), (8, 256)) for i in (c, 1 - c))
+    share = own + shift(other, "c", 1)
     share = share + flip(share, "x", 1)
     return share + flip(share, "x", 2)
 
@@ -338,7 +343,7 @@
             (neighbour,) = over_slots(
                 backward_kernel,
                 "backward",
-                [(32, WIDTH + 32 * len(extra), 128)],
+                [(32, WIDTH + 16 * len(extra), 128)],
                 backward_targets,
                 backward_places,
                 info,
@@ -346,15 +351,18 @@
                 pieces,
                 extra,
             )
+            if h == 1:
+                neighbour, returned[0] = lax.optimization_barrier((neighbour, returned[0]))
             returned.append(lax.all_to_all(neighbour, DOM, 0, 0, tiled=True))
 
+    with jax.named_scope("final"):
+        grad_features = place(0, asked, grad_pre, w_self, returned[0])
+        weight_rows = returned[1][:, WIDTH:, :]
+        weight_rows, grad_features = lax.optimization_barrier((weight_rows, grad_features))
+        grad_features = place(1, asked, grad_pre, w_self, returned[1], grad_features)
+
     with jax.named_scope("weights"):
-        grad_w_self, grad_w_neigh = assemble(returned[1])
-
-    with jax.named_scope("final"):
-        grad_features = None
-        for h in range(PARTS):
-            grad_features = place(h, asked, grad_pre, w_self, returned[h], grad_features)
+        grad_w_self, grad_w_neigh = assemble(weight_rows)
 
     return (output, grad_features.reshape(512, 256), grad_w_self, grad_w_neigh)
 

time: 198 us -> 196 us (0.990)
  waiting for transfers between devices: 103 us -> 99.3 us
  starting transfers between devices: 58.3 us -> 61.9 us
    ppermute x18 -> x20, starting transfers between devices: 18.7 us -> 24.3 us  [shift(): return lax.ppermute(a, axis, [(i, (i + by) % size) for i in range(size)])]
    all_to_all x2, waiting for transfers between devices: 32.4 us -> 28.9 us  [body(): returned.append(lax.all_to_all(neighbour, DOM, 0, 0, tiled=True))]
    ppermute x3 -> x2, starting transfers between devices: 5.42 us -> 2.16 us  [flip(): lax.ppermute(a, axis, [(i, i ^ bit) for i in range(lax.axis_size(axis))])]
    ppermute x18 -> x20, waiting for transfers between devices: 20.8 us -> 19.7 us  [shift(): return lax.ppermute(a, axis, [(i, (i + by) % size) for i in range(size)])]
  transfers between devices with their start and end apart: 25 -> 26, of which waited for: 17 -> 16; matrix products, arithmetic and copies ran while one was open for 0% -> 0% of each run, Pallas kernels for 9% -> 10%
where the time goes in v4:
time: 196 us
  waiting for transfers between devices  99.3 us (51%)
  starting transfers between devices  61.9 us (32%)
  Pallas kernels  29.8 us (15%)
  local copies, waits for them, and re-layouts  2.63 us (1%)
    all_to_all x1, waiting for transfers between devices, body(): columns = lax.all_to_all(outgoing, DOM, 0, 0, tiled=True)  47.7 us
    all_to_all x2, waiting for transfers between devices, body(): returned.append(lax.all_to_all(neighbour, DOM, 0, 0, tiled=True))  28.9 us
    ppermute x20, starting transfers between devices, shift(): return lax.ppermute(a, axis, [(i, (i + by) % size) for i in range(size)])  24.3 us
    pallas_call x3, Pallas kernels, over_slots(): pl.pallas_call(kernel, out_shape=[jax.ShapeDtypeStruct(shape, BF16) for s...  19.9 us
    ppermute x20, waiting for transfers between devices, shift(): return lax.ppermute(a, axis, [(i, (i + by) % size) for i in range(size)])  19.7 us
    all_to_all x2, starting transfers between devices, body(): returned.append(lax.all_to_all(neighbour, DOM, 0, 0, tiled=True))  15.6 us
    all_to_all x1, starting transfers between devices, body(): columns = lax.all_to_all(outgoing, DOM, 0, 0, tiled=True)  12.2 us
    all_to_all x1, starting transfers between devices, body(): lax.all_to_all(local_weights.reshape(32, 16, 256), DOM, 0, 0, tiled=True)  7.7 us
  transfers between devices with their start and end apart: 26, of which 16 were waited for; matrix products, arithmetic and copies ran while one was open for 0% of the time, Pallas kernels for 10%

profile of v4, /device:TPU:1, one launch (start us, length us, event | category | flops | bytes accessed | tf_op | source)
XLA Modules:
  0.0 195.7 jit_solution(10050724718411863877)
XLA Ops:
  2.3 0.9 copy-done.2
  3.2 2.0 %select.13 = bf16[32,128,256]{2,1,0:T(8,128)(2,1)} custom-call(s32[32]{0:T(128)S(1)} %dynamic-slice_reduce_fusion.index, bf16[4,128,256]{2,1,0:T(8,128)(2,1)S(1)} %bitcast.25), custom_call_target="tpu_custom_call" | custom-call | tf_op jit(solution)/shard_map/gather_columns/select/pallas_call | solution.py:32
  5.3 12.2 %all-to-all-start = ((bf16[32,128,256]{2,1,0:T(8,128)(2,1)}), bf16[32,128,256]{2,1,0:T(8,128)(2,1)S(1)}, u32[]{:S(2)}, u32[]{:S(2)}) async-start(bf16[32,128,256]{2,1,0:T(8,128)(2,1)} %select.13), calls=%async_computation | async-start | bytes 4194304 | tf_op jit(solution)/shard_map/gather_columns/all_to_all | solution.py:310
  18.2 47.7 %all-to-all-done.columns = bf16[32,128,256]{2,1,0:T(8,128)(2,1)S(1)} async-done(((bf16[32,128,256]{2,1,0:T(8,128)(2,1)}), bf16[32,128,256]{2,1,0:T(8,128)(2,1)S(1)}, u32[]{:S(2)}, u32[]{:S(2)}) %all-to-all-start) | async-done | bytes 2097184 | tf_op jit(solution)/shard_map/gather_columns/all_to_all | solution.py:310
  65.9 5.5 %forward.1 = (bf16[4,4,128,256]{3,2,1,0:T(8,128)(2,1)S(1)}, bf16[4,4,128,256]{3,2,1,0:T(8,128)(2,1)S(1)}) custom-call(s32[256]{0:T(256)S(1)} %get-tuple-element.43.targets, s32[256]{0:T(256)S(1)} %bitcast.30, s32[3]{0:T(128)S(1)} %pad_add_fusion.info, bf16[256,128,128]{2,1,0:T(8,128)(2,1)} %bitcast.32, bf16[32,128,256]{2,1,0:T(8,128)(2,1)S(1)} %all-to-all-done.columns), custom_call_target="tpu_custom_call" | custom-call | flops 2147483648 | bytes 12582912 | tf_op jit(solution)/shard_map/aggregate/forward/pallas_call | solution.py:141
  71.5 2.7 %collective-permute-start = (bf16[4,4,128,256]{3,2,1,0:T(8,128)(2,1)S(1)}, bf16[4,4,128,256]{3,2,1,0:T(8,128)(2,1)S(1)}, u32[]{:S(2)}, u32[]{:S(2)}) collective-permute-start(bf16[4,4,128,256]{3,2,1,0:T(8,128)(2,1)S(1)} %get-tuple-element.21), channel_id=1, source_target_pairs={{0,1},{1,0},{2,3},{3,2},{4,5},{5,4},{6,7},{7,6},{8,9},{9,8},{10,11... | collective-permute-start | bytes 3145736 | tf_op jit(solution)/shard_map/aggregate/ppermute | solution.py:286
  74.3 2.3 %collective-permute-done = bf16[4,4,128,256]{3,2,1,0:T(8,128)(2,1)S(1)} collective-permute-done((bf16[4,4,128,256]{3,2,1,0:T(8,128)(2,1)S(1)}, bf16[4,4,128,256]{3,2,1,0:T(8,128)(2,1)S(1)}, u32[]{:S(2)}, u32[]{:S(2)}) %collective-permute-start) | collective-permute-done | bytes 1048608 | tf_op jit(solution)/shard_map/aggregate/ppermute | solution.py:286
  77.8 2.9 %collective-permute-start.2 = (bf16[4,128,256]{2,1,0:T(8,128)(2,1)S(1)}, bf16[4,128,256]{2,1,0:T(8,128)(2,1)S(1)}, u32[]{:S(2)}, u32[]{:S(2)}) collective-permute-start(bf16[4,128,256]{2,1,0:T(8,128)(2,1)S(1)} %get-tuple-element.37), channel_id=1, source_target_pairs={{0,4},{2,6},{4,0},{6,2},{1,5},{3,7},{5,1},{7,3},{8,12},{10,14},{12... | collective-permute-start | bytes 786440 | tf_op jit(solution)/shard_map/aggregate/ppermute | solution.py:286
  80.6 1.2 collective-permute-start.3
  81.8 3.9 %collective-permute-done.1 = bf16[4,128,256]{2,1,0:T(8,128)(2,1)S(1)} collective-permute-done((bf16[4,128,256]{2,1,0:T(8,128)(2,1)S(1)}, bf16[4,128,256]{2,1,0:T(8,128)(2,1)S(1)}, u32[]{:S(2)}, u32[]{:S(2)}) %collective-permute-start.1) | collective-permute-done | bytes 262176 | tf_op jit(solution)/shard_map/aggregate/ppermute | solution.py:286
  85.7 6.6 %collective-permute-done.2 = bf16[4,128,256]{2,1,0:T(8,128)(2,1)S(1)} collective-permute-done((bf16[4,128,256]{2,1,0:T(8,128)(2,1)S(1)}, bf16[4,128,256]{2,1,0:T(8,128)(2,1)S(1)}, u32[]{:S(2)}, u32[]{:S(2)}) %collective-permute-start.2) | collective-permute-done | bytes 262176 | tf_op jit(solution)/shard_map/aggregate/ppermute | solution.py:286
  92.3 1.6 dense.1
  94.0 1.0 collective-permute-start.11
  95.0 1.7 collective-permute-start.12
  96.7 2.4 %collective-permute-done.11.refs_1_ = bf16[4,128,128]{2,1,0:T(8,128)(2,1)S(1)} collective-permute-done((bf16[4,128,128]{2,1,0:T(8,128)(2,1)S(1)}, bf16[4,128,128]{2,1,0:T(8,128)(2,1)S(1)}, u32[]{:S(2)}, u32[]{:S(2)}) %collective-permute-start.11) | collective-permute-done | bytes 131104 | tf_op jit(solution)/shard_map/backward/ppermute | solution.py:286
  99.0 7.7 %all-to-all-start.1 = ((bf16[32,16,256]{2,1,0:T(8,128)(2,1)}), bf16[32,16,256]{2,1,0:T(8,128)(2,1)S(1)}, u32[]{:S(2)}, u32[]{:S(2)}) async-start(bf16[32,16,256]{2,1,0:T(8,128)(2,1)} %bitcast.15), calls=%async_computation.1 | async-start | bytes 524288 | tf_op jit(solution)/shard_map/backward/all_to_all | solution.py:336
  106.7 2.4 %collective-permute-start.17 = (bf16[4,128,128]{2,1,0:T(8,128)(2,1)S(1)}, bf16[4,128,128]{2,1,0:T(8,128)(2,1)S(1)}, u32[]{:S(2)}, u32[]{:S(2)}) collective-permute-start(bf16[4,128,128]{2,1,0:T(8,128)(2,1)S(1)} %get-tuple-element.26.refs_0_), channel_id=1, source_target_pairs={{0,1},{1,0},{2,3},{3,2},{4,5},{5,4},{6,7},{7,6},{8,9},{9,8},{10,11... | collective-permute-start | bytes 393224 | tf_op jit(solution)/shard_map/backward/ppermute | solution.py:286
  111.0 7.1 %backward.3 = bf16[32,128,128]{2,1,0:T(8,128)(2,1)} custom-call(s32[256]{0:T(256)S(1)} %fusion.6.targets, s32[256]{0:T(256)S(1)} %get-tuple-element.42.places, s32[3]{0:T(128)S(1)} %pad_add_fusion.info, bf16[256,128,128]{2,1,0:T(8,128)(2,1)} %bitcast.33, bf16[4,128,128]{2,1,0:T(8,128)(2,1)S(1)} %get-tuple-element.26.refs_0_, ...), custom_call_target="tpu_custom_call" | custom-call | flops 2147483648 | bytes 12582912 | tf_op jit(solution)/shard_map/backward/backward/pallas_call | solution.py:141
  118.1 9.7 %all-to-all-start.2 = ((bf16[32,128,128]{2,1,0:T(8,128)(2,1)}), bf16[32,128,128]{2,1,0:T(8,128)(2,1)S(1)}, u32[]{:S(2)}, u32[]{:S(2)}) async-start(bf16[32,128,128]{2,1,0:T(8,128)(2,1)} %backward.3), calls=%async_computation.2 | async-start | bytes 2097152 | tf_op jit(solution)/shard_map/backward/all_to_all | solution.py:356
  127.8 1.8 collective-permute-start.4
  129.7 1.9 collective-permute-start.13
  131.6 2.1 %collective-permute-done.4.refs_1_ = bf16[4,128,128]{2,1,0:T(8,128)(2,1)S(1)} collective-permute-done((bf16[4,128,128]{2,1,0:T(8,128)(2,1)S(1)}, bf16[4,128,128]{2,1,0:T(8,128)(2,1)S(1)}, u32[]{:S(2)}, u32[]{:S(2)}) %collective-permute-start.4) | collective-permute-done | bytes 131104 | tf_op jit(solution)/shard_map/backward/ppermute | solution.py:286
  133.8 3.0 %collective-permute-done.14 = f32[8,256]{1,0:T(8,128)S(1)} collective-permute-done((f32[8,256]{1,0:T(8,128)S(1)}, f32[8,256]{1,0:T(8,128)S(1)}, u32[]{:S(2)}, u32[]{:S(2)}) %collective-permute-start.14) | collective-permute-done | bytes 8224 | tf_op jit(solution)/shard_map/backward/ppermute | solution.py:290
  136.8 2.1 %collective-permute-start.15 = (f32[8,256]{1,0:T(8,128)S(1)}, f32[8,256]{1,0:T(8,128)S(1)}, u32[]{:S(2)}, u32[]{:S(2)}) collective-permute-start(f32[8,256]{1,0:T(8,128)S(1)} %add.77), channel_id=1, source_target_pairs={{0,4},{2,6},{4,0},{6,2},{1,5},{3,7},{5,1},{7,3},{8,12},{10,14},{12... | collective-permute-start | bytes 24584 | tf_op jit(solution)/shard_map/backward/ppermute | solution.py:290
  138.9 2.9 %collective-permute-start.7 = (bf16[4,128,128]{2,1,0:T(8,128)(2,1)S(1)}, bf16[4,128,128]{2,1,0:T(8,128)(2,1)S(1)}, u32[]{:S(2)}, u32[]{:S(2)}) collective-permute-start(bf16[4,128,128]{2,1,0:T(8,128)(2,1)S(1)} %get-tuple-element.24.refs_0_), channel_id=1, source_target_pairs={{0,1},{1,0},{2,3},{3,2},{4,5},{5,4},{6,7},{7,6},{8,9},{9,8},{10,11... | collective-permute-start | bytes 393224 | tf_op jit(solution)/shard_map/backward/ppermute | solution.py:286
  143.6 7.2 %backward.2 = bf16[32,144,128]{2,1,0:T(8,128)(2,1)} custom-call(s32[256]{0:T(256)S(1)} %fusion.6.targets, s32[256]{0:T(256)S(1)} %get-tuple-element.42.places, s32[3]{0:T(128)S(1)} %pad_add_fusion.info, bf16[256,128,128]{2,1,0:T(8,128)(2,1)} %bitcast.34, bf16[4,128,128]{2,1,0:T(8,128)(2,1)S(1)} %get-tuple-element.24.refs_0_, ...), custom_call_target="tpu_custom_call" | custom-call | flops 2147483648 | bytes 12582912 | tf_op jit(solution)/shard_map/backward/backward/pallas_call | solution.py:141
  150.8 4.0 %all-to-all-done.2.returned = bf16[32,128,128]{2,1,0:T(8,128)(2,1)S(1)} async-done(((bf16[32,128,128]{2,1,0:T(8,128)(2,1)}), bf16[32,128,128]{2,1,0:T(8,128)(2,1)S(1)}, u32[]{:S(2)}, u32[]{:S(2)}) %all-to-all-start.2) | async-done | bytes 1048608 | tf_op jit(solution)/shard_map/backward/all_to_all | solution.py:356
  154.8 5.9 %all-to-all-start.3 = ((bf16[32,144,128]{2,1,0:T(8,128)(2,1)}), bf16[32,144,128]{2,1,0:T(8,128)(2,1)S(1)}, u32[]{:S(2)}, u32[]{:S(2)}) async-start(bf16[32,144,128]{2,1,0:T(8,128)(2,1)} %backward.2), calls=%async_computation.3 | async-start | bytes 2359296 | tf_op jit(solution)/shard_map/backward/all_to_all | solution.py:356
  160.8 3.2 %place.2.refs_0_ = bf16[4,128,256]{2,1,0:T(8,128)(2,1)} custom-call(s32[32]{0:T(128)S(1)} %dynamic-slice_reduce_fusion.index, bf16[512,256]{1,0:T(8,128)(2,1)S(1)} %get-tuple-element.23.grad_pre, bf16[256,256]{1,0:T(8,128)(2,1)S(1)} %copy-done.1, bf16[32,128,128]{2,1,0:T(8,128)(2,1)S(1)} %all-to-all-done.2.returned), custom_call_target="tpu_custom_call" | custom-call | tf_op jit(solution)/shard_map/final/place/pallas_call | solution.py:226
  164.0 24.9 %all-to-all-done.3.returned = bf16[32,144,128]{2,1,0:T(8,128)(2,1)S(1)} async-done(((bf16[32,144,128]{2,1,0:T(8,128)(2,1)}), bf16[32,144,128]{2,1,0:T(8,128)(2,1)S(1)}, u32[]{:S(2)}, u32[]{:S(2)}) %all-to-all-start.3) | async-done | bytes 1179680 | tf_op jit(solution)/shard_map/backward/all_to_all | solution.py:356
  188.8 3.8 %collective-permute-start.21 = (bf16[32,16,128]{2,1,0:T(8,128)(2,1)S(1)}, bf16[32,16,128]{2,1,0:T(8,128)(2,1)S(1)}, u32[]{:S(2)}, u32[]{:S(2)}) collective-permute-start(bf16[32,16,128]{2,1,0:T(8,128)(2,1)S(1)} %slice.50.own), channel_id=1, source_target_pairs={{0,1},{1,0},{2,3},{3,2},{4,5},{5,4},{6,7},{7,6},{8,9},{9,8},{10,11... | collective-permute-start | bytes 393224 | tf_op jit(solution)/shard_map/weights/ppermute | solution.py:286
  192.6 2.2 %place.3 = bf16[4,128,256]{2,1,0:T(8,128)(2,1)} custom-call(s32[32]{0:T(128)S(1)} %dynamic-slice_reduce_fusion.index, bf16[512,256]{1,0:T(8,128)(2,1)S(1)} %get-tuple-element.23.grad_pre, bf16[256,256]{1,0:T(8,128)(2,1)S(1)} %copy-done.1, bf16[32,144,128]{2,1,0:T(8,128)(2,1)S(1)} %all-to-all-done.3.returned, ...), custom_call_target="tpu_custom_call", output_to_operand_aliasing={{}: (4, {})} | custom-call | tf_op jit(solution)/shard_map/final/place/pallas_call | solution.py:226
  (57 shorter events, 7.7 us)
Async XLA Ops:
  5.3 12.9 %copy-start.7 = (s32[1,1,256]{2,1,0:T(1,128)S(1)}, s32[1,1,256]{2,1,0:T(1,128)}, u32[]{:S(2)}) copy-start(s32[1,1,256]{2,1,0:T(1,128)} %param.14) | copy-start | bytes 3076
  5.3 60.7 %copy-start.6 = (s32[1,1,256]{2,1,0:T(1,128)S(1)}, s32[1,1,256]{2,1,0:T(1,128)}, u32[]{:S(2)}) copy-start(s32[1,1,256]{2,1,0:T(1,128)} %param.15) | copy-start | bytes 3076
  5.3 60.7 %all-to-all-start = ((bf16[32,128,256]{2,1,0:T(8,128)(2,1)}), bf16[32,128,256]{2,1,0:T(8,128)(2,1)S(1)}, u32[]{:S(2)}, u32[]{:S(2)}) async-start(bf16[32,128,256]{2,1,0:T(8,128)(2,1)} %select.13), calls=%async_computation | async-start | bytes 4194304 | tf_op jit(solution)/shard_map/gather_columns/all_to_all | solution.py:310
  71.5 20.8 %copy-start.1 = (bf16[256,256]{1,0:T(8,128)(2,1)S(1)}, bf16[256,256]{1,0:T(8,128)(2,1)}, u32[]{:S(2)}) copy-start(bf16[256,256]{1,0:T(8,128)(2,1)} %w_self.5) | copy-start | bytes 393220
  71.5 20.8 %copy-start.3 = (bf16[512,256]{1,0:T(8,128)(2,1)S(1)}, bf16[512,256]{1,0:T(8,128)(2,1)}, u32[]{:S(2)}) copy-start(bf16[512,256]{1,0:T(8,128)(2,1)} %features.1) | copy-start | bytes 786436
  71.5 20.8 %copy-start.4 = (bf16[512,256]{1,0:T(8,128)(2,1)S(1)}, bf16[512,256]{1,0:T(8,128)(2,1)}, u32[]{:S(2)}) copy-start(bf16[512,256]{1,0:T(8,128)(2,1)} %cotangent.1) | copy-start | bytes 786436
  71.5 20.8 %copy-start.5 = (bf16[256,256]{1,0:T(8,128)(2,1)S(1)}, bf16[256,256]{1,0:T(8,128)(2,1)}, u32[]{:S(2)}) copy-start(bf16[256,256]{1,0:T(8,128)(2,1)} %w_neigh.1) | copy-start | bytes 393220
  71.5 5.0 %collective-permute-start = (bf16[4,4,128,256]{3,2,1,0:T(8,128)(2,1)S(1)}, bf16[4,4,128,256]{3,2,1,0:T(8,128)(2,1)S(1)}, u32[]{:S(2)}, u32[]{:S(2)}) collective-permute-start(bf16[4,4,128,256]{3,2,1,0:T(8,128)(2,1)S(1)} %get-tuple-element.21), channel_id=1, source_target_pairs={{0,1},{1,0},{2,3},{3,2},{4,5},{5,4},{6,7},{7,6},{8,9},{9,8},{10,11... | collective-permute-start | bytes 3145736 | tf_op jit(solution)/shard_map/aggregate/ppermute | solution.py:286
  76.9 8.8 %collective-permute-start.1 = (bf16[4,128,256]{2,1,0:T(8,128)(2,1)S(1)}, bf16[4,128,256]{2,1,0:T(8,128)(2,1)S(1)}, u32[]{:S(2)}, u32[]{:S(2)}) collective-permute-start(bf16[4,128,256]{2,1,0:T(8,128)(2,1)S(1)} %get-tuple-element.38), channel_id=1, source_target_pairs={{0,2},{2,4},{4,6},{6,0},{1,3},{3,5},{5,7},{7,1},{8,10},{10,12},{12... | collective-permute-start | bytes 786440 | tf_op jit(solution)/shard_map/aggregate/ppermute | solution.py:286
  77.8 14.5 %collective-permute-start.2 = (bf16[4,128,256]{2,1,0:T(8,128)(2,1)S(1)}, bf16[4,128,256]{2,1,0:T(8,128)(2,1)S(1)}, u32[]{:S(2)}, u32[]{:S(2)}) collective-permute-start(bf16[4,128,256]{2,1,0:T(8,128)(2,1)S(1)} %get-tuple-element.37), channel_id=1, source_target_pairs={{0,4},{2,6},{4,0},{6,2},{1,5},{3,7},{5,1},{7,3},{8,12},{10,14},{12... | collective-permute-start | bytes 786440 | tf_op jit(solution)/shard_map/aggregate/ppermute | solution.py:286
  80.6 11.7 %collective-permute-start.3 = (bf16[4,128,256]{2,1,0:T(8,128)(2,1)S(1)}, bf16[4,128,256]{2,1,0:T(8,128)(2,1)S(1)}, u32[]{:S(2)}, u32[]{:S(2)}) collective-permute-start(bf16[4,128,256]{2,1,0:T(8,128)(2,1)S(1)} %get-tuple-element.36), channel_id=1, source_target_pairs={{0,6},{2,0},{4,2},{6,4},{1,7},{3,1},{5,3},{7,5},{8,14},{10,8},{12,... | collective-permute-start | bytes 786440 | tf_op jit(solution)/shard_map/aggregate/ppermute | solution.py:286
  94.0 5.0 %collective-permute-start.11 = (bf16[4,128,128]{2,1,0:T(8,128)(2,1)S(1)}, bf16[4,128,128]{2,1,0:T(8,128)(2,1)S(1)}, u32[]{:S(2)}, u32[]{:S(2)}) collective-permute-start(bf16[4,128,128]{2,1,0:T(8,128)(2,1)S(1)} %get-tuple-element.26.refs_0_), channel_id=1, source_target_pairs={{0,2},{2,4},{4,6},{6,0},{1,3},{3,5},{5,7},{7,1},{8,10},{10,12},{12... | collective-permute-start | bytes 393224 | tf_op jit(solution)/shard_map/backward/ppermute | solution.py:286
  95.0 4.0 %collective-permute-start.12 = (bf16[4,128,128]{2,1,0:T(8,128)(2,1)S(1)}, bf16[4,128,128]{2,1,0:T(8,128)(2,1)S(1)}, u32[]{:S(2)}, u32[]{:S(2)}) collective-permute-start(bf16[4,128,128]{2,1,0:T(8,128)(2,1)S(1)} %get-tuple-element.26.refs_0_), channel_id=1, source_target_pairs={{0,6},{2,0},{4,2},{6,4},{1,7},{3,1},{5,3},{7,5},{8,14},{10,8},{12,... | collective-permute-start | bytes 393224 | tf_op jit(solution)/shard_map/backward/ppermute | solution.py:286
  99.0 10.6 %collective-permute-start.16 = (bf16[4,128,128]{2,1,0:T(8,128)(2,1)S(1)}, bf16[4,128,128]{2,1,0:T(8,128)(2,1)S(1)}, u32[]{:S(2)}, u32[]{:S(2)}) collective-permute-start(bf16[4,128,128]{2,1,0:T(8,128)(2,1)S(1)} %collective-permute-done.11.refs_1_), channel_id=1, source_target_pairs={{0,2},{2,4},{4,6},{6,0},{1,3},{3,5},{5,7},{7,1},{8,10},{10,12},{12... | collective-permute-start | bytes 393224 | tf_op jit(solution)/shard_map/backward/ppermute | solution.py:286
  99.0 19.1 %all-to-all-start.1 = ((bf16[32,16,256]{2,1,0:T(8,128)(2,1)}), bf16[32,16,256]{2,1,0:T(8,128)(2,1)S(1)}, u32[]{:S(2)}, u32[]{:S(2)}) async-start(bf16[32,16,256]{2,1,0:T(8,128)(2,1)} %bitcast.15), calls=%async_computation.1 | async-start | bytes 524288 | tf_op jit(solution)/shard_map/backward/all_to_all | solution.py:336
  106.7 3.4 %collective-permute-start.17 = (bf16[4,128,128]{2,1,0:T(8,128)(2,1)S(1)}, bf16[4,128,128]{2,1,0:T(8,128)(2,1)S(1)}, u32[]{:S(2)}, u32[]{:S(2)}) collective-permute-start(bf16[4,128,128]{2,1,0:T(8,128)(2,1)S(1)} %get-tuple-element.26.refs_0_), channel_id=1, source_target_pairs={{0,1},{1,0},{2,3},{3,2},{4,5},{5,4},{6,7},{7,6},{8,9},{9,8},{10,11... | collective-permute-start | bytes 393224 | tf_op jit(solution)/shard_map/backward/ppermute | solution.py:286
  109.1 1.3 collective-permute-start.18
  109.2 1.4 collective-permute-start.20
  109.6 1.3 collective-permute-start.19
  118.1 36.7 %all-to-all-start.2 = ((bf16[32,128,128]{2,1,0:T(8,128)(2,1)}), bf16[32,128,128]{2,1,0:T(8,128)(2,1)S(1)}, u32[]{:S(2)}, u32[]{:S(2)}) async-start(bf16[32,128,128]{2,1,0:T(8,128)(2,1)} %backward.3), calls=%async_computation.2 | async-start | bytes 2097152 | tf_op jit(solution)/shard_map/backward/all_to_all | solution.py:356
  127.8 5.9 %collective-permute-start.4 = (bf16[4,128,128]{2,1,0:T(8,128)(2,1)S(1)}, bf16[4,128,128]{2,1,0:T(8,128)(2,1)S(1)}, u32[]{:S(2)}, u32[]{:S(2)}) collective-permute-start(bf16[4,128,128]{2,1,0:T(8,128)(2,1)S(1)} %get-tuple-element.24.refs_0_), channel_id=1, source_target_pairs={{0,2},{2,4},{4,6},{6,0},{1,3},{3,5},{5,7},{7,1},{8,10},{10,12},{12... | collective-permute-start | bytes 393224 | tf_op jit(solution)/shard_map/backward/ppermute | solution.py:286
  129.7 4.0 %collective-permute-start.13 = (f32[8,256]{1,0:T(8,128)S(1)}, f32[8,256]{1,0:T(8,128)S(1)}, u32[]{:S(2)}, u32[]{:S(2)}) collective-permute-start(f32[8,256]{1,0:T(8,128)S(1)} %constant_dynamic-slice_fusion), channel_id=1, source_target_pairs={{0,1},{1,0},{2,3},{3,2},{4,5},{5,4},{6,7},{7,6},{8,9},{9,8},{10,11... | collective-permute-start | bytes 24584 | tf_op jit(solution)/shard_map/backward/ppermute | solution.py:286
  131.6 10.2 %collective-permute-start.6 = (bf16[4,128,128]{2,1,0:T(8,128)(2,1)S(1)}, bf16[4,128,128]{2,1,0:T(8,128)(2,1)S(1)}, u32[]{:S(2)}, u32[]{:S(2)}) collective-permute-start(bf16[4,128,128]{2,1,0:T(8,128)(2,1)S(1)} %get-tuple-element.24.refs_0_), channel_id=1, source_target_pairs={{0,6},{2,0},{4,2},{6,4},{1,7},{3,1},{5,3},{7,5},{8,14},{10,8},{12,... | collective-permute-start | bytes 393224 | tf_op jit(solution)/shard_map/backward/ppermute | solution.py:286
  133.7 8.6 %collective-permute-start.5 = (bf16[4,128,128]{2,1,0:T(8,128)(2,1)S(1)}, bf16[4,128,128]{2,1,0:T(8,128)(2,1)S(1)}, u32[]{:S(2)}, u32[]{:S(2)}) collective-permute-start(bf16[4,128,128]{2,1,0:T(8,128)(2,1)S(1)} %collective-permute-done.4.refs_1_), channel_id=1, source_target_pairs={{0,2},{2,4},{4,6},{6,0},{1,3},{3,5},{5,7},{7,1},{8,10},{10,12},{12... | collective-permute-start | bytes 393224 | tf_op jit(solution)/shard_map/backward/ppermute | solution.py:286
  133.7 3.1 %collective-permute-start.14 = (f32[8,256]{1,0:T(8,128)S(1)}, f32[8,256]{1,0:T(8,128)S(1)}, u32[]{:S(2)}, u32[]{:S(2)}) collective-permute-start(f32[8,256]{1,0:T(8,128)S(1)} %dynamic-slice_add_fusion), channel_id=1, source_target_pairs={{0,2},{2,0},{4,6},{6,4},{1,3},{3,1},{5,7},{7,5},{8,10},{10,8},{12,... | collective-permute-start | bytes 24584 | tf_op jit(solution)/shard_map/backward/ppermute | solution.py:290
  136.8 5.5 %collective-permute-start.15 = (f32[8,256]{1,0:T(8,128)S(1)}, f32[8,256]{1,0:T(8,128)S(1)}, u32[]{:S(2)}, u32[]{:S(2)}) collective-permute-start(f32[8,256]{1,0:T(8,128)S(1)} %add.77), channel_id=1, source_target_pairs={{0,4},{2,6},{4,0},{6,2},{1,5},{3,7},{5,1},{7,3},{8,12},{10,14},{12... | collective-permute-start | bytes 24584 | tf_op jit(solution)/shard_map/backward/ppermute | solution.py:290
  138.9 3.8 %collective-permute-start.7 = (bf16[4,128,128]{2,1,0:T(8,128)(2,1)S(1)}, bf16[4,128,128]{2,1,0:T(8,128)(2,1)S(1)}, u32[]{:S(2)}, u32[]{:S(2)}) collective-permute-start(bf16[4,128,128]{2,1,0:T(8,128)(2,1)S(1)} %get-tuple-element.24.refs_0_), channel_id=1, source_target_pairs={{0,1},{1,0},{2,3},{3,2},{4,5},{5,4},{6,7},{7,6},{8,9},{9,8},{10,11... | collective-permute-start | bytes 393224 | tf_op jit(solution)/shard_map/backward/ppermute | solution.py:286
  141.8 1.5 collective-permute-start.8
  141.8 1.5 collective-permute-start.10
  142.3 1.3 collective-permute-start.9
  154.8 34.0 %all-to-all-start.3 = ((bf16[32,144,128]{2,1,0:T(8,128)(2,1)}), bf16[32,144,128]{2,1,0:T(8,128)(2,1)S(1)}, u32[]{:S(2)}, u32[]{:S(2)}) async-start(bf16[32,144,128]{2,1,0:T(8,128)(2,1)} %backward.2), calls=%async_computation.3 | async-start | bytes 2359296 | tf_op jit(solution)/shard_map/backward/all_to_all | solution.py:356
  188.8 6.0 %collective-permute-start.21 = (bf16[32,16,128]{2,1,0:T(8,128)(2,1)S(1)}, bf16[32,16,128]{2,1,0:T(8,128)(2,1)S(1)}, u32[]{:S(2)}, u32[]{:S(2)}) collective-permute-start(bf16[32,16,128]{2,1,0:T(8,128)(2,1)S(1)} %slice.50.own), channel_id=1, source_target_pairs={{0,1},{1,0},{2,3},{3,2},{4,5},{5,4},{6,7},{7,6},{8,9},{9,8},{10,11... | collective-permute-start | bytes 393224 | tf_op jit(solution)/shard_map/weights/ppermute | solution.py:286
  (2 other events, 1.9 us)

commit v5 on v4

--- a/solution.py
+++ b/solution.py
@@ -23,24 +23,26 @@
 REP = ("x", "c")
 
 
-def select_kernel(index, blocks, out):
+def select_kernel(index, *refs):
+    blocks, out = refs[:-1], refs[-1]
     for i in range(out.shape[0]):
-        out[i] = blocks[index[i]]
+        out[i] = blocks[i % len(blocks)][index[i]]
 
 
 def select(index, blocks):
+    shape = (index.shape[0],) + blocks[0].shape[1:]
     return pl.pallas_call(
         select_kernel,
-        out_shape=jax.ShapeDtypeStruct((index.shape[0],) + blocks.shape[1:], blocks.dtype),
+        out_shape=jax.ShapeDtypeStruct(shape, blocks[0].dtype),
         grid_spec=pltpu.PrefetchScalarGridSpec(
             num_scalar_prefetch=1,
             grid=(),
-            in_specs=[pl.BlockSpec(memory_space=pltpu.VMEM)],
+            in_specs=[pl.BlockSpec(memory_space=pltpu.VMEM)] * len(blocks),
             out_specs=pl.BlockSpec(memory_space=pltpu.VMEM),
         ),
         compiler_params=pltpu.CompilerParams(vmem_limit_bytes=8 * 2**20),
         name="select",
-    )(index, blocks)
+    )(index, *blocks)
 
 
 def copies_of(source, target, size, sems):
@@ -87,13 +89,18 @@
     lax.fori_loop(0, values.shape[0] // GROUP, group, 0)
 
 
-def forward_kernel(targets, places, info, values, columns, keep, send, tiles, total, sems):
+def forward_kernel(targets, places, info, values, first, second, keep, send, *scratch):
+    tiles, total, sems, held, piece_sems = scratch
     used, x, core = info[0], info[1], info[2]
 
     def add_slot(k):
-        total[targets[k]] += jnp.dot(tiles[k], columns[places[k]], preferred_element_type=F32)
-
-    accumulate_slots(used, values, tiles, total, sems, [], add_slot)
+        total[targets[k]] += jnp.dot(tiles[k], held[places[k]], preferred_element_type=F32)
+
+    piece_copies = [
+        pltpu.make_async_copy(piece, held.at[pl.ds(i * 16, 16)], piece_sems.at[i])
+        for i, piece in enumerate((first, second))
+    ]
+    accumulate_slots(used, values, tiles, total, sems, piece_copies, add_slot)
     for k in range(4):
         chip = lax.rem(x + k, 4) * 8
         keep[k] = total[pl.ds(chip + core * 4, 4)].astype(BF16)
@@ -131,13 +138,10 @@
         pltpu.VMEM((33,) + tile, F32),
         pltpu.SemaphoreType.DMA((slots // BLOCK,)),
     ]
-    if len(pieces) > 1:
-        scratch += [
-            pltpu.VMEM((32,) + tile, BF16),
-            pltpu.SemaphoreType.DMA((len(pieces),)),
-            pltpu.VMEM(out_shapes[0], BF16),
-        ]
-    piece_space = pl.ANY if len(pieces) > 1 else pltpu.VMEM
+    scratch += [pltpu.VMEM((32,) + tile, BF16), pltpu.SemaphoreType.DMA((len(pieces),))]
+    if len(out_shapes) == 1:
+        scratch.append(pltpu.VMEM(out_shapes[0], BF16))
+    out_space = pl.ANY if len(out_shapes) == 1 else pltpu.VMEM
     return pl.pallas_call(
         kernel,
         out_shape=[jax.ShapeDtypeStruct(shape, BF16) for shape in out_shapes],
@@ -145,9 +149,9 @@
             num_scalar_prefetch=3,
             grid=(),
             in_specs=[pl.BlockSpec(memory_space=pltpu.HBM)]
-            + [pl.BlockSpec(memory_space=piece_space)] * len(pieces)
+            + [pl.BlockSpec(memory_space=pl.ANY)] * len(pieces)
             + [pl.BlockSpec(memory_space=pltpu.VMEM)] * len(extra),
-            out_specs=[pl.BlockSpec(memory_space=piece_space)] * len(out_shapes),
+            out_specs=[pl.BlockSpec(memory_space=out_space)] * len(out_shapes),
             scratch_shapes=scratch,
         ),
         compiler_params=pltpu.CompilerParams(vmem_limit_bytes=VMEM_LIMIT),
@@ -306,13 +310,28 @@
 
     with jax.named_scope("gather_columns"):
         asked = lax.dynamic_slice(needed, (0, rank, z * 4 + y), (32, 1, 1)).reshape(32)
-        outgoing = select(asked, features.reshape(4, 128, 256))
-        columns = lax.all_to_all(outgoing, DOM, 0, 0, tiled=True)
+        wanted = lax.dynamic_slice(
+            needed.reshape(8, 4, 8, 8, 4), (z, 0, rank, 0, y), (1, 4, 1, 8, 1)
+        ).reshape(4, 8)
+        blocks = {0: features.reshape(4, 128, 256)}
+        for k in (1, 2, 3, 4):
+            blocks[k] = shift(blocks[k - 1], "z", 1)
+            if k < 4:
+                blocks[8 - k] = shift(blocks[(9 - k) % 8], "z", 7)
+        columns = []
+        for group in ((0, 1, 7, 2), (6, 3, 5, 4)):
+            index = jnp.stack([wanted[:, (z - k) % 8] for k in group], 1).reshape(16)
+            outgoing = select(index, [blocks[k] for k in group])
+            if not columns:
+                asked, outgoing = lax.optimization_barrier((asked, outgoing))
+            columns.append(lax.all_to_all(outgoing, "y", 0, 0, tiled=True))
+        order = jnp.array([0, 1, 3, 5, 7, 6, 4, 2], jnp.int32)[(z - sources // 4) % 8]
+        forward_places = order // 4 * 16 + sources % 4 * 4 + order % 4
 
     with jax.named_scope("aggregate"):
         shapes = [(4, 4, 128, 256)] * 2
         kept, sent = over_slots(
-            forward_kernel, "forward", shapes, forward_targets, sources, info, values, [columns]
+            forward_kernel, "forward", shapes, forward_targets, forward_places, info, values, columns
         )
         other = shift(sent, "c", 1)
         sums = []

time: 196 us -> 195 us (level)
  waiting for transfers between devices: 99.3 us -> 80.4 us
  starting transfers between devices: 61.9 us -> 76.3 us
    all_to_all x1 -> x2, waiting for transfers between devices: 47.7 us -> 8.95 us  [body(): columns.append(lax.all_to_all(outgoing, 'y', 0, 0, tiled=True))]
    ppermute x20 -> x27, waiting for transfers between devices: 19.7 us -> 40.1 us  [shift(): return lax.ppermute(a, axis, [(i, (i + by) % size) for i in range(size)])]
    ppermute x20 -> x27, starting transfers between devices: 24.3 us -> 42.3 us  [shift(): return lax.ppermute(a, axis, [(i, (i + by) % size) for i in range(size)])]
    all_to_all x1 -> x2, starting transfers between devices: 12.2 us -> 8.55 us  [body(): columns.append(lax.all_to_all(outgoing, 'y', 0, 0, tiled=True))]
  transfers between devices with their start and end apart: 26 -> 34, of which waited for: 16 -> 20; matrix products, arithmetic and copies ran while one was open for 0% -> 2% of each run, Pallas kernels for 10% -> 11%
where the time goes in v5:
time: 195 us; the launch traced here: 194 us
  waiting for transfers between devices  80.4 us (41%)
  starting transfers between devices  76.3 us (39%)
  Pallas kernels  31.1 us (16%)
  local copies, waits for them, and re-layouts  3.92 us (2%)
    ppermute x27, starting transfers between devices, shift(): return lax.ppermute(a, axis, [(i, (i + by) % size) for i in range(size)])  42.3 us
    ppermute x27, waiting for transfers between devices, shift(): return lax.ppermute(a, axis, [(i, (i + by) % size) for i in range(size)])  40.1 us
    all_to_all x2, waiting for transfers between devices, body(): returned.append(lax.all_to_all(neighbour, DOM, 0, 0, tiled=True))  28.6 us
    pallas_call x3, Pallas kernels, over_slots(): pl.pallas_call(kernel, out_shape=[jax.ShapeDtypeStruct(shape, BF16) for s...  20 us
    all_to_all x2, starting transfers between devices, body(): returned.append(lax.all_to_all(neighbour, DOM, 0, 0, tiled=True))  16 us
    all_to_all x2, waiting for transfers between devices, body(): columns.append(lax.all_to_all(outgoing, 'y', 0, 0, tiled=True))  8.95 us
    all_to_all x2, starting transfers between devices, body(): columns.append(lax.all_to_all(outgoing, 'y', 0, 0, tiled=True))  8.55 us
    all_to_all x1, starting transfers between devices, body(): lax.all_to_all(local_weights.reshape(32, 16, 256), DOM, 0, 0, tiled=True)  7.02 us
  transfers between devices with their start and end apart: 34, of which 20 were waited for; matrix products, arithmetic and copies ran while one was open for 2% of the time, Pallas kernels for 11%

profile of v5, /device:TPU:1, one launch (start us, length us, event | category | flops | bytes accessed | tf_op | source)
XLA Modules:
  0.0 193.7 jit_solution(7489320198964416517)
XLA Ops:
  0.6 2.5 %collective-permute-start = (bf16[4,128,256]{2,1,0:T(8,128)(2,1)}, bf16[4,128,256]{2,1,0:T(8,128)(2,1)S(1)}, u32[]{:S(2)}, u32[]{:S(2)}) collective-permute-start(bf16[4,128,256]{2,1,0:T(8,128)(2,1)} %bitcast.45), channel_id=1, source_target_pairs={{0,32},{32,64},{64,96},{96,128},{128,160},{160,192},{192,224},{224... | collective-permute-start | bytes 786440 | tf_op jit(solution)/shard_map/gather_columns/ppermute | solution.py:290
  3.2 4.0 %collective-permute-start.1 = (bf16[4,128,256]{2,1,0:T(8,128)(2,1)}, bf16[4,128,256]{2,1,0:T(8,128)(2,1)S(1)}, u32[]{:S(2)}, u32[]{:S(2)}) collective-permute-start(bf16[4,128,256]{2,1,0:T(8,128)(2,1)} %bitcast.46), channel_id=1, source_target_pairs={{0,224},{32,0},{64,32},{96,64},{128,96},{160,128},{192,160},{224,1... | collective-permute-start | bytes 786440 | tf_op jit(solution)/shard_map/gather_columns/ppermute | solution.py:290
  7.2 6.2 %collective-permute-done.refs_1_ = bf16[4,128,256]{2,1,0:T(8,128)(2,1)S(1)} collective-permute-done((bf16[4,128,256]{2,1,0:T(8,128)(2,1)}, bf16[4,128,256]{2,1,0:T(8,128)(2,1)S(1)}, u32[]{:S(2)}, u32[]{:S(2)}) %collective-permute-start) | collective-permute-done | bytes 262176 | tf_op jit(solution)/shard_map/gather_columns/ppermute | solution.py:290
  17.1 4.0 %collective-permute-done.2.refs_3_ = bf16[4,128,256]{2,1,0:T(8,128)(2,1)S(1)} collective-permute-done((bf16[4,128,256]{2,1,0:T(8,128)(2,1)S(1)}, bf16[4,128,256]{2,1,0:T(8,128)(2,1)S(1)}, u32[]{:S(2)}, u32[]{:S(2)}) %collective-permute-start.2) | collective-permute-done | bytes 262176 | tf_op jit(solution)/shard_map/gather_columns/ppermute | solution.py:290
  22.7 4.2 %all-to-all-start = ((bf16[16,128,256]{2,1,0:T(8,128)(2,1)}), bf16[16,128,256]{2,1,0:T(8,128)(2,1)S(1)}, u32[]{:S(2)}, u32[]{:S(2)}) async-start(bf16[16,128,256]{2,1,0:T(8,128)(2,1)} %select.128), calls=%async_computation | async-start | bytes 2097152 | tf_op jit(solution)/shard_map/gather_columns/all_to_all | solution.py:327
  28.4 3.8 %collective-permute-done.3.refs_0_ = bf16[4,128,256]{2,1,0:T(8,128)(2,1)S(1)} collective-permute-done((bf16[4,128,256]{2,1,0:T(8,128)(2,1)S(1)}, bf16[4,128,256]{2,1,0:T(8,128)(2,1)S(1)}, u32[]{:S(2)}, u32[]{:S(2)}) %collective-permute-start.3) | collective-permute-done | bytes 262176 | tf_op jit(solution)/shard_map/gather_columns/ppermute | solution.py:290
  34.1 4.1 %collective-permute-done.5.refs_2_ = bf16[4,128,256]{2,1,0:T(8,128)(2,1)S(1)} collective-permute-done((bf16[4,128,256]{2,1,0:T(8,128)(2,1)S(1)}, bf16[4,128,256]{2,1,0:T(8,128)(2,1)S(1)}, u32[]{:S(2)}, u32[]{:S(2)}) %collective-permute-start.5) | collective-permute-done | bytes 262176 | tf_op jit(solution)/shard_map/gather_columns/ppermute | solution.py:290
  38.1 2.0 %collective-permute-done.6.refs_3_ = bf16[4,128,256]{2,1,0:T(8,128)(2,1)S(1)} collective-permute-done((bf16[4,128,256]{2,1,0:T(8,128)(2,1)S(1)}, bf16[4,128,256]{2,1,0:T(8,128)(2,1)S(1)}, u32[]{:S(2)}, u32[]{:S(2)}) %collective-permute-start.6) | collective-permute-done | bytes 262176 | tf_op jit(solution)/shard_map/gather_columns/ppermute | solution.py:290
  41.7 4.4 %all-to-all-start.1 = ((bf16[16,128,256]{2,1,0:T(8,128)(2,1)}), bf16[16,128,256]{2,1,0:T(8,128)(2,1)S(1)}, u32[]{:S(2)}, u32[]{:S(2)}) async-start(bf16[16,128,256]{2,1,0:T(8,128)(2,1)} %select.129), calls=%async_computation.1 | async-start | bytes 2097152 | tf_op jit(solution)/shard_map/gather_columns/all_to_all | solution.py:327
  46.9 8.9 %all-to-all-done.1.second = bf16[16,128,256]{2,1,0:T(8,128)(2,1)S(1)} async-done(((bf16[16,128,256]{2,1,0:T(8,128)(2,1)}), bf16[16,128,256]{2,1,0:T(8,128)(2,1)S(1)}, u32[]{:S(2)}, u32[]{:S(2)}) %all-to-all-start.1) | async-done | bytes 1048608 | tf_op jit(solution)/shard_map/gather_columns/all_to_all | solution.py:327
  55.8 5.7 %forward.1 = (bf16[4,4,128,256]{3,2,1,0:T(8,128)(2,1)S(1)}, bf16[4,4,128,256]{3,2,1,0:T(8,128)(2,1)S(1)}) custom-call(s32[256]{0:T(256)S(1)} %get-tuple-element.57.targets, s32[256]{0:T(256)S(1)} %get-tuple-element.62.places, s32[3]{0:T(128)S(1)} %pad_add_fusion.2.info, bf16[256,128,128]{2,1,0:T(8,128)(2,1)} %bitcast.52, ...), custom_call_target="tpu_custom_call" | custom-call | flops 2147483648 | bytes 12582912 | tf_op jit(solution)/shard_map/aggregate/forward/pallas_call | solution.py:145
  61.5 6.4 %collective-permute-start.7 = (bf16[4,4,128,256]{3,2,1,0:T(8,128)(2,1)S(1)}, bf16[4,4,128,256]{3,2,1,0:T(8,128)(2,1)S(1)}, u32[]{:S(2)}, u32[]{:S(2)}) collective-permute-start(bf16[4,4,128,256]{3,2,1,0:T(8,128)(2,1)S(1)} %get-tuple-element.24), channel_id=1, source_target_pairs={{0,1},{1,0},{2,3},{3,2},{4,5},{5,4},{6,7},{7,6},{8,9},{9,8},{10,11... | collective-permute-start | bytes 3145736 | tf_op jit(solution)/shard_map/aggregate/ppermute | solution.py:290
  68.0 2.3 %collective-permute-done.7 = bf16[4,4,128,256]{3,2,1,0:T(8,128)(2,1)S(1)} collective-permute-done((bf16[4,4,128,256]{3,2,1,0:T(8,128)(2,1)S(1)}, bf16[4,4,128,256]{3,2,1,0:T(8,128)(2,1)S(1)}, u32[]{:S(2)}, u32[]{:S(2)}) %collective-permute-start.7) | collective-permute-done | bytes 1048608 | tf_op jit(solution)/shard_map/aggregate/ppermute | solution.py:290
  71.5 2.9 %collective-permute-start.9 = (bf16[4,128,256]{2,1,0:T(8,128)(2,1)S(1)}, bf16[4,128,256]{2,1,0:T(8,128)(2,1)S(1)}, u32[]{:S(2)}, u32[]{:S(2)}) collective-permute-start(bf16[4,128,256]{2,1,0:T(8,128)(2,1)S(1)} %get-tuple-element.51), channel_id=1, source_target_pairs={{0,4},{2,6},{4,0},{6,2},{1,5},{3,7},{5,1},{7,3},{8,12},{10,14},{12... | collective-permute-start | bytes 786440 | tf_op jit(solution)/shard_map/aggregate/ppermute | solution.py:290
  75.5 3.9 %collective-permute-done.8 = bf16[4,128,256]{2,1,0:T(8,128)(2,1)S(1)} collective-permute-done((bf16[4,128,256]{2,1,0:T(8,128)(2,1)S(1)}, bf16[4,128,256]{2,1,0:T(8,128)(2,1)S(1)}, u32[]{:S(2)}, u32[]{:S(2)}) %collective-permute-start.8) | collective-permute-done | bytes 262176 | tf_op jit(solution)/shard_map/aggregate/ppermute | solution.py:290
  79.4 6.6 %collective-permute-done.9 = bf16[4,128,256]{2,1,0:T(8,128)(2,1)S(1)} collective-permute-done((bf16[4,128,256]{2,1,0:T(8,128)(2,1)S(1)}, bf16[4,128,256]{2,1,0:T(8,128)(2,1)S(1)}, u32[]{:S(2)}, u32[]{:S(2)}) %collective-permute-start.9) | collective-permute-done | bytes 262176 | tf_op jit(solution)/shard_map/aggregate/ppermute | solution.py:290
  90.3 2.4 %collective-permute-done.18.refs_1_ = bf16[4,128,128]{2,1,0:T(8,128)(2,1)S(1)} collective-permute-done((bf16[4,128,128]{2,1,0:T(8,128)(2,1)S(1)}, bf16[4,128,128]{2,1,0:T(8,128)(2,1)S(1)}, u32[]{:S(2)}, u32[]{:S(2)}) %collective-permute-start.18) | collective-permute-done | bytes 131104 | tf_op jit(solution)/shard_map/backward/ppermute | solution.py:290
  92.7 7.0 %all-to-all-start.2 = ((bf16[32,16,256]{2,1,0:T(8,128)(2,1)}), bf16[32,16,256]{2,1,0:T(8,128)(2,1)S(1)}, u32[]{:S(2)}, u32[]{:S(2)}) async-start(bf16[32,16,256]{2,1,0:T(8,128)(2,1)} %bitcast.18), calls=%async_computation.2 | async-start | bytes 524288 | tf_op jit(solution)/shard_map/backward/all_to_all | solution.py:355
  100.3 3.1 %collective-permute-start.24 = (bf16[4,128,128]{2,1,0:T(8,128)(2,1)S(1)}, bf16[4,128,128]{2,1,0:T(8,128)(2,1)S(1)}, u32[]{:S(2)}, u32[]{:S(2)}) collective-permute-start(bf16[4,128,128]{2,1,0:T(8,128)(2,1)S(1)} %get-tuple-element.30.refs_0_), channel_id=1, source_target_pairs={{0,1},{1,0},{2,3},{3,2},{4,5},{5,4},{6,7},{7,6},{8,9},{9,8},{10,11... | collective-permute-start | bytes 393224 | tf_op jit(solution)/shard_map/backward/ppermute | solution.py:290
  104.8 3.5 %collective-permute-start.26 = (bf16[4,128,128]{2,1,0:T(8,128)(2,1)S(1)}, bf16[4,128,128]{2,1,0:T(8,128)(2,1)S(1)}, u32[]{:S(2)}, u32[]{:S(2)}) collective-permute-start(bf16[4,128,128]{2,1,0:T(8,128)(2,1)S(1)} %collective-permute-done.23.refs_2_), channel_id=1, source_target_pairs={{0,1},{1,0},{2,3},{3,2},{4,5},{5,4},{6,7},{7,6},{8,9},{9,8},{10,11... | collective-permute-start | bytes 393224 | tf_op jit(solution)/shard_map/backward/ppermute | solution.py:290
  109.3 7.1 %backward.3 = bf16[32,128,128]{2,1,0:T(8,128)(2,1)} custom-call(s32[256]{0:T(256)S(1)} %get-tuple-element.63.targets, s32[256]{0:T(256)S(1)} %get-tuple-element.56.places, s32[3]{0:T(128)S(1)} %pad_add_fusion.2.info, bf16[256,128,128]{2,1,0:T(8,128)(2,1)} %bitcast.53, bf16[4,128,128]{2,1,0:T(8,128)(2,1)S(1)} %get-tuple-element.30.refs_0_, ...), custom_call_target="tpu_custom_call" | custom-call | flops 2147483648 | bytes 12582912 | tf_op jit(solution)/shard_map/backward/backward/pallas_call | solution.py:145
  116.4 9.5 %all-to-all-start.3 = ((bf16[32,128,128]{2,1,0:T(8,128)(2,1)}), bf16[32,128,128]{2,1,0:T(8,128)(2,1)S(1)}, u32[]{:S(2)}, u32[]{:S(2)}) async-start(bf16[32,128,128]{2,1,0:T(8,128)(2,1)} %backward.3), calls=%async_computation.3 | async-start | bytes 2097152 | tf_op jit(solution)/shard_map/backward/all_to_all | solution.py:375
  131.7 2.8 %collective-permute-done.21 = f32[8,256]{1,0:T(8,128)S(1)} collective-permute-done((f32[8,256]{1,0:T(8,128)S(1)}, f32[8,256]{1,0:T(8,128)S(1)}, u32[]{:S(2)}, u32[]{:S(2)}) %collective-permute-start.21) | collective-permute-done | bytes 8224 | tf_op jit(solution)/shard_map/backward/ppermute | solution.py:294
  134.5 2.3 %collective-permute-start.22 = (f32[8,256]{1,0:T(8,128)S(1)}, f32[8,256]{1,0:T(8,128)S(1)}, u32[]{:S(2)}, u32[]{:S(2)}) collective-permute-start(f32[8,256]{1,0:T(8,128)S(1)} %add.249), channel_id=1, source_target_pairs={{0,4},{2,6},{4,0},{6,2},{1,5},{3,7},{5,1},{7,3},{8,12},{10,14},{12... | collective-permute-start | bytes 24584 | tf_op jit(solution)/shard_map/backward/ppermute | solution.py:294
  136.8 2.6 %collective-permute-start.14 = (bf16[4,128,128]{2,1,0:T(8,128)(2,1)S(1)}, bf16[4,128,128]{2,1,0:T(8,128)(2,1)S(1)}, u32[]{:S(2)}, u32[]{:S(2)}) collective-permute-start(bf16[4,128,128]{2,1,0:T(8,128)(2,1)S(1)} %get-tuple-element.28.refs_0_), channel_id=1, source_target_pairs={{0,1},{1,0},{2,3},{3,2},{4,5},{5,4},{6,7},{7,6},{8,9},{9,8},{10,11... | collective-permute-start | bytes 393224 | tf_op jit(solution)/shard_map/backward/ppermute | solution.py:290
  141.3 7.2 %backward.2 = bf16[32,144,128]{2,1,0:T(8,128)(2,1)} custom-call(s32[256]{0:T(256)S(1)} %get-tuple-element.63.targets, s32[256]{0:T(256)S(1)} %get-tuple-element.56.places, s32[3]{0:T(128)S(1)} %pad_add_fusion.2.info, bf16[256,128,128]{2,1,0:T(8,128)(2,1)} %bitcast.54, bf16[4,128,128]{2,1,0:T(8,128)(2,1)S(1)} %get-tuple-element.28.refs_0_, ...), custom_call_target="tpu_custom_call" | custom-call | flops 2147483648 | bytes 12582912 | tf_op jit(solution)/shard_map/backward/backward/pallas_call | solution.py:145
  148.6 3.7 %all-to-all-done.3.returned = bf16[32,128,128]{2,1,0:T(8,128)(2,1)S(1)} async-done(((bf16[32,128,128]{2,1,0:T(8,128)(2,1)}), bf16[32,128,128]{2,1,0:T(8,128)(2,1)S(1)}, u32[]{:S(2)}, u32[]{:S(2)}) %all-to-all-start.3) | async-done | bytes 1048608 | tf_op jit(solution)/shard_map/backward/all_to_all | solution.py:375
  152.3 6.5 %all-to-all-start.4 = ((bf16[32,144,128]{2,1,0:T(8,128)(2,1)}), bf16[32,144,128]{2,1,0:T(8,128)(2,1)S(1)}, u32[]{:S(2)}, u32[]{:S(2)}) async-start(bf16[32,144,128]{2,1,0:T(8,128)(2,1)} %backward.2), calls=%async_computation.4 | async-start | bytes 2359296 | tf_op jit(solution)/shard_map/backward/all_to_all | solution.py:375
  158.8 3.2 %place.2.refs_0_ = bf16[4,128,256]{2,1,0:T(8,128)(2,1)} custom-call(s32[32]{0:T(128)S(1)} %dynamic-slice_reduce_fusion.index, bf16[512,256]{1,0:T(8,128)(2,1)S(1)} %get-tuple-element.27.grad_pre, bf16[256,256]{1,0:T(8,128)(2,1)S(1)} %copy-done, bf16[32,128,128]{2,1,0:T(8,128)(2,1)S(1)} %all-to-all-done.3.returned), custom_call_target="tpu_custom_call" | custom-call | tf_op jit(solution)/shard_map/final/place/pallas_call | solution.py:230
  162.0 24.8 %all-to-all-done.4.returned = bf16[32,144,128]{2,1,0:T(8,128)(2,1)S(1)} async-done(((bf16[32,144,128]{2,1,0:T(8,128)(2,1)}), bf16[32,144,128]{2,1,0:T(8,128)(2,1)S(1)}, u32[]{:S(2)}, u32[]{:S(2)}) %all-to-all-start.4) | async-done | bytes 1179680 | tf_op jit(solution)/shard_map/backward/all_to_all | solution.py:375
  186.9 3.8 %collective-permute-start.28 = (bf16[32,16,128]{2,1,0:T(8,128)(2,1)S(1)}, bf16[32,16,128]{2,1,0:T(8,128)(2,1)S(1)}, u32[]{:S(2)}, u32[]{:S(2)}) collective-permute-start(bf16[32,16,128]{2,1,0:T(8,128)(2,1)S(1)} %slice.59.own), channel_id=1, source_target_pairs={{0,1},{1,0},{2,3},{3,2},{4,5},{5,4},{6,7},{7,6},{8,9},{9,8},{10,11... | collective-permute-start | bytes 393224 | tf_op jit(solution)/shard_map/weights/ppermute | solution.py:290
  190.7 2.2 %place.3 = bf16[4,128,256]{2,1,0:T(8,128)(2,1)} custom-call(s32[32]{0:T(128)S(1)} %dynamic-slice_reduce_fusion.index, bf16[512,256]{1,0:T(8,128)(2,1)S(1)} %get-tuple-element.27.grad_pre, bf16[256,256]{1,0:T(8,128)(2,1)S(1)} %copy-done, bf16[32,144,128]{2,1,0:T(8,128)(2,1)S(1)} %all-to-all-done.4.returned, ...), custom_call_target="tpu_custom_call", output_to_operand_aliasing={{}: (4, {})} | custom-call | tf_op jit(solution)/shard_map/final/place/pallas_call | solution.py:230
  (78 shorter events, 28.6 us)
Async XLA Ops:
  0.6 12.7 %collective-permute-start = (bf16[4,128,256]{2,1,0:T(8,128)(2,1)}, bf16[4,128,256]{2,1,0:T(8,128)(2,1)S(1)}, u32[]{:S(2)}, u32[]{:S(2)}) collective-permute-start(bf16[4,128,256]{2,1,0:T(8,128)(2,1)} %bitcast.45), channel_id=1, source_target_pairs={{0,32},{32,64},{64,96},{96,128},{128,160},{160,192},{192,224},{224... | collective-permute-start | bytes 786440 | tf_op jit(solution)/shard_map/gather_columns/ppermute | solution.py:290
  3.2 13.9 %collective-permute-start.1 = (bf16[4,128,256]{2,1,0:T(8,128)(2,1)}, bf16[4,128,256]{2,1,0:T(8,128)(2,1)S(1)}, u32[]{:S(2)}, u32[]{:S(2)}) collective-permute-start(bf16[4,128,256]{2,1,0:T(8,128)(2,1)} %bitcast.46), channel_id=1, source_target_pairs={{0,224},{32,0},{64,32},{96,64},{128,96},{160,128},{192,160},{224,1... | collective-permute-start | bytes 786440 | tf_op jit(solution)/shard_map/gather_columns/ppermute | solution.py:290
  13.4 7.8 %collective-permute-start.2 = (bf16[4,128,256]{2,1,0:T(8,128)(2,1)S(1)}, bf16[4,128,256]{2,1,0:T(8,128)(2,1)S(1)}, u32[]{:S(2)}, u32[]{:S(2)}) collective-permute-start(bf16[4,128,256]{2,1,0:T(8,128)(2,1)S(1)} %collective-permute-done.refs_1_), channel_id=1, source_target_pairs={{0,32},{32,64},{64,96},{96,128},{128,160},{160,192},{192,224},{224... | collective-permute-start | bytes 786440 | tf_op jit(solution)/shard_map/gather_columns/ppermute | solution.py:290
  22.7 18.9 %all-to-all-start = ((bf16[16,128,256]{2,1,0:T(8,128)(2,1)}), bf16[16,128,256]{2,1,0:T(8,128)(2,1)S(1)}, u32[]{:S(2)}, u32[]{:S(2)}) async-start(bf16[16,128,256]{2,1,0:T(8,128)(2,1)} %select.128), calls=%async_computation | async-start | bytes 2097152 | tf_op jit(solution)/shard_map/gather_columns/all_to_all | solution.py:327
  26.9 5.2 %collective-permute-start.3 = (bf16[4,128,256]{2,1,0:T(8,128)(2,1)S(1)}, bf16[4,128,256]{2,1,0:T(8,128)(2,1)S(1)}, u32[]{:S(2)}, u32[]{:S(2)}) collective-permute-start(bf16[4,128,256]{2,1,0:T(8,128)(2,1)S(1)} %collective-permute-done.1.refs_2_), channel_id=1, source_target_pairs={{0,224},{32,0},{64,32},{96,64},{128,96},{160,128},{192,160},{224,1... | collective-permute-start | bytes 786440 | tf_op jit(solution)/shard_map/gather_columns/ppermute | solution.py:290
  26.9 6.4 %collective-permute-start.4 = (bf16[4,128,256]{2,1,0:T(8,128)(2,1)S(1)}, bf16[4,128,256]{2,1,0:T(8,128)(2,1)S(1)}, u32[]{:S(2)}, u32[]{:S(2)}) collective-permute-start(bf16[4,128,256]{2,1,0:T(8,128)(2,1)S(1)} %collective-permute-done.2.refs_3_), channel_id=1, source_target_pairs={{0,32},{32,64},{64,96},{96,128},{128,160},{160,192},{192,224},{224... | collective-permute-start | bytes 786440 | tf_op jit(solution)/shard_map/gather_columns/ppermute | solution.py:290
  32.2 6.0 %collective-permute-start.5 = (bf16[4,128,256]{2,1,0:T(8,128)(2,1)S(1)}, bf16[4,128,256]{2,1,0:T(8,128)(2,1)S(1)}, u32[]{:S(2)}, u32[]{:S(2)}) collective-permute-start(bf16[4,128,256]{2,1,0:T(8,128)(2,1)S(1)} %collective-permute-done.3.refs_0_), channel_id=1, source_target_pairs={{0,224},{32,0},{64,32},{96,64},{128,96},{160,128},{192,160},{224,1... | collective-permute-start | bytes 786440 | tf_op jit(solution)/shard_map/gather_columns/ppermute | solution.py:290
  33.4 6.7 %collective-permute-start.6 = (bf16[4,128,256]{2,1,0:T(8,128)(2,1)S(1)}, bf16[4,128,256]{2,1,0:T(8,128)(2,1)S(1)}, u32[]{:S(2)}, u32[]{:S(2)}) collective-permute-start(bf16[4,128,256]{2,1,0:T(8,128)(2,1)S(1)} %collective-permute-done.4.refs_1_), channel_id=1, source_target_pairs={{0,32},{32,64},{64,96},{96,128},{128,160},{160,192},{192,224},{224... | collective-permute-start | bytes 786440 | tf_op jit(solution)/shard_map/gather_columns/ppermute | solution.py:290
  41.7 14.1 %all-to-all-start.1 = ((bf16[16,128,256]{2,1,0:T(8,128)(2,1)}), bf16[16,128,256]{2,1,0:T(8,128)(2,1)S(1)}, u32[]{:S(2)}, u32[]{:S(2)}) async-start(bf16[16,128,256]{2,1,0:T(8,128)(2,1)} %select.129), calls=%async_computation.1 | async-start | bytes 2097152 | tf_op jit(solution)/shard_map/gather_columns/all_to_all | solution.py:327
  61.5 8.7 %collective-permute-start.7 = (bf16[4,4,128,256]{3,2,1,0:T(8,128)(2,1)S(1)}, bf16[4,4,128,256]{3,2,1,0:T(8,128)(2,1)S(1)}, u32[]{:S(2)}, u32[]{:S(2)}) collective-permute-start(bf16[4,4,128,256]{3,2,1,0:T(8,128)(2,1)S(1)} %get-tuple-element.24), channel_id=1, source_target_pairs={{0,1},{1,0},{2,3},{3,2},{4,5},{5,4},{6,7},{7,6},{8,9},{9,8},{10,11... | collective-permute-start | bytes 3145736 | tf_op jit(solution)/shard_map/aggregate/ppermute | solution.py:290
  70.6 8.8 %collective-permute-start.8 = (bf16[4,128,256]{2,1,0:T(8,128)(2,1)S(1)}, bf16[4,128,256]{2,1,0:T(8,128)(2,1)S(1)}, u32[]{:S(2)}, u32[]{:S(2)}) collective-permute-start(bf16[4,128,256]{2,1,0:T(8,128)(2,1)S(1)} %get-tuple-element.52), channel_id=1, source_target_pairs={{0,2},{2,4},{4,6},{6,0},{1,3},{3,5},{5,7},{7,1},{8,10},{10,12},{12... | collective-permute-start | bytes 786440 | tf_op jit(solution)/shard_map/aggregate/ppermute | solution.py:290
  71.5 14.5 %collective-permute-start.9 = (bf16[4,128,256]{2,1,0:T(8,128)(2,1)S(1)}, bf16[4,128,256]{2,1,0:T(8,128)(2,1)S(1)}, u32[]{:S(2)}, u32[]{:S(2)}) collective-permute-start(bf16[4,128,256]{2,1,0:T(8,128)(2,1)S(1)} %get-tuple-element.51), channel_id=1, source_target_pairs={{0,4},{2,6},{4,0},{6,2},{1,5},{3,7},{5,1},{7,3},{8,12},{10,14},{12... | collective-permute-start | bytes 786440 | tf_op jit(solution)/shard_map/aggregate/ppermute | solution.py:290
  74.3 11.7 %collective-permute-start.10 = (bf16[4,128,256]{2,1,0:T(8,128)(2,1)S(1)}, bf16[4,128,256]{2,1,0:T(8,128)(2,1)S(1)}, u32[]{:S(2)}, u32[]{:S(2)}) collective-permute-start(bf16[4,128,256]{2,1,0:T(8,128)(2,1)S(1)} %get-tuple-element.50), channel_id=1, source_target_pairs={{0,6},{2,0},{4,2},{6,4},{1,7},{3,1},{5,3},{7,5},{8,14},{10,8},{12,... | collective-permute-start | bytes 786440 | tf_op jit(solution)/shard_map/aggregate/ppermute | solution.py:290
  87.6 5.0 %collective-permute-start.18 = (bf16[4,128,128]{2,1,0:T(8,128)(2,1)S(1)}, bf16[4,128,128]{2,1,0:T(8,128)(2,1)S(1)}, u32[]{:S(2)}, u32[]{:S(2)}) collective-permute-start(bf16[4,128,128]{2,1,0:T(8,128)(2,1)S(1)} %get-tuple-element.30.refs_0_), channel_id=1, source_target_pairs={{0,2},{2,4},{4,6},{6,0},{1,3},{3,5},{5,7},{7,1},{8,10},{10,12},{12... | collective-permute-start | bytes 393224 | tf_op jit(solution)/shard_map/backward/ppermute | solution.py:290
  88.7 4.0 %collective-permute-start.19 = (bf16[4,128,128]{2,1,0:T(8,128)(2,1)S(1)}, bf16[4,128,128]{2,1,0:T(8,128)(2,1)S(1)}, u32[]{:S(2)}, u32[]{:S(2)}) collective-permute-start(bf16[4,128,128]{2,1,0:T(8,128)(2,1)S(1)} %get-tuple-element.30.refs_0_), channel_id=1, source_target_pairs={{0,6},{2,0},{4,2},{6,4},{1,7},{3,1},{5,3},{7,5},{8,14},{10,8},{12,... | collective-permute-start | bytes 393224 | tf_op jit(solution)/shard_map/backward/ppermute | solution.py:290
  92.7 23.7 %all-to-all-start.2 = ((bf16[32,16,256]{2,1,0:T(8,128)(2,1)}), bf16[32,16,256]{2,1,0:T(8,128)(2,1)S(1)}, u32[]{:S(2)}, u32[]{:S(2)}) async-start(bf16[32,16,256]{2,1,0:T(8,128)(2,1)} %bitcast.18), calls=%async_computation.2 | async-start | bytes 524288 | tf_op jit(solution)/shard_map/backward/all_to_all | solution.py:355
  99.7 5.1 %collective-permute-start.23 = (bf16[4,128,128]{2,1,0:T(8,128)(2,1)S(1)}, bf16[4,128,128]{2,1,0:T(8,128)(2,1)S(1)}, u32[]{:S(2)}, u32[]{:S(2)}) collective-permute-start(bf16[4,128,128]{2,1,0:T(8,128)(2,1)S(1)} %collective-permute-done.18.refs_1_), channel_id=1, source_target_pairs={{0,2},{2,4},{4,6},{6,0},{1,3},{3,5},{5,7},{7,1},{8,10},{10,12},{12... | collective-permute-start | bytes 393224 | tf_op jit(solution)/shard_map/backward/ppermute | solution.py:290
  100.3 8.0 %collective-permute-start.24 = (bf16[4,128,128]{2,1,0:T(8,128)(2,1)S(1)}, bf16[4,128,128]{2,1,0:T(8,128)(2,1)S(1)}, u32[]{:S(2)}, u32[]{:S(2)}) collective-permute-start(bf16[4,128,128]{2,1,0:T(8,128)(2,1)S(1)} %get-tuple-element.30.refs_0_), channel_id=1, source_target_pairs={{0,1},{1,0},{2,3},{3,2},{4,5},{5,4},{6,7},{7,6},{8,9},{9,8},{10,11... | collective-permute-start | bytes 393224 | tf_op jit(solution)/shard_map/backward/ppermute | solution.py:290
  103.4 4.9 %collective-permute-start.25 = (bf16[4,128,128]{2,1,0:T(8,128)(2,1)S(1)}, bf16[4,128,128]{2,1,0:T(8,128)(2,1)S(1)}, u32[]{:S(2)}, u32[]{:S(2)}) collective-permute-start(bf16[4,128,128]{2,1,0:T(8,128)(2,1)S(1)} %collective-permute-done.18.refs_1_), channel_id=1, source_target_pairs={{0,1},{1,0},{2,3},{3,2},{4,5},{5,4},{6,7},{7,6},{8,9},{9,8},{10,11... | collective-permute-start | bytes 393224 | tf_op jit(solution)/shard_map/backward/ppermute | solution.py:290
  103.4 4.9 %collective-permute-start.27 = (bf16[4,128,128]{2,1,0:T(8,128)(2,1)S(1)}, bf16[4,128,128]{2,1,0:T(8,128)(2,1)S(1)}, u32[]{:S(2)}, u32[]{:S(2)}) collective-permute-start(bf16[4,128,128]{2,1,0:T(8,128)(2,1)S(1)} %collective-permute-done.19.refs_3_), channel_id=1, source_target_pairs={{0,1},{1,0},{2,3},{3,2},{4,5},{5,4},{6,7},{7,6},{8,9},{9,8},{10,11... | collective-permute-start | bytes 393224 | tf_op jit(solution)/shard_map/backward/ppermute | solution.py:290
  104.8 4.5 %collective-permute-start.26 = (bf16[4,128,128]{2,1,0:T(8,128)(2,1)S(1)}, bf16[4,128,128]{2,1,0:T(8,128)(2,1)S(1)}, u32[]{:S(2)}, u32[]{:S(2)}) collective-permute-start(bf16[4,128,128]{2,1,0:T(8,128)(2,1)S(1)} %collective-permute-done.23.refs_2_), channel_id=1, source_target_pairs={{0,1},{1,0},{2,3},{3,2},{4,5},{5,4},{6,7},{7,6},{8,9},{9,8},{10,11... | collective-permute-start | bytes 393224 | tf_op jit(solution)/shard_map/backward/ppermute | solution.py:290
  116.4 35.9 %all-to-all-start.3 = ((bf16[32,128,128]{2,1,0:T(8,128)(2,1)}), bf16[32,128,128]{2,1,0:T(8,128)(2,1)S(1)}, u32[]{:S(2)}, u32[]{:S(2)}) async-start(bf16[32,128,128]{2,1,0:T(8,128)(2,1)} %backward.3), calls=%async_computation.3 | async-start | bytes 2097152 | tf_op jit(solution)/shard_map/backward/all_to_all | solution.py:375
  125.9 5.7 %collective-permute-start.11 = (bf16[4,128,128]{2,1,0:T(8,128)(2,1)S(1)}, bf16[4,128,128]{2,1,0:T(8,128)(2,1)S(1)}, u32[]{:S(2)}, u32[]{:S(2)}) collective-permute-start(bf16[4,128,128]{2,1,0:T(8,128)(2,1)S(1)} %get-tuple-element.28.refs_0_), channel_id=1, source_target_pairs={{0,2},{2,4},{4,6},{6,0},{1,3},{3,5},{5,7},{7,1},{8,10},{10,12},{12... | collective-permute-start | bytes 393224 | tf_op jit(solution)/shard_map/backward/ppermute | solution.py:290
  126.1 5.5 %collective-permute-start.20 = (f32[8,256]{1,0:T(8,128)S(1)}, f32[8,256]{1,0:T(8,128)S(1)}, u32[]{:S(2)}, u32[]{:S(2)}) collective-permute-start(f32[8,256]{1,0:T(8,128)S(1)} %constant_dynamic-slice_fusion), channel_id=1, source_target_pairs={{0,1},{1,0},{2,3},{3,2},{4,5},{5,4},{6,7},{7,6},{8,9},{9,8},{10,11... | collective-permute-start | bytes 24584 | tf_op jit(solution)/shard_map/backward/ppermute | solution.py:290
  127.9 11.6 %collective-permute-start.13 = (bf16[4,128,128]{2,1,0:T(8,128)(2,1)S(1)}, bf16[4,128,128]{2,1,0:T(8,128)(2,1)S(1)}, u32[]{:S(2)}, u32[]{:S(2)}) collective-permute-start(bf16[4,128,128]{2,1,0:T(8,128)(2,1)S(1)} %get-tuple-element.28.refs_0_), channel_id=1, source_target_pairs={{0,6},{2,0},{4,2},{6,4},{1,7},{3,1},{5,3},{7,5},{8,14},{10,8},{12,... | collective-permute-start | bytes 393224 | tf_op jit(solution)/shard_map/backward/ppermute | solution.py:290
  131.6 8.4 %collective-permute-start.12 = (bf16[4,128,128]{2,1,0:T(8,128)(2,1)S(1)}, bf16[4,128,128]{2,1,0:T(8,128)(2,1)S(1)}, u32[]{:S(2)}, u32[]{:S(2)}) collective-permute-start(bf16[4,128,128]{2,1,0:T(8,128)(2,1)S(1)} %collective-permute-done.11.refs_1_), channel_id=1, source_target_pairs={{0,2},{2,4},{4,6},{6,0},{1,3},{3,5},{5,7},{7,1},{8,10},{10,12},{12... | collective-permute-start | bytes 393224 | tf_op jit(solution)/shard_map/backward/ppermute | solution.py:290
  131.6 2.9 %collective-permute-start.21 = (f32[8,256]{1,0:T(8,128)S(1)}, f32[8,256]{1,0:T(8,128)S(1)}, u32[]{:S(2)}, u32[]{:S(2)}) collective-permute-start(f32[8,256]{1,0:T(8,128)S(1)} %dynamic-slice_add_fusion), channel_id=1, source_target_pairs={{0,2},{2,0},{4,6},{6,4},{1,3},{3,1},{5,7},{7,5},{8,10},{10,8},{12,... | collective-permute-start | bytes 24584 | tf_op jit(solution)/shard_map/backward/ppermute | solution.py:294
  134.5 5.6 %collective-permute-start.22 = (f32[8,256]{1,0:T(8,128)S(1)}, f32[8,256]{1,0:T(8,128)S(1)}, u32[]{:S(2)}, u32[]{:S(2)}) collective-permute-start(f32[8,256]{1,0:T(8,128)S(1)} %add.249), channel_id=1, source_target_pairs={{0,4},{2,6},{4,0},{6,2},{1,5},{3,7},{5,1},{7,3},{8,12},{10,14},{12... | collective-permute-start | bytes 24584 | tf_op jit(solution)/shard_map/backward/ppermute | solution.py:294
  136.8 3.6 %collective-permute-start.14 = (bf16[4,128,128]{2,1,0:T(8,128)(2,1)S(1)}, bf16[4,128,128]{2,1,0:T(8,128)(2,1)S(1)}, u32[]{:S(2)}, u32[]{:S(2)}) collective-permute-start(bf16[4,128,128]{2,1,0:T(8,128)(2,1)S(1)} %get-tuple-element.28.refs_0_), channel_id=1, source_target_pairs={{0,1},{1,0},{2,3},{3,2},{4,5},{5,4},{6,7},{7,6},{8,9},{9,8},{10,11... | collective-permute-start | bytes 393224 | tf_op jit(solution)/shard_map/backward/ppermute | solution.py:290
  139.5 1.5 collective-permute-start.17
  152.3 34.6 %all-to-all-start.4 = ((bf16[32,144,128]{2,1,0:T(8,128)(2,1)}), bf16[32,144,128]{2,1,0:T(8,128)(2,1)S(1)}, u32[]{:S(2)}, u32[]{:S(2)}) async-start(bf16[32,144,128]{2,1,0:T(8,128)(2,1)} %backward.2), calls=%async_computation.4 | async-start | bytes 2359296 | tf_op jit(solution)/shard_map/backward/all_to_all | solution.py:375
  186.9 6.0 %collective-permute-start.28 = (bf16[32,16,128]{2,1,0:T(8,128)(2,1)S(1)}, bf16[32,16,128]{2,1,0:T(8,128)(2,1)S(1)}, u32[]{:S(2)}, u32[]{:S(2)}) collective-permute-start(bf16[32,16,128]{2,1,0:T(8,128)(2,1)S(1)} %slice.59.own), channel_id=1, source_target_pairs={{0,1},{1,0},{2,3},{3,2},{4,5},{5,4},{6,7},{7,6},{8,9},{9,8},{10,11... | collective-permute-start | bytes 393224 | tf_op jit(solution)/shard_map/weights/ppermute | solution.py:290
  (8 other events, 80.7 us)
